TPU v7x, 512 devices: a whole 4x8x8 slice. The times are simulated.
512 devices in a mesh: dp: 32 (over x, z_lo, core), mp: 16 (over y, z_hi).
Axes of the slice: x: 4, y: 8, z: 8 (z_hi: 2, z_lo: 4; z = z_hi * 4 + z_lo), core: 2. Of those that a mesh axis runs over, the one named last changes fastest.
Arguments:
- sig_feat: bfloat16 [256, 64, 1152], P('dp', None, 'mp'), may hold values from -6 to 6
- conv_feat: bfloat16 [256, 64, 3072], P('dp', None, 'mp'), may hold values from -6 to 6
- proj_weight: bfloat16 [4224, 7168], P('dp', 'mp'), may hold values from -0.09375 to 0.09375
- norm_gain: float32 [7168], P('mp'), may hold values from 0.5 to 1.5
- text_embed: bfloat16 [16384, 7168], P('dp', 'mp'), may hold values from -6 to 6
- grad_out: bfloat16 [16384, 7168], P('dp', 'mp'), may hold values from -6 to 6
- tile_count: int32 [32], P('dp'), may hold values from 1 to 8, 144 in all
- tile_block: int32 [32, 8], P('dp'), may hold values from 0 to 7, each once within a row
Outputs:
- normed: bfloat16 [16384, 7168], P('dp', 'mp')
- grad_sig: bfloat16 [256, 64, 1152], P('dp', None, 'mp')
- grad_conv: bfloat16 [256, 64, 3072], P('dp', None, 'mp')
Inputs may be any that keep to these rules, and one draw needn't show every extreme that they name: `tile_block`: each row holds every block number of a shard once.
All inputs are finite; a program needn't handle non-finite values. No bound on the sum of `tile_count` on one device may be relied on, other than what follows from the above.
Results may differ from a plain program's by a relative error of at most 0.019.
Values may be sent and summed in bfloat16 or wider, within the bound.
No kernel may reach another device: no remote copies, remote signals or barrier semaphores. Data moves between devices by JAX's collectives and lax.ppermute only.
A program may use at most 64 MiB of HBM per device.

v0:
```python
import jax
import jax.numpy as jnp
from jax import lax
from jax.sharding import PartitionSpec as P


def from_behind(x, axis, by):
    devices = lax.axis_size(axis)
    return lax.ppermute(x, axis, [(i, (i + by) % devices) for i in range(devices)])


def gelu_tanh(value):
    return jax.nn.gelu(value, approximate=True)


def per_device(
    sig_feat, conv_feat, proj_weight, norm_gain, text_embed, grad_out, tile_count, tile_block
):
    half_way = lax.axis_size("dp") // 2
    model_groups = lax.axis_size("mp")
    tile_slots, tile_tokens, sig_width = sig_feat.shape
    conv_width = conv_feat.shape[2]
    sig_total = sig_width * model_groups
    conv_total = conv_width * model_groups
    tile_rows = tile_slots * tile_tokens
    conv_wide = lax.all_gather(conv_feat, "mp", axis=2, tiled=True)
    conv_all = from_behind(conv_wide, "dp", half_way)
    sig_all = lax.all_gather(sig_feat, "mp", axis=2, tiled=True)
    weight = lax.all_gather(proj_weight, "dp", axis=0, tiled=True)
    sig_flat = sig_all.reshape(tile_rows, sig_total)
    conv_flat = conv_all.reshape(tile_rows, conv_total)
    pre_act = jnp.dot(sig_flat, weight[:sig_total], preferred_element_type=jnp.float32) + jnp.dot(
        conv_flat, weight[sig_total:], preferred_element_type=jnp.float32
    )
    image = gelu_tanh(pre_act).astype(jnp.bfloat16)
    width_local = weight.shape[1]
    seq_tokens = text_embed.shape[0]
    n_blocks = seq_tokens // tile_tokens
    live_tile = jnp.arange(tile_slots, dtype=jnp.int32) < tile_count[0]
    block_of = tile_block[0, :tile_slots]
    chooser = (block_of[None, :] == jnp.arange(n_blocks, dtype=jnp.int32)[:, None]) & live_tile[
        None, :
    ]
    placed = jnp.einsum(
        "bi,itd->btd",
        chooser.astype(jnp.bfloat16),
        image.reshape(tile_slots, tile_tokens, width_local),
        preferred_element_type=jnp.float32,
    )
    is_image = jnp.any(chooser, axis=1)
    mixed = jnp.where(
        is_image[:, None, None],
        placed,
        text_embed.reshape(n_blocks, tile_tokens, width_local).astype(jnp.float32),
    ).astype(jnp.bfloat16)
    embed_f = mixed.reshape(seq_tokens, width_local).astype(jnp.float32)
    scaled_cot = grad_out.astype(jnp.float32) * norm_gain[None, :]
    square_sum = jnp.sum(embed_f * embed_f, axis=1)
    cross_sum = jnp.sum(scaled_cot * embed_f, axis=1)
    square_sum = lax.psum(square_sum, "mp")
    cross_sum = lax.psum(cross_sum, "mp")
    model_width = width_local * model_groups
    inv_rms = lax.rsqrt(square_sum / model_width + 1e-05)
    normed = (embed_f * inv_rms[:, None] * norm_gain[None, :]).astype(jnp.bfloat16)
    grad_mixed = (
        inv_rms[:, None] * scaled_cot - embed_f * (inv_rms**3 * cross_sum / model_width)[:, None]
    )
    grad_image = jnp.einsum(
        "bi,btd->itd",
        chooser.astype(jnp.float32),
        grad_mixed.reshape(n_blocks, tile_tokens, width_local),
        precision=lax.Precision.HIGHEST,
    ).reshape(tile_rows, width_local)
    unused, pull_back = jax.vjp(gelu_tanh, pre_act)
    grad_pre = pull_back(grad_image)[0].astype(jnp.bfloat16)
    group_rows = sig_width + conv_width
    first_group = jnp.int32(0) // group_rows
    group_count = group_rows * lax.axis_size("mp") // group_rows
    sig_weight = lax.dynamic_slice_in_dim(
        weight, first_group * sig_width, group_count * sig_width, 0
    )
    conv_weight = lax.dynamic_slice_in_dim(weight, sig_total, group_count * conv_width, 0)
    sig_term = lax.dot_general(
        sig_weight, grad_pre, (((1,), (1,)), ((), ())), preferred_element_type=jnp.float32
    )
    conv_term = lax.dot_general(
        conv_weight, grad_pre, (((1,), (1,)), ((), ())), preferred_element_type=jnp.float32
    )
    joined = jnp.concatenate(
        [
            sig_term.reshape(group_count, sig_width, tile_rows),
            conv_term.reshape(group_count, conv_width, tile_rows),
        ],
        axis=1,
    )
    feature_grad = lax.psum_scatter(
        joined.reshape(group_rows * lax.axis_size("mp"), tile_rows).astype(jnp.bfloat16),
        "mp",
        scatter_dimension=0,
        tiled=True,
    )
    feature_rows = feature_grad.T
    grad_sig = feature_rows[:, :sig_width].reshape(tile_slots, tile_tokens, sig_width)
    grad_home = feature_rows[:, sig_width:].reshape(tile_slots, tile_tokens, conv_width)
    grad_conv = from_behind(grad_home, "dp", half_way)
    return (normed, grad_sig, grad_conv)


def solution(mesh):
    placed = (
        P("dp", None, "mp"),
        P("dp", None, "mp"),
        P("dp", "mp"),
        P("mp"),
        P("dp", "mp"),
        P("dp", "mp"),
        P("dp"),
        P("dp", None),
    )
    return jax.shard_map(
        per_device,
        mesh=mesh,
        in_specs=placed,
        out_specs=(P("dp", "mp"), P("dp", None, "mp"), P("dp", None, "mp")),
        check_vma=False,
    )
```

profile of v0, /device:TPU:6, one launch (start us, length us, event | category | flops | bytes accessed | tf_op | source)
XLA Modules:
  0.0 694.1 jit_solution(10532465517859568287)
XLA Ops:
  7.2 0.0 all-gather.7.cloned.1.call-start
  7.2 1.9 copy.67
  9.1 0.0 all-gather.7.cloned.1.call-update
  9.2 0.0 all-gather.5.cloned.1.call-start
  9.2 1.7 copy.65
  10.9 0.0 all-gather.5.cloned.1.call-update
  10.9 0.0 all-gather.9.cloned.1.call-start
  11.0 0.7 all-gather.9.cloned.1.call-update
  11.7 0.0 reduce-scatter.2.cloned.1.call-start
  11.7 167.0 %all-gather.7.cloned.1.call-done = bf16[8,64,3072]{1,0,2:T(8,128)(2,1)} async-done(((bf16[8,64,192]{1,0,2:T(8,128)(2,1)}), bf16[8,64,3072]{1,0,2:T(8,128)(2,1)}) %all-gather.7.cloned.1.call-update) | async-done | bytes 3145744 | tf_op jit(solution)/shard_map/all_gather | solution.py:26
  178.7 7.6 %copy.68 = bf16[8,64,3072]{2,1,0:T(8,128)(2,1)} copy(bf16[8,64,3072]{1,0,2:T(8,128)(2,1)} %all-gather.7.cloned.1.call-done) | data formatting | bytes 6291456 | tf_op jit(solution)/shard_map/all_gather | solution.py:26
  186.3 3.3 collective-permute-start
  190.3 0.2 copy.72
  190.6 0.2 copy.76
  190.8 0.1 fusion.29
  190.9 96.1 %all-gather.5.cloned.1.call-done = bf16[8,64,1152]{1,0,2:T(8,128)(2,1)} async-done(((bf16[8,64,72]{1,0,2:T(8,128)(2,1)}), bf16[8,64,1152]{1,0,2:T(8,128)(2,1)}) %all-gather.5.cloned.1.call-update) | async-done | bytes 1179664 | tf_op jit(solution)/shard_map/all_gather | solution.py:28
  287.0 3.1 copy.66
  290.1 58.1 %all-gather.9.cloned.1.call-done = bf16[32,132,448]{2,1,0:T(8,128)(2,1)} async-done(((bf16[1,132,448]{2,1,0:T(8,128)(2,1)}), bf16[32,132,448]{2,1,0:T(8,128)(2,1)}) %all-gather.9.cloned.1.call-update) | async-done | bytes 3784720 | tf_op jit(solution)/shard_map/all_gather | solution.py:29
  348.2 7.3 %reshape.64 = bf16[4224,448]{1,0:T(8,128)(2,1)} reshape(bf16[32,132,448]{2,1,0:T(8,128)(2,1)} %all-gather.9.cloned.1.call-done) | data formatting | bytes 7569408
  355.5 2.1 fusion.17
  357.6 4.7 multiply_convert_fusion
  362.3 0.2 copy.69
  362.5 0.8 multiply_reduce_fusion
  363.3 0.6 copy.74
  363.9 0.1 copy.75
  364.0 0.1 reduce_sum.21
  364.1 0.2 fusion.12
  364.3 52.9 %all-reduce = (f32[512]{0:T(512)S(1)}, f32[512]{0:T(512)S(1)}) all-reduce(f32[512]{0:T(512)S(1)} %reduce_sum.21, f32[512]{0:T(512)S(1)} %fusion.12), channel_id=1, replica_groups=mesh['dp'=32,'mp'=16] {'mp'}, use_global_device_ids=true, to_apply=%region_2.3 | all-reduce | flops 1024 | bytes 8192 | tf_op jit(solution)/shard_map/psum | solution.py:60
  417.3 1.1 fusion.13
  418.4 1.2 fusion.14
  419.6 0.6 copy.78
  420.2 0.3 copy.79
  420.5 0.6 fusion.25
  421.1 2.2 fusion.4
  423.3 5.4 fusion
  428.7 1.5 copy.81
  430.2 3.2 copy.82
  433.4 3.7 pad_maximum_fusion
  437.1 0.0 reduce-scatter.2.cloned.1.call-update
  437.1 238.9 %reduce-scatter.2.cloned.1.call-done = bf16[264,512]{1,0:T(8,128)(2,1)} async-done(((bf16[4224,512]{1,0:T(8,128)(2,1)}), bf16[264,512]{1,0:T(8,128)(2,1)}) %reduce-scatter.2.cloned.1.call-update) | async-done | bytes 270352 | tf_op jit(solution)/shard_map/reduce_scatter | solution.py:96
  676.0 0.9 slice.20
  677.0 0.1 copy.83
  677.1 3.5 collective-permute-start.1
  680.6 1.0 copy.84
  681.5 0.9 slice.19
  682.4 0.8 copy.88
  683.2 3.7 collective-permute-done.1
  686.9 0.7 copy.98
  (13 shorter events, 0.0 us)
Async XLA Ops:
  7.2 171.6 %all-gather.7.cloned.1.call-start = ((), (), s32[]{:S(2)}) async-start(), calls=%async_computation.2 | async-start | bytes 6684672 | tf_op jit(solution)/shard_map/all_gather | solution.py:26
  9.2 277.8 %all-gather.5.cloned.1.call-start = ((), (), s32[]{:S(2)}) async-start(), calls=%async_computation.1 | async-start | bytes 2506752 | tf_op jit(solution)/shard_map/all_gather | solution.py:28
  10.9 337.3 %all-gather.9.cloned.1.call-start = ((), (), s32[]{:S(2)}) async-start(), calls=%async_computation.4 | async-start | bytes 4595712 | tf_op jit(solution)/shard_map/all_gather | solution.py:29
  11.7 178.7 %copy-start.1 = (bf16[512,448]{0,1:T(8,128)(2,1)S(1)}, bf16[512,448]{0,1:T(8,128)(2,1)}, u32[]{:S(2)}) copy-start(bf16[512,448]{0,1:T(8,128)(2,1)} %param.12) | copy-start | bytes 1376260
  11.7 178.9 %copy-start.2 = (bf16[512,448]{0,1:T(8,128)(2,1)S(1)}, bf16[512,448]{0,1:T(8,128)(2,1)}, u32[]{:S(2)}) copy-start(bf16[512,448]{0,1:T(8,128)(2,1)} %param.13) | copy-start | bytes 1376260
  11.7 179.1 %copy-start.4 = (s32[1,8]{1,0:T(1,128)S(1)}, s32[1,8]{1,0:T(1,128)}, u32[]{:S(2)}) copy-start(s32[1,8]{1,0:T(1,128)} %param.15) | copy-start | bytes 100
  11.7 664.3 %reduce-scatter.2.cloned.1.call-start = ((), (), s32[]{:S(2)}) async-start(), calls=%async_computation.3 | async-start | bytes 4595712 | tf_op jit(solution)/shard_map/reduce_scatter | solution.py:96
  186.3 171.3 %collective-permute-start = (bf16[8,64,3072]{2,1,0:T(8,128)(2,1)}, bf16[8,64,3072]{2,1,0:T(8,128)(2,1)}, u32[]{:S(2)}, u32[]{:S(2)}) collective-permute-start(bf16[8,64,3072]{2,1,0:T(8,128)(2,1)} %copy.68), channel_id=1, source_target_pairs={{0,256},{16,272},{32,288},{48,304},{64,320},{80,336},{96,352},{112... | collective-permute-start | bytes 9437192 | tf_op jit(solution)/shard_map/ppermute | solution.py:9
  362.3 1.8 copy-start.3
  437.1 243.5 %copy-start = (bf16[512,448]{1,0:T(8,128)(2,1)S(1)}, bf16[512,448]{1,0:T(8,128)(2,1)}, u32[]{:S(2)}) copy-start(bf16[512,448]{1,0:T(8,128)(2,1)} %get-tuple-element.18) | copy-start | bytes 1376260
  677.1 9.8 %collective-permute-start.1 = (bf16[8,64,192]{2,1,0:T(8,128)(2,1)S(1)}, bf16[8,64,192]{2,1,0:T(8,128)(2,1)S(1)}, u32[]{:S(2)}, u32[]{:S(2)}) collective-permute-start(bf16[8,64,192]{2,1,0:T(8,128)(2,1)S(1)} %bitcast.54), channel_id=1, source_target_pairs={{0,256},{16,272},{32,288},{48,304},{64,320},{80,336},{96,352},{112... | collective-permute-start | bytes 589832 | tf_op jit(solution)/shard_map/ppermute | solution.py:9
Sparse Core Ops, SparseCore 0:
  11.8 166.9 all-gather.6
  182.5 104.4 all-gather.4
  289.1 59.0 all-gather.8
  437.2 238.7 reduce-scatter.1
where the time goes:
time: 695 us; the launch traced here: 694 us
  waiting for transfers between devices  564 us (81%)
  blocking collectives  52.9 us (8%)
  local copies, waits for them, and re-layouts  33.1 us (5%)
  matrix products  16.3 us (2%)
  between operations  14.6 us (2%)
  starting transfers between devices  6.96 us (1%)
    reduce_scatter x1, waiting for transfers between devices, per_device(): lax.psum_scatter(joined.reshape(group_rows * lax.axis_size('mp'), tile_ro...  239 us
    all_gather x1, waiting for transfers between devices, per_device(): conv_wide = lax.all_gather(conv_feat, 'mp', axis=2, tiled=True)  167 us
    all_gather x1, waiting for transfers between devices, per_device(): sig_all = lax.all_gather(sig_feat, 'mp', axis=2, tiled=True)  96.1 us
    all_gather x1, waiting for transfers between devices, per_device(): weight = lax.all_gather(proj_weight, 'dp', axis=0, tiled=True)  58.1 us
    psum x1, blocking collectives, per_device(): square_sum = lax.psum(square_sum, 'mp')  52.9 us
  transfers between devices with their start and end apart: 6, of which 5 were waited for; matrix products, arithmetic and copies ran while one was open for 4% of the time, Pallas kernels for 0%

commit v1 on v0

v1 whole, which is shorter than its diff:
```python
import functools
import math

import jax
import jax.numpy as jnp
from jax import lax
from jax.experimental import pallas as pl
from jax.experimental.pallas import tpu as pltpu
from jax.sharding import Mesh
from jax.sharding import PartitionSpec as P

BF = jnp.bfloat16
F32 = jnp.float32
EPS = 1e-05
GELU_K = 0.7978845608
GELU_C = 0.044715

AXES = ("x", "zl", "core", "y", "zh")
ROWS = 132
ROWS_PAD = 136
COLS = 448
COLS_PAD = 512
HALF = 256
SIG = 72
CONV = 192


def shift(x, axis, by):
    n = lax.axis_size(axis)
    return lax.ppermute(x, axis, [(i, (i + by) % n) for i in range(n)])


def swap(x, dx, dz):
    nx, nz = lax.axis_size("x"), lax.axis_size("zh")
    pairs = [
        (a * nz + b, ((a + dx) % nx) * nz + (b + dz) % nz) for a in range(nx) for b in range(nz)
    ]
    return lax.ppermute(x, ("x", "zh"), pairs)


def ordered(zh, keep, got, axis):
    first = jnp.where(zh == 0, keep, got)
    second = jnp.where(zh == 0, got, keep)
    return jnp.concatenate([first, second], axis=axis)


def gather_y(block):
    n = lax.axis_size("y")
    me = lax.axis_index("y")
    rows = block.shape[0]
    full = jnp.zeros((n,) + block.shape, block.dtype)

    def put(full, part, owner, row=0):
        return lax.dynamic_update_slice(full, part[None], (owner % n, row, 0))

    full = put(full, block, me)
    right = left = block
    for step in range(1, n // 2):
        right = shift(right, "y", 1)
        left = shift(left, "y", -1)
        full = put(full, right, me - step + n)
        full = put(full, left, me + step)
    half = rows // 2
    far = me + n // 2
    full = put(full, shift(right[:half], "y", 1), far)
    full = put(full, shift(left[half:], "y", -1), far, half)
    return full


def forward_kernel(ft_ref, w_ref, g_ref, gain_ref, img_ref, a_ref, b_ref, stat_ref, acc_ref):
    step = pl.program_id(0)

    @pl.when(step == 0)
    def _():
        acc_ref[...] = jnp.zeros_like(acc_ref)

    for c in range(2):
        total = acc_ref[c]
        for j in range(ft_ref.shape[0]):
            total += jnp.dot(ft_ref[j], w_ref[c, j], preferred_element_type=F32)
        acc_ref[c] = total

    @pl.when(step == pl.num_programs(0) - 1)
    def _():
        square = jnp.zeros((1, HALF), F32)
        cross = jnp.zeros((1, HALF), F32)
        for c in range(2):
            v = acc_ref[c].T
            v2 = v * v
            t = jnp.tanh(GELU_K * (v + GELU_C * v2 * v))
            image = (0.5 * v * (1.0 + t)).astype(BF)
            slope = 0.5 * (1.0 + t) + 0.5 * v * (1.0 - t * t) * GELU_K * (
                1.0 + 3.0 * GELU_C * v2
            )
            img_ref[c] = image
            m = image.astype(F32)
            cot = g_ref[c].astype(F32) * gain_ref[c]
            square += jnp.sum(m * m, axis=0, keepdims=True)
            cross += jnp.sum(cot * m, axis=0, keepdims=True)
            a_ref[c] = slope * cot
            b_ref[c] = slope * m
        stat_ref[0:1] = square
        stat_ref[1:2] = cross


def forward(ft, w, g, gain, per_step=8):
    steps = ft.shape[0] // per_step
    full = lambda *s: pl.BlockSpec(s, lambda i: (0,) * len(s))
    return pl.pallas_call(
        forward_kernel,
        grid=(steps,),
        in_specs=[
            pl.BlockSpec((per_step, HALF, ROWS_PAD), lambda i: (i, 0, 0)),
            pl.BlockSpec((2, per_step, ROWS_PAD, COLS_PAD), lambda i: (0, i, 0, 0)),
            full(2, COLS_PAD, HALF),
            full(2, COLS_PAD, 1),
        ],
        out_specs=[
            full(2, COLS_PAD, HALF),
            full(2, COLS_PAD, HALF),
            full(2, COLS_PAD, HALF),
            full(2, HALF),
        ],
        out_shape=[
            jax.ShapeDtypeStruct((2, COLS_PAD, HALF), BF),
            jax.ShapeDtypeStruct((2, COLS_PAD, HALF), F32),
            jax.ShapeDtypeStruct((2, COLS_PAD, HALF), F32),
            jax.ShapeDtypeStruct((2, HALF), F32),
        ],
        scratch_shapes=[pltpu.VMEM((2, HALF, COLS_PAD), F32)],
        compiler_params=pltpu.CompilerParams(vmem_limit_bytes=48 << 20),
        name="forward",
    )(ft, w, g, gain)


def backward_kernel(width, w_ref, a_ref, b_ref, img_ref, gain_ref, stat_ref, p_ref, n_ref, gp_ref):
    @pl.when(pl.program_id(0) == 0)
    def _():
        inv = lax.rsqrt(stat_ref[0:1] / width + EPS)
        back = inv * inv * inv * stat_ref[1:2] / width
        for c in range(2):
            gp_ref[c] = (inv * a_ref[c] - back * b_ref[c]).astype(BF)
            n_ref[c] = (img_ref[c].astype(F32) * inv * gain_ref[c]).astype(BF)

    for j in range(p_ref.shape[0]):
        p = jnp.dot(w_ref[0, j], gp_ref[0], preferred_element_type=F32)
        p += jnp.dot(w_ref[1, j], gp_ref[1], preferred_element_type=F32)
        p_ref[j] = p.astype(BF)


def backward(w, a, b, image, gain, stat, width, per_step=8):
    steps = w.shape[1] // per_step
    full = lambda *s: pl.BlockSpec(s, lambda i: (0,) * len(s))
    return pl.pallas_call(
        functools.partial(backward_kernel, width),
        grid=(steps,),
        in_specs=[
            pl.BlockSpec((2, per_step, ROWS_PAD, COLS_PAD), lambda i: (0, i, 0, 0)),
            full(2, COLS_PAD, HALF),
            full(2, COLS_PAD, HALF),
            full(2, COLS_PAD, HALF),
            full(2, COLS_PAD, 1),
            full(2, HALF),
        ],
        out_specs=[
            pl.BlockSpec((per_step, ROWS_PAD, HALF), lambda i: (i, 0, 0)),
            full(2, COLS_PAD, HALF),
        ],
        out_shape=[
            jax.ShapeDtypeStruct((w.shape[1], ROWS_PAD, HALF), BF),
            jax.ShapeDtypeStruct((2, COLS_PAD, HALF), BF),
        ],
        scratch_shapes=[pltpu.VMEM((2, COLS_PAD, HALF), BF)],
        compiler_params=pltpu.CompilerParams(vmem_limit_bytes=48 << 20),
        name="backward",
    )(w, a, b, image, gain, stat)


def per_device(sig_feat, conv_feat, weight, gain, text, grad_out, tile_count, tile_block):
    zh = lax.axis_index("zh")
    n_y = lax.axis_size("y")
    n_dp = lax.axis_size("x") * lax.axis_size("zl") * lax.axis_size("core")
    slots, tile_tokens = sig_feat.shape[:2]
    tokens = slots * tile_tokens
    model_width = COLS * n_y * 2

    g0 = gain.astype(BF)
    g1 = (gain - g0.astype(F32)).astype(BF)
    g2 = (gain - g0.astype(F32) - g1.astype(F32)).astype(BF)
    spare = jnp.stack([g0, g1, g2, jnp.zeros_like(g0)])
    w_own = jnp.pad(jnp.concatenate([weight, spare]), ((0, 0), (0, COLS_PAD - COLS)))
    w_all = lax.all_gather(w_own, ("zh", "x", "zl", "core"), axis=0)
    w_all = w_all.reshape(2, n_dp, ROWS_PAD, COLS_PAD)

    def half_of(x, which):
        return lax.dynamic_slice_in_dim(x, which * HALF, HALF, 1)

    sig_t = sig_feat.reshape(tokens, SIG).T
    conv_t = conv_feat.reshape(tokens, CONV).T
    half_way = lax.axis_size("x") // 2
    sig_got = swap(half_of(sig_t, 1 - zh), 0, 1)
    conv_got = swap(half_of(conv_t, 1 - zh), half_way, 1)
    conv_keep = swap(half_of(conv_t, zh), half_way, 0)
    block = jnp.concatenate(
        [
            ordered(zh, half_of(sig_t, zh), sig_got, 0),
            ordered(zh, conv_keep, conv_got, 0),
        ]
    )
    feats = gather_y(block)
    feats = jnp.concatenate(
        [feats[:, : 2 * SIG].reshape(-1, HALF), feats[:, 2 * SIG :].reshape(-1, HALF)]
    )
    feats = feats.reshape(n_dp, ROWS, HALF).transpose(0, 2, 1)
    feats = jnp.pad(feats, ((0, 0), (0, 0), (0, ROWS_PAD - ROWS)))

    live = jnp.arange(slots, dtype=jnp.int32) < tile_count[0]
    block_of = jnp.where(live, tile_block[0, :slots], -1)
    slot_block = jnp.repeat(block_of, tile_tokens)
    place = jnp.arange(tokens, dtype=jnp.int32) % tile_tokens
    seq_block = jnp.arange(tokens, dtype=jnp.int32) // tile_tokens
    chooser = (
        (slot_block[:, None] == seq_block[None, :]) & (place[:, None] == place[None, :])
    ).astype(BF)
    is_image = jnp.any(block_of[:, None] == jnp.arange(slots, dtype=jnp.int32)[None, :], axis=0)
    is_image = jnp.repeat(is_image, tile_tokens)

    text_t = text.T
    grad_t = grad_out.T
    grad_slots = lax.dot_general(
        grad_t, chooser, (((1,), (1,)), ((), ())), preferred_element_type=F32
    ).astype(BF)
    grad_got = swap(half_of(grad_slots, 1 - zh), 0, 1)
    g = ordered(zh, half_of(grad_slots, zh)[None], grad_got[None], 0)
    g = jnp.pad(g, ((0, 0), (0, COLS_PAD - COLS), (0, 0)))

    spare = w_all[:, 0, ROWS : ROWS + 3].astype(F32)
    gain_pair = (spare[:, 0] + spare[:, 1] + spare[:, 2])[:, :, None]

    image, a, b, stat = forward(feats, w_all, g, gain_pair)

    text_f = text_t.astype(F32)
    text_square = jnp.sum(text_f * text_f, axis=0)
    sums = lax.psum(jnp.concatenate([stat.reshape(-1), text_square]), "y")
    stat = sums[: 2 * HALF].reshape(2, HALF)
    text_square = sums[2 * HALF :]

    p, n_image = backward(w_all, a, b, image, gain_pair, stat, float(model_width))
    p = p[:, :ROWS].reshape(n_dp * ROWS, HALF)
    sig_total = SIG * 2 * n_y
    p = jnp.concatenate(
        [
            p[:sig_total].reshape(n_y, 2 * SIG, HALF),
            p[sig_total:].reshape(n_y, 2 * CONV, HALF),
        ],
        axis=1,
    ).reshape(n_dp * ROWS, HALF)
    grads = lax.psum_scatter(p, "y", scatter_dimension=0, tiled=True)

    n_image = n_image[:, :COLS]
    n_keep = lax.dynamic_index_in_dim(n_image, zh, 0, keepdims=False)
    n_got = swap(lax.dynamic_index_in_dim(n_image, 1 - zh, 0, keepdims=False), 0, 1)
    n_slots = ordered(zh, n_keep, n_got, 1)
    n_placed = jnp.dot(n_slots, chooser, preferred_element_type=F32).astype(BF)
    text_square = text_square + shift(text_square, "zh", 1)
    inv_text = lax.rsqrt(text_square / model_width + EPS)
    n_text = (text_f * inv_text[None, :] * gain[:, None]).astype(BF)
    normed = jnp.where(is_image[None, :], n_placed, n_text).T

    sig_g = grads[: 2 * SIG].reshape(2, SIG, HALF)
    conv_g = grads[2 * SIG :].reshape(2, CONV, HALF)

    def pick(x, which):
        return lax.dynamic_index_in_dim(x, which, 0, keepdims=False)

    sig_got = swap(pick(sig_g, 1 - zh), 0, 1)
    conv_got = swap(pick(conv_g, 1 - zh), half_way, 1)
    conv_keep = swap(pick(conv_g, zh), half_way, 0)
    grad_sig = ordered(zh, pick(sig_g, zh), sig_got, 1).T.reshape(slots, tile_tokens, SIG)
    grad_conv = ordered(zh, conv_keep, conv_got, 1).T.reshape(slots, tile_tokens, CONV)
    return normed, grad_sig, grad_conv


def solution(mesh):
    fine = Mesh(mesh.devices.reshape(4, 4, 2, 8, 2), AXES)
    dp, mp = ("x", "zl", "core"), ("y", "zh")
    return jax.shard_map(
        per_device,
        mesh=fine,
        in_specs=(
            P(dp, None, mp),
            P(dp, None, mp),
            P(dp, mp),
            P(mp),
            P(dp, mp),
            P(dp, mp),
            P(dp),
            P(dp, None),
        ),
        out_specs=(P(dp, mp), P(dp, None, mp), P(dp, None, mp)),
        check_vma=False,
    )
```

time: 695 us -> 284 us (0.41)
  waiting for transfers between devices: 564 us -> 96.8 us
  starting transfers between devices: 6.96 us -> 81.3 us
  blocking collectives: 52.9 us -> 16.8 us
  Pallas kernels: 0 us -> 15.2 us
  matrix products: 16.3 us -> 1.97 us
  local copies, waits for them, and re-layouts: 33.1 us -> 46.1 us
    all_gather x3 -> x1, waiting for transfers between devices: 321 us -> 44.8 us  [per_device(): w_all = lax.all_gather(w_own, ('zh', 'x', 'zl', 'core'), axis=0)]
    reduce_scatter x1, waiting for transfers between devices: 239 us -> 25 us  [per_device(): grads = lax.psum_scatter(p, 'y', scatter_dimension=0, tiled=True)]
    ppermute x2 -> x17, starting transfers between devices: 6.8 us -> 81.2 us  [the longest x8 46.6 us: swap(): return lax.ppermute(x, ('x', 'zh'), pairs)]
    psum x1, blocking collectives: 52.9 us -> 16.8 us  [per_device(): sums = lax.psum(jnp.concatenate([stat.reshape(-1), text_square]), 'y')]
    ppermute x2 -> x17, waiting for transfers between devices: 3.69 us -> 27 us  [the longest x8 18.3 us: swap(): return lax.ppermute(x, ('x', 'zh'), pairs)]
    pallas_call x0 -> x2, Pallas kernels: none -> 15.2 us  [the longest x1 8.97 us: forward(): pl.pallas_call(forward_kernel, grid=(steps,), in_specs=[pl.BlockSpec((per...]
    dot_general x6 -> x2, matrix products: 16.3 us -> 1.97 us  [the longest x1 1.34 us: per_device(): n_placed = jnp.dot(n_slots, chooser, preferred_element_type=F32).astype(BF)]
    reshape x1 -> x3, local copies, waits for them, and re-layouts: 0.31 us -> 11.3 us  [the longest x2 9.34 us: per_device(): feats = feats.reshape(n_dp, ROWS, HALF).transpose(0, 2, 1)]
  transfers between devices with their start and end apart: 6 -> 19, of which waited for: 5 -> 10; matrix products, arithmetic and copies ran while one was open for 4% -> 13% of each run, Pallas kernels for 0% -> 0%
where the time goes in v1:
time: 284 us; the launch traced here: 281 us
  waiting for transfers between devices  96.8 us (34%)
  starting transfers between devices  81.3 us (29%)
  local copies, waits for them, and re-layouts  46.1 us (16%)
  blocking collectives  16.8 us (6%)
  between operations  15.3 us (5%)
  Pallas kernels  15.2 us (5%)
  other arithmetic  7.79 us (3%)
    ppermute x8, starting transfers between devices, swap(): return lax.ppermute(x, ('x', 'zh'), pairs)  46.6 us
    all_gather x1, waiting for transfers between devices, per_device(): w_all = lax.all_gather(w_own, ('zh', 'x', 'zl', 'core'), axis=0)  44.8 us
    ppermute x9, starting transfers between devices, shift(): return lax.ppermute(x, axis, [(i, (i + by) % n) for i in range(n)])  34.6 us
    reduce_scatter x1, waiting for transfers between devices, per_device(): grads = lax.psum_scatter(p, 'y', scatter_dimension=0, tiled=True)  25 us
    ppermute x8, waiting for transfers between devices, swap(): return lax.ppermute(x, ('x', 'zh'), pairs)  18.3 us
    psum x1, blocking collectives, per_device(): sums = lax.psum(jnp.concatenate([stat.reshape(-1), text_square]), 'y')  16.8 us
    reshape x2, local copies, waits for them, and re-layouts, per_device(): feats = feats.reshape(n_dp, ROWS, HALF).transpose(0, 2, 1)  9.34 us
    unnamed x28, local copies, waits for them, and re-layouts  8.98 us
  transfers between devices with their start and end apart: 19, of which 10 were waited for; matrix products, arithmetic and copies ran while one was open for 13% of the time, Pallas kernels for 0%

profile of v1, /device:TPU:6, one launch (start us, length us, event | category | flops | bytes accessed | tf_op | source)
XLA Modules:
  0.0 281.3 jit_solution(1423251141453772353)
XLA Ops:
  8.0 1.0 concatenate.27
  9.7 1.0 dynamic-slice_bitcast_fusion.3
  10.7 3.3 %collective-permute-start.1 = (bf16[192,256]{0,1:T(8,128)(2,1)S(1)}, bf16[192,256]{0,1:T(8,128)(2,1)S(1)}, u32[]{:S(2)}, u32[]{:S(2)}) collective-permute-start(bf16[192,256]{0,1:T(8,128)(2,1)S(1)} %get-tuple-element.32), channel_id=1, source_target_pairs={{0,256},{1,257},{128,384},{129,385},{256,0},{257,1},{384,128},{385... | collective-permute-start | bytes 294920 | tf_op jit(solution)/shard_map/ppermute | solution.py:38
  14.1 12.5 %collective-permute-start.2 = (bf16[192,256]{0,1:T(8,128)(2,1)S(1)}, bf16[192,256]{0,1:T(8,128)(2,1)S(1)}, u32[]{:S(2)}, u32[]{:S(2)}) collective-permute-start(bf16[192,256]{0,1:T(8,128)(2,1)S(1)} %get-tuple-element.33), channel_id=1, source_target_pairs={{0,257},{1,256},{128,385},{129,384},{256,1},{257,0},{384,129},{385... | collective-permute-start | bytes 294920 | tf_op jit(solution)/shard_map/ppermute | solution.py:38
  27.6 1.9 collective-permute-start
  32.3 7.8 %collective-permute-start.11 = (bf16[448,256]{1,0:T(8,128)(2,1)}, bf16[448,256]{1,0:T(8,128)(2,1)}, u32[]{:S(2)}, u32[]{:S(2)}) collective-permute-start(bf16[448,256]{1,0:T(8,128)(2,1)} %dynamic-slice_bitcast_fusion.1), channel_id=1, source_target_pairs={{0,1},{1,0},{128,129},{129,128},{256,257},{257,256},{384,385},{385... | collective-permute-start | bytes 688136 | tf_op jit(solution)/shard_map/ppermute | solution.py:38
  40.8 3.5 %collective-permute-start.3 = (bf16[528,256]{0,1:T(8,128)(2,1)S(1)}, bf16[528,256]{0,1:T(8,128)(2,1)S(1)}, u32[]{:S(2)}, u32[]{:S(2)}) collective-permute-start(bf16[528,256]{0,1:T(8,128)(2,1)S(1)} %pad_maximum_fusion.2), channel_id=1, source_target_pairs={{0,2},{2,4},{4,6},{6,8},{8,10},{10,12},{12,14},{14,0},{1,3},{3,5},... | collective-permute-start | bytes 811016 | tf_op jit(solution)/shard_map/ppermute | solution.py:30
  44.3 3.8 %collective-permute-start.4 = (bf16[528,256]{0,1:T(8,128)(2,1)S(1)}, bf16[528,256]{0,1:T(8,128)(2,1)S(1)}, u32[]{:S(2)}, u32[]{:S(2)}) collective-permute-start(bf16[528,256]{0,1:T(8,128)(2,1)S(1)} %pad_maximum_fusion.2), channel_id=1, source_target_pairs={{0,14},{2,0},{4,2},{6,4},{8,6},{10,8},{12,10},{14,12},{1,15},{3,1}... | collective-permute-start | bytes 811016 | tf_op jit(solution)/shard_map/ppermute | solution.py:30
  48.8 1.5 broadcast_in_dim.65
  51.0 1.8 collective-permute-done.3
  52.8 1.9 collective-permute-start.5
  54.7 5.1 %collective-permute-start.6 = (bf16[528,256]{0,1:T(8,128)(2,1)S(1)}, bf16[528,256]{0,1:T(8,128)(2,1)S(1)}, u32[]{:S(2)}, u32[]{:S(2)}) collective-permute-start(bf16[528,256]{0,1:T(8,128)(2,1)S(1)} %collective-permute-done.4), channel_id=1, source_target_pairs={{0,14},{2,0},{4,2},{6,4},{8,6},{10,8},{12,10},{14,12},{1,15},{3,1}... | collective-permute-start | bytes 811016 | tf_op jit(solution)/shard_map/ppermute | solution.py:30
  59.9 1.0 fusion.18
  62.0 1.7 collective-permute-done.5
  63.7 1.9 collective-permute-start.7
  65.6 5.1 %collective-permute-start.8 = (bf16[528,256]{0,1:T(8,128)(2,1)S(1)}, bf16[528,256]{0,1:T(8,128)(2,1)S(1)}, u32[]{:S(2)}, u32[]{:S(2)}) collective-permute-start(bf16[528,256]{0,1:T(8,128)(2,1)S(1)} %collective-permute-done.6), channel_id=1, source_target_pairs={{0,14},{2,0},{4,2},{6,4},{8,6},{10,8},{12,10},{14,12},{1,15},{3,1}... | collective-permute-start | bytes 811016 | tf_op jit(solution)/shard_map/ppermute | solution.py:30
  74.0 1.9 collective-permute-start.9
  76.1 5.1 %collective-permute-start.10 = (bf16[264,256]{0,1:T(8,128)(2,1)S(1)}, bf16[264,256]{0,1:T(8,128)(2,1)S(1)}, u32[]{:S(2)}, u32[]{:S(2)}) collective-permute-start(bf16[264,256]{0,1:T(8,128)(2,1)S(1)} %slice.76), channel_id=1, source_target_pairs={{0,14},{2,0},{4,2},{6,4},{8,6},{10,8},{12,10},{14,12},{1,15},{3,1}... | collective-permute-start | bytes 405512 | tf_op jit(solution)/shard_map/ppermute | solution.py:30
  83.0 1.4 collective-permute-done.10
  85.9 1.6 slice.78
  87.4 1.1 slice.77
  88.5 1.5 pad_maximum_fusion
  90.0 4.0 %reshape.142 = bf16[32,132,256]{2,1,0:T(8,128)(2,1)} reshape(bf16[4224,256]{1,0:T(8,128)(2,1)} %pad_maximum_fusion) | data formatting | bytes 4325376 | tf_op jit(solution)/shard_map/reshape | solution.py:214
  94.0 5.4 %copy.50 = bf16[32,132,256]{1,2,0:T(8,128)(2,1)} copy(bf16[32,132,256]{2,1,0:T(8,128)(2,1)} %reshape.142) | data formatting | bytes 4325376 | tf_op jit(solution)/shard_map/reshape | solution.py:214
  99.3 5.1 %pad.13.ft_ref = bf16[32,256,136]{2,1,0:T(8,128)(2,1)} pad(bf16[32,256,132]{2,1,0:T(8,128)(2,1)} %bitcast.78, bf16[]{:T(256)} %constant.124.clone.1), padding=0_0x0_0x0_4 | pad | bytes 4390914 | tf_op jit(solution)/shard_map/jit(_pad)/pad | solution.py:215
  104.5 44.8 %all-gather.3.cloned.1.call-done = bf16[8704,512]{1,0:T(8,128)(2,1)} async-done(((bf16[136,512]{1,0:T(8,128)(2,1)}), bf16[8704,512]{1,0:T(8,128)(2,1)}) %all-gather.3.cloned.1.call-update) | async-done | bytes 8912912 | tf_op jit(solution)/shard_map/all_gather | solution.py:192
  150.2 9.0 %forward.1 = (bf16[2,512,256]{2,1,0:T(8,128)(2,1)S(1)}, f32[2,512,256]{2,1,0:T(8,128)S(1)}, f32[2,512,256]{2,1,0:T(8,128)S(1)}, f32[2,256]{1,0:T(2,128)S(1)}) custom-call(bf16[32,256,136]{2,1,0:T(8,128)(2,1)} %pad.13.ft_ref, bf16[2,32,136,512]{3,2,1,0:T(8,128)(2,1)} %bitcast.76, bf16[2,512,256]{2,1,0:T(8,128)(2,1)S(1)} %fusion.6.g_ref, ...), custom_call_target="tpu_custom_call" | custom-call | tf_op jit(solution)/shard_map/forward/pallas_call | solution.py:109
  159.2 1.0 copy-done.1
  160.1 1.0 copy-done.3
  161.9 16.8 %psum.7 = f32[1024]{0:T(1024)S(1)} all-reduce(f32[1024]{0:T(1024)S(1)} %pad_maximum_fusion.4), channel_id=1, replica_groups=mesh['x'=4,'zl'=4,'core'=2,'y'=8,'zh'=2] {'y'}, use_global_device_ids=true, to_apply=%region_2.3 | all-reduce | flops 1024 | bytes 8192 | tf_op jit(solution)/shard_map/psum | solution.py:244
  178.7 6.2 %collective-permute-start.13 = (f32[512]{0:T(512)S(1)}, f32[512]{0:T(512)S(1)}, u32[]{:S(2)}, u32[]{:S(2)}) collective-permute-start(f32[512]{0:T(512)S(1)} %slice.69), channel_id=1, source_target_pairs={{0,1},{1,0},{2,3},{3,2},{4,5},{5,4},{6,7},{7,6},{8,9},{9,8},{10,11... | collective-permute-start | bytes 6152 | tf_op jit(solution)/shard_map/ppermute | solution.py:30
  184.9 3.2 %collective-permute-done.13 = f32[512]{0:T(512)S(1)} collective-permute-done((f32[512]{0:T(512)S(1)}, f32[512]{0:T(512)S(1)}, u32[]{:S(2)}, u32[]{:S(2)}) %collective-permute-start.13) | collective-permute-done | bytes 2080 | tf_op jit(solution)/shard_map/ppermute | solution.py:30
  188.1 1.2 copy-done.2
  189.3 1.2 copy-done.4
  190.6 1.0 copy-done.6
  191.6 6.2 %backward.1 = (bf16[32,136,256]{2,1,0:T(8,128)(2,1)S(1)}, bf16[2,512,256]{2,1,0:T(8,128)(2,1)S(1)}) custom-call(bf16[2,32,136,512]{3,2,1,0:T(8,128)(2,1)} %bitcast.77, f32[2,512,256]{2,1,0:T(8,128)S(1)} %copy-done.2, f32[2,512,256]{2,1,0:T(8,128)S(1)} %copy-done.4, bf16[2,512,256]{2,1,0:T(8,128)(2,1)S(1)} %copy-done.6, f32[2,512,1]{2,1,0:T(8,128)S(1)} %add.201.gain_ref, ...), custom_call_target="tpu_custom_call" | custom-call | tf_op jit(solution)/shard_map/backward/pallas_call | solution.py:154
  198.6 2.0 reshape.144
  200.6 1.4 slice-done
  202.1 1.5 pad_maximum_fusion.1
  203.7 1.0 copy-done.8
  204.8 6.2 %collective-permute-start.12 = (bf16[448,256]{1,0:T(8,128)(2,1)S(1)}, bf16[448,256]{1,0:T(8,128)(2,1)S(1)}, u32[]{:S(2)}, u32[]{:S(2)}) collective-permute-start(bf16[448,256]{1,0:T(8,128)(2,1)S(1)} %dynamic-slice_bitcast_fusion), channel_id=1, source_target_pairs={{0,1},{1,0},{128,129},{129,128},{256,257},{257,256},{384,385},{385... | collective-permute-start | bytes 688136 | tf_op jit(solution)/shard_map/ppermute | solution.py:38
  211.3 8.1 %collective-permute-done.12 = bf16[448,256]{1,0:T(8,128)(2,1)S(1)} collective-permute-done((bf16[448,256]{1,0:T(8,128)(2,1)S(1)}, bf16[448,256]{1,0:T(8,128)(2,1)S(1)}, u32[]{:S(2)}, u32[]{:S(2)}) %collective-permute-start.12) | collective-permute-done | bytes 229408 | tf_op jit(solution)/shard_map/ppermute | solution.py:38
  219.4 1.3 fusion
  220.8 25.0 %reduce-scatter.2.cloned.1.call-done = bf16[528,256]{1,0:T(8,128)(2,1)} async-done(((bf16[4224,256]{1,0:T(8,128)(2,1)}), bf16[528,256]{1,0:T(8,128)(2,1)}) %reduce-scatter.2.cloned.1.call-update) | async-done | bytes 270352 | tf_op jit(solution)/shard_map/reduce_scatter | solution.py:258
  246.7 8.0 %collective-permute-start.14 = (bf16[72,256]{1,0:T(8,128)(2,1)S(1)}, bf16[72,256]{1,0:T(8,128)(2,1)S(1)}, u32[]{:S(2)}, u32[]{:S(2)}) collective-permute-start(bf16[72,256]{1,0:T(8,128)(2,1)S(1)} %dynamic-slice_bitcast_fusion.4), channel_id=1, source_target_pairs={{0,1},{1,0},{128,129},{129,128},{256,257},{257,256},{384,385},{385... | collective-permute-start | bytes 110600 | tf_op jit(solution)/shard_map/ppermute | solution.py:38
  255.8 3.2 %collective-permute-start.15 = (bf16[192,256]{0,1:T(8,128)(2,1)S(1)}, bf16[192,256]{0,1:T(8,128)(2,1)S(1)}, u32[]{:S(2)}, u32[]{:S(2)}) collective-permute-start(bf16[192,256]{0,1:T(8,128)(2,1)S(1)} %bitcast.97), channel_id=1, source_target_pairs={{0,256},{1,257},{128,384},{129,385},{256,0},{257,1},{384,128},{385... | collective-permute-start | bytes 294920 | tf_op jit(solution)/shard_map/ppermute | solution.py:38
  259.2 3.6 %collective-permute-start.16 = (bf16[192,256]{0,1:T(8,128)(2,1)S(1)}, bf16[192,256]{0,1:T(8,128)(2,1)S(1)}, u32[]{:S(2)}, u32[]{:S(2)}) collective-permute-start(bf16[192,256]{0,1:T(8,128)(2,1)S(1)} %bitcast.98), channel_id=1, source_target_pairs={{0,257},{1,256},{128,385},{129,384},{256,1},{257,0},{384,129},{385... | collective-permute-start | bytes 294920 | tf_op jit(solution)/shard_map/ppermute | solution.py:38
  264.2 9.5 %collective-permute-done.16 = bf16[192,256]{0,1:T(8,128)(2,1)S(1)} collective-permute-done((bf16[192,256]{0,1:T(8,128)(2,1)S(1)}, bf16[192,256]{0,1:T(8,128)(2,1)S(1)}, u32[]{:S(2)}, u32[]{:S(2)}) %collective-permute-start.16) | collective-permute-done | bytes 98336 | tf_op jit(solution)/shard_map/ppermute | solution.py:38
  (104 shorter events, 21.5 us)
Async XLA Ops:
  7.2 23.8 %copy-start = (bf16[512,448]{0,1:T(8,128)(2,1)S(1)}, bf16[512,448]{0,1:T(8,128)(2,1)}, u32[]{:S(2)}) copy-start(bf16[512,448]{0,1:T(8,128)(2,1)} %param.13) | copy-start | bytes 1376260
  7.2 142.1 %all-gather.3.cloned.1.call-start = ((), (), s32[]{:S(2)}) async-start(), calls=%async_computation.2 | async-start | bytes 9052160 | tf_op jit(solution)/shard_map/all_gather | solution.py:192
  9.7 236.1 %reduce-scatter.2.cloned.1.call-start = ((), (), s32[]{:S(2)}) async-start(), calls=%async_computation.1 | async-start | bytes 2433024 | tf_op jit(solution)/shard_map/reduce_scatter | solution.py:258
  10.7 29.8 %collective-permute-start.1 = (bf16[192,256]{0,1:T(8,128)(2,1)S(1)}, bf16[192,256]{0,1:T(8,128)(2,1)S(1)}, u32[]{:S(2)}, u32[]{:S(2)}) collective-permute-start(bf16[192,256]{0,1:T(8,128)(2,1)S(1)} %get-tuple-element.32), channel_id=1, source_target_pairs={{0,256},{1,257},{128,384},{129,385},{256,0},{257,1},{384,128},{385... | collective-permute-start | bytes 294920 | tf_op jit(solution)/shard_map/ppermute | solution.py:38
  14.1 26.5 %collective-permute-start.2 = (bf16[192,256]{0,1:T(8,128)(2,1)S(1)}, bf16[192,256]{0,1:T(8,128)(2,1)S(1)}, u32[]{:S(2)}, u32[]{:S(2)}) collective-permute-start(bf16[192,256]{0,1:T(8,128)(2,1)S(1)} %get-tuple-element.33), channel_id=1, source_target_pairs={{0,257},{1,256},{128,385},{129,384},{256,1},{257,0},{384,129},{385... | collective-permute-start | bytes 294920 | tf_op jit(solution)/shard_map/ppermute | solution.py:38
  26.5 21.6 %copy-start.9 = (bf16[512,448]{0,1:T(8,128)(2,1)S(1)}, bf16[512,448]{0,1:T(8,128)(2,1)}, u32[]{:S(2)}) copy-start(bf16[512,448]{0,1:T(8,128)(2,1)} %param.12) | copy-start | bytes 1376260
  27.6 12.7 %collective-permute-start = (bf16[72,256]{1,0:T(8,128)(2,1)S(1)}, bf16[72,256]{1,0:T(8,128)(2,1)S(1)}, u32[]{:S(2)}, u32[]{:S(2)}) collective-permute-start(bf16[72,256]{1,0:T(8,128)(2,1)S(1)} %bitcast.101), channel_id=1, source_target_pairs={{0,1},{1,0},{128,129},{129,128},{256,257},{257,256},{384,385},{385... | collective-permute-start | bytes 110600 | tf_op jit(solution)/shard_map/ppermute | solution.py:38
  32.3 27.5 %collective-permute-start.11 = (bf16[448,256]{1,0:T(8,128)(2,1)}, bf16[448,256]{1,0:T(8,128)(2,1)}, u32[]{:S(2)}, u32[]{:S(2)}) collective-permute-start(bf16[448,256]{1,0:T(8,128)(2,1)} %dynamic-slice_bitcast_fusion.1), channel_id=1, source_target_pairs={{0,1},{1,0},{128,129},{129,128},{256,257},{257,256},{384,385},{385... | collective-permute-start | bytes 688136 | tf_op jit(solution)/shard_map/ppermute | solution.py:38
  40.8 12.0 %collective-permute-start.3 = (bf16[528,256]{0,1:T(8,128)(2,1)S(1)}, bf16[528,256]{0,1:T(8,128)(2,1)S(1)}, u32[]{:S(2)}, u32[]{:S(2)}) collective-permute-start(bf16[528,256]{0,1:T(8,128)(2,1)S(1)} %pad_maximum_fusion.2), channel_id=1, source_target_pairs={{0,2},{2,4},{4,6},{6,8},{8,10},{10,12},{12,14},{14,0},{1,3},{3,5},... | collective-permute-start | bytes 811016 | tf_op jit(solution)/shard_map/ppermute | solution.py:30
  44.3 10.4 %collective-permute-start.4 = (bf16[528,256]{0,1:T(8,128)(2,1)S(1)}, bf16[528,256]{0,1:T(8,128)(2,1)S(1)}, u32[]{:S(2)}, u32[]{:S(2)}) collective-permute-start(bf16[528,256]{0,1:T(8,128)(2,1)S(1)} %pad_maximum_fusion.2), channel_id=1, source_target_pairs={{0,14},{2,0},{4,2},{6,4},{8,6},{10,8},{12,10},{14,12},{1,15},{3,1}... | collective-permute-start | bytes 811016 | tf_op jit(solution)/shard_map/ppermute | solution.py:30
  52.8 10.9 %collective-permute-start.5 = (bf16[528,256]{0,1:T(8,128)(2,1)S(1)}, bf16[528,256]{0,1:T(8,128)(2,1)S(1)}, u32[]{:S(2)}, u32[]{:S(2)}) collective-permute-start(bf16[528,256]{0,1:T(8,128)(2,1)S(1)} %collective-permute-done.3), channel_id=1, source_target_pairs={{0,2},{2,4},{4,6},{6,8},{8,10},{10,12},{12,14},{14,0},{1,3},{3,5},... | collective-permute-start | bytes 811016 | tf_op jit(solution)/shard_map/ppermute | solution.py:30
  54.7 10.9 %collective-permute-start.6 = (bf16[528,256]{0,1:T(8,128)(2,1)S(1)}, bf16[528,256]{0,1:T(8,128)(2,1)S(1)}, u32[]{:S(2)}, u32[]{:S(2)}) collective-permute-start(bf16[528,256]{0,1:T(8,128)(2,1)S(1)} %collective-permute-done.4), channel_id=1, source_target_pairs={{0,14},{2,0},{4,2},{6,4},{8,6},{10,8},{12,10},{14,12},{1,15},{3,1}... | collective-permute-start | bytes 811016 | tf_op jit(solution)/shard_map/ppermute | solution.py:30
  63.7 10.2 %collective-permute-start.7 = (bf16[528,256]{0,1:T(8,128)(2,1)S(1)}, bf16[528,256]{0,1:T(8,128)(2,1)S(1)}, u32[]{:S(2)}, u32[]{:S(2)}) collective-permute-start(bf16[528,256]{0,1:T(8,128)(2,1)S(1)} %collective-permute-done.5), channel_id=1, source_target_pairs={{0,2},{2,4},{4,6},{6,8},{8,10},{10,12},{12,14},{14,0},{1,3},{3,5},... | collective-permute-start | bytes 811016 | tf_op jit(solution)/shard_map/ppermute | solution.py:30
  65.6 10.4 %collective-permute-start.8 = (bf16[528,256]{0,1:T(8,128)(2,1)S(1)}, bf16[528,256]{0,1:T(8,128)(2,1)S(1)}, u32[]{:S(2)}, u32[]{:S(2)}) collective-permute-start(bf16[528,256]{0,1:T(8,128)(2,1)S(1)} %collective-permute-done.6), channel_id=1, source_target_pairs={{0,14},{2,0},{4,2},{6,4},{8,6},{10,8},{12,10},{14,12},{1,15},{3,1}... | collective-permute-start | bytes 811016 | tf_op jit(solution)/shard_map/ppermute | solution.py:30
  74.0 8.8 %collective-permute-start.9 = (bf16[264,256]{0,1:T(8,128)(2,1)S(1)}, bf16[264,256]{0,1:T(8,128)(2,1)S(1)}, u32[]{:S(2)}, u32[]{:S(2)}) collective-permute-start(bf16[264,256]{0,1:T(8,128)(2,1)S(1)} %slice.75), channel_id=1, source_target_pairs={{0,2},{2,4},{4,6},{6,8},{8,10},{10,12},{12,14},{14,0},{1,3},{3,5},... | collective-permute-start | bytes 405512 | tf_op jit(solution)/shard_map/ppermute | solution.py:30
  76.1 8.3 %collective-permute-start.10 = (bf16[264,256]{0,1:T(8,128)(2,1)S(1)}, bf16[264,256]{0,1:T(8,128)(2,1)S(1)}, u32[]{:S(2)}, u32[]{:S(2)}) collective-permute-start(bf16[264,256]{0,1:T(8,128)(2,1)S(1)} %slice.76), channel_id=1, source_target_pairs={{0,14},{2,0},{4,2},{6,4},{8,6},{10,8},{12,10},{14,12},{1,15},{3,1}... | collective-permute-start | bytes 405512 | tf_op jit(solution)/shard_map/ppermute | solution.py:30
  159.2 1.0 copy-start.1
  160.1 1.0 copy-start.3
  161.1 0.8 copy-start.5
  178.7 9.4 %collective-permute-start.13 = (f32[512]{0:T(512)S(1)}, f32[512]{0:T(512)S(1)}, u32[]{:S(2)}, u32[]{:S(2)}) collective-permute-start(f32[512]{0:T(512)S(1)} %slice.69), channel_id=1, source_target_pairs={{0,1},{1,0},{2,3},{3,2},{4,5},{5,4},{6,7},{7,6},{8,9},{9,8},{10,11... | collective-permute-start | bytes 6152 | tf_op jit(solution)/shard_map/ppermute | solution.py:30
  188.1 1.2 copy-start.2
  189.3 1.2 copy-start.4
  190.6 1.0 copy-start.6
  197.8 0.8 copy-start.7
  200.6 1.4 slice-start
  200.6 1.5 slice-start.1
  203.7 1.0 copy-start.8
  203.7 15.7 %copy-start.10 = (bf16[512,448]{0,1:T(8,128)(2,1)S(1)}, bf16[512,448]{0,1:T(8,128)(2,1)}, u32[]{:S(2)}) copy-start(bf16[512,448]{0,1:T(8,128)(2,1)} %param.12) | copy-start | bytes 1376260
  203.7 15.7 %copy-start.11 = (f32[448]{0:T(512)S(1)}, f32[448]{0:T(512)}, u32[]{:S(2)}) copy-start(f32[448]{0:T(512)} %param.11) | copy-start | bytes 5380
  204.8 14.6 %collective-permute-start.12 = (bf16[448,256]{1,0:T(8,128)(2,1)S(1)}, bf16[448,256]{1,0:T(8,128)(2,1)S(1)}, u32[]{:S(2)}, u32[]{:S(2)}) collective-permute-start(bf16[448,256]{1,0:T(8,128)(2,1)S(1)} %dynamic-slice_bitcast_fusion), channel_id=1, source_target_pairs={{0,1},{1,0},{128,129},{129,128},{256,257},{257,256},{384,385},{385... | collective-permute-start | bytes 688136 | tf_op jit(solution)/shard_map/ppermute | solution.py:38
  246.7 16.0 %collective-permute-start.14 = (bf16[72,256]{1,0:T(8,128)(2,1)S(1)}, bf16[72,256]{1,0:T(8,128)(2,1)S(1)}, u32[]{:S(2)}, u32[]{:S(2)}) collective-permute-start(bf16[72,256]{1,0:T(8,128)(2,1)S(1)} %dynamic-slice_bitcast_fusion.4), channel_id=1, source_target_pairs={{0,1},{1,0},{128,129},{129,128},{256,257},{257,256},{384,385},{385... | collective-permute-start | bytes 110600 | tf_op jit(solution)/shard_map/ppermute | solution.py:38
  255.8 8.4 %collective-permute-start.15 = (bf16[192,256]{0,1:T(8,128)(2,1)S(1)}, bf16[192,256]{0,1:T(8,128)(2,1)S(1)}, u32[]{:S(2)}, u32[]{:S(2)}) collective-permute-start(bf16[192,256]{0,1:T(8,128)(2,1)S(1)} %bitcast.97), channel_id=1, source_target_pairs={{0,256},{1,257},{128,384},{129,385},{256,0},{257,1},{384,128},{385... | collective-permute-start | bytes 294920 | tf_op jit(solution)/shard_map/ppermute | solution.py:38
  259.2 14.6 %collective-permute-start.16 = (bf16[192,256]{0,1:T(8,128)(2,1)S(1)}, bf16[192,256]{0,1:T(8,128)(2,1)S(1)}, u32[]{:S(2)}, u32[]{:S(2)}) collective-permute-start(bf16[192,256]{0,1:T(8,128)(2,1)S(1)} %bitcast.98), channel_id=1, source_target_pairs={{0,257},{1,256},{128,385},{129,384},{256,1},{257,0},{384,129},{385... | collective-permute-start | bytes 294920 | tf_op jit(solution)/shard_map/ppermute | solution.py:38
Sparse Core Ops, SparseCore 0:
  10.7 138.4 all-gather.2
  203.8 41.9 reduce-scatter.1

commit v2 on v1

v2 whole, which is shorter than its diff:
```python
import functools

import jax
import jax.numpy as jnp
from jax import lax
from jax.experimental import pallas as pl
from jax.experimental.pallas import tpu as pltpu
from jax.sharding import Mesh
from jax.sharding import PartitionSpec as P

BF = jnp.bfloat16
F32 = jnp.float32
EPS = 1e-05
GELU_K = 0.7978845608
GELU_C = 0.044715

AXES = ("xh", "xl", "zl", "core", "y", "zh")
SIZES = (2, 2, 4, 2, 8, 2)
N_X, N_ZL, N_Y = 4, 4, 8
ROWS = 132
ROWS_PAD = 136
DEEP = N_X * ROWS_PAD
TOTAL = 4224
COLS = 448
COLS_PAD = 512
HALF = 256
SIG = 72
CONV = 192
PAIR_SIG, PAIR_CONV = 2 * SIG, 2 * CONV
PAIR = PAIR_SIG + PAIR_CONV
VMEM_LIMIT = 34 << 20

VMEM = pl.BlockSpec(memory_space=pltpu.VMEM)
SMEM = pl.BlockSpec(memory_space=pltpu.SMEM)


def shift(x, axis, by):
    n = lax.axis_size(axis)
    return lax.ppermute(x, axis, [(i, (i + by) % n) for i in range(n)])


def ordered(zh, keep, got, axis):
    first = jnp.where(zh == 0, keep, got)
    second = jnp.where(zh == 0, got, keep)
    return jnp.concatenate([first, second], axis=axis)


def gather_y(block):
    n = lax.axis_size("y")
    me = lax.axis_index("y")
    rows = block.shape[0]
    full = jnp.zeros((n,) + block.shape, block.dtype)

    def put(full, part, owner, row=0):
        return lax.dynamic_update_slice(full, part[None], (owner % n, row, 0))

    full = put(full, block, me)
    right = left = block
    for step in range(1, n // 2):
        right = shift(right, "y", 1)
        left = shift(left, "y", -1)
        full = put(full, right, me - step + n)
        full = put(full, left, me + step)
    half = rows // 2
    far = me + n // 2
    full = put(full, shift(right[:half], "y", 1), far)
    full = put(full, shift(left[half:], "y", -1), far, half)
    return full


def exchange(sig, conv):
    xh = lax.axis_index("xh")
    sig = jnp.pad(sig, ((0, 0), (0, CONV - SIG), (0, 0)))
    first = jnp.where(xh == 0, sig, conv)
    second = jnp.where(xh == 0, conv, sig)
    got = lax.all_to_all(
        jnp.concatenate([first, second]), ("xh", "zh"), split_axis=0, concat_axis=0, tiled=True
    )
    got = got.reshape((2, 2) + conv.shape[1:])
    return (
        jnp.where(xh == 0, got[0, :, :SIG], got[1, :, :SIG]),
        jnp.where(xh == 0, got[1], got[0]),
    )


def forward_kernel(
    at_ref, feat_ref, g_ref, gain_ref, mine_ref, other_ref,
    img_ref, a_ref, b_ref, stat_ref, nat_ref, part_ref, fp_ref, acc_ref,
):
    for y in range(N_Y):
        nat_ref[PAIR_SIG * y : PAIR_SIG * (y + 1)] = feat_ref[y, :PAIR_SIG].astype(F32)
        base = PAIR_SIG * N_Y + PAIR_CONV * y
        nat_ref[base : base + PAIR_CONV] = feat_ref[y, PAIR_SIG:].astype(F32)
    for x in range(N_X):
        part_ref[x * ROWS_PAD + ROWS : (x + 1) * ROWS_PAD] = jnp.zeros(
            (ROWS_PAD - ROWS, HALF), F32
        )
    for c in range(2):
        for z in range(N_ZL):
            for x in range(N_X):
                row = ((x * N_ZL + z) * 2 + c) * ROWS
                part_ref[x * ROWS_PAD : x * ROWS_PAD + ROWS] = nat_ref[row : row + ROWS]
            fp_ref[c, z] = part_ref[...].astype(BF)
    core = at_ref[0]
    for c in range(2):
        for k, (w_ref, which) in enumerate(((mine_ref, core), (other_ref, 1 - core))):
            for z in range(N_ZL):
                term = lax.dot_general(
                    fp_ref[which, z],
                    w_ref[c * N_ZL + z],
                    (((0,), (0,)), ((), ())),
                    preferred_element_type=F32,
                )
                if k == 0 and z == 0:
                    acc_ref[...] = term
                else:
                    acc_ref[...] += term
        v = acc_ref[...].T
        v2 = v * v
        t = jnp.tanh(GELU_K * (v + GELU_C * v2 * v))
        image = (0.5 * v * (1.0 + t)).astype(BF)
        slope = 0.5 * (1.0 + t) + 0.5 * v * (1.0 - t * t) * GELU_K * (1.0 + 3.0 * GELU_C * v2)
        img_ref[c] = image
        m = image.astype(F32)
        cot = g_ref[c].astype(F32) * gain_ref[c]
        square = jnp.sum(m * m, axis=0, keepdims=True)
        cross = jnp.sum(cot * m, axis=0, keepdims=True)
        a_ref[c] = slope * cot
        b_ref[c] = slope * m
        if c == 0:
            stat_ref[0:1] = square
            stat_ref[1:2] = cross
        else:
            stat_ref[0:1] += square
            stat_ref[1:2] += cross


def forward(at, feats, g, gain, mine, other):
    return pl.pallas_call(
        forward_kernel,
        in_specs=[SMEM] + [VMEM] * 5,
        out_specs=[VMEM] * 4,
        out_shape=[
            jax.ShapeDtypeStruct((2, COLS_PAD, HALF), BF),
            jax.ShapeDtypeStruct((2, COLS_PAD, HALF), F32),
            jax.ShapeDtypeStruct((2, COLS_PAD, HALF), F32),
            jax.ShapeDtypeStruct((2, HALF), F32),
        ],
        scratch_shapes=[
            pltpu.VMEM((TOTAL, HALF), F32),
            pltpu.VMEM((DEEP, HALF), F32),
            pltpu.VMEM((2, N_ZL, DEEP, HALF), BF),
            pltpu.VMEM((HALF, COLS_PAD), F32),
        ],
        compiler_params=pltpu.CompilerParams(vmem_limit_bytes=VMEM_LIMIT),
        name="forward",
    )(at, feats, g, gain, mine, other)


def backward_kernel(
    width, at_ref, a_ref, b_ref, img_ref, gain_ref, stat_ref, mine_ref, other_ref,
    p_ref, n_ref, gp_ref, pp_ref, nat_ref,
):
    stat = jnp.sum(stat_ref[...], axis=0)
    inv = lax.rsqrt(stat[0:1] / width + EPS)
    back = inv * inv * inv * stat[1:2] / width
    for c in range(2):
        gp_ref[c] = (inv * a_ref[c] - back * b_ref[c]).astype(BF)
        n_ref[c] = (img_ref[c].astype(F32) * inv * gain_ref[c]).astype(BF)
    core = at_ref[0]
    for w_ref, which in ((mine_ref, core), (other_ref, 1 - core)):
        for z in range(N_ZL):
            p = jnp.dot(w_ref[z], gp_ref[0], preferred_element_type=F32)
            p += jnp.dot(w_ref[N_ZL + z], gp_ref[1], preferred_element_type=F32)
            pp_ref[which, z] = p
    for c in range(2):
        for z in range(N_ZL):
            for x in range(N_X):
                row = ((x * N_ZL + z) * 2 + c) * ROWS
                nat_ref[row : row + ROWS] = pp_ref[c, z, x * ROWS_PAD : x * ROWS_PAD + ROWS]
    for y in range(N_Y):
        p_ref[y, :PAIR_SIG] = nat_ref[PAIR_SIG * y : PAIR_SIG * (y + 1)].astype(BF)
        base = PAIR_SIG * N_Y + PAIR_CONV * y
        p_ref[y, PAIR_SIG:] = nat_ref[base : base + PAIR_CONV].astype(BF)


def backward(at, a, b, image, gain, stat, mine, other, width):
    return pl.pallas_call(
        functools.partial(backward_kernel, width),
        in_specs=[SMEM] + [VMEM] * 7,
        out_specs=[VMEM] * 2,
        out_shape=[
            jax.ShapeDtypeStruct((N_Y, PAIR, HALF), BF),
            jax.ShapeDtypeStruct((2, COLS_PAD, HALF), BF),
        ],
        scratch_shapes=[
            pltpu.VMEM((2, COLS_PAD, HALF), BF),
            pltpu.VMEM((2, N_ZL, DEEP, HALF), F32),
            pltpu.VMEM((TOTAL, HALF), F32),
        ],
        compiler_params=pltpu.CompilerParams(vmem_limit_bytes=VMEM_LIMIT),
        name="backward",
    )(at, a, b, image, gain, stat, mine, other)


def per_device(sig_feat, conv_feat, weight, gain, text, grad_out, tile_count, tile_block):
    zh = lax.axis_index("zh")
    slots, tile_tokens = sig_feat.shape[:2]
    tokens = slots * tile_tokens
    model_width = COLS * N_Y * 2
    at = lax.axis_index("core").astype(jnp.int32).reshape(1)

    g0 = gain.astype(BF)
    g1 = (gain - g0.astype(F32)).astype(BF)
    g2 = (gain - g0.astype(F32) - g1.astype(F32)).astype(BF)
    spare = jnp.stack([g0, g1, g2, jnp.zeros_like(g0)])
    w_own = jnp.pad(jnp.concatenate([weight, spare]), ((0, 0), (0, COLS_PAD - COLS)))
    w_x = lax.all_gather(w_own, ("xh", "xl"), axis=0)
    w_x, sig_feat, conv_feat = lax.optimization_barrier((w_x, sig_feat, conv_feat))
    mine = lax.all_gather(w_x.reshape(DEEP, COLS_PAD), ("zh", "zl"), axis=0)

    def by_half(x):
        return jnp.stack([x[:, :HALF], x[:, HALF:]])

    sig, conv = exchange(
        by_half(sig_feat.reshape(tokens, SIG).T), by_half(conv_feat.reshape(tokens, CONV).T)
    )
    feats = gather_y(
        jnp.concatenate([sig.reshape(PAIR_SIG, HALF), conv.reshape(PAIR_CONV, HALF)])
    )

    live = jnp.arange(slots, dtype=jnp.int32) < tile_count[0]
    block_of = jnp.where(live, tile_block[0, :slots], -1)
    slot_block = jnp.repeat(block_of, tile_tokens)
    place = jnp.arange(tokens, dtype=jnp.int32) % tile_tokens
    seq_block = jnp.arange(tokens, dtype=jnp.int32) // tile_tokens
    chooser = (
        (slot_block[:, None] == seq_block[None, :]) & (place[:, None] == place[None, :])
    ).astype(BF)
    is_image = jnp.any(block_of[:, None] == jnp.arange(slots, dtype=jnp.int32)[None, :], axis=0)
    is_image = jnp.repeat(is_image, tile_tokens)

    def half_of(x, which):
        return lax.dynamic_slice_in_dim(x, which * HALF, HALF, 1)

    grad_slots = lax.dot_general(
        grad_out.T, chooser, (((1,), (1,)), ((), ())), preferred_element_type=F32
    ).astype(BF)
    grad_got = shift(half_of(grad_slots, 1 - zh), "zh", 1)
    g = ordered(zh, half_of(grad_slots, zh)[None], grad_got[None], 0)
    g = jnp.pad(g, ((0, 0), (0, COLS_PAD - COLS), (0, 0)))

    mine, feats, g = lax.optimization_barrier((mine, feats, g))
    other = shift(mine, "core", 1)
    spare = mine[::N_ZL, ROWS : ROWS + 3].astype(F32)
    gain_pair = (spare[:, 0] + spare[:, 1] + spare[:, 2])[:, :, None]

    image, a, b, stat = forward(at, feats, g, gain_pair, mine, other)
    stat = lax.all_to_all(
        jnp.broadcast_to(stat[None], (N_Y,) + stat.shape), "y", 0, 0, tiled=True
    )
    p, n_image = backward(at, a, b, image, gain_pair, stat, mine, other, float(model_width))
    text_f = text.T.astype(F32)
    text_square, p = lax.optimization_barrier((jnp.sum(text_f * text_f, axis=0), p))
    grads = lax.psum_scatter(
        p.reshape(TOTAL, HALF), "y", scatter_dimension=0, tiled=True
    )

    n_image = n_image[:, :COLS]
    n_keep = lax.dynamic_index_in_dim(n_image, zh, 0, keepdims=False)
    n_got = shift(lax.dynamic_index_in_dim(n_image, 1 - zh, 0, keepdims=False), "zh", 1)
    n_slots = ordered(zh, n_keep, n_got, 1)
    n_placed = jnp.dot(n_slots, chooser, preferred_element_type=F32).astype(BF)
    text_square = lax.psum(text_square, "y")
    text_square = text_square + shift(text_square, "zh", 1)
    inv_text = lax.rsqrt(text_square / model_width + EPS)
    n_text = (text_f * inv_text[None, :] * gain[:, None]).astype(BF)
    normed = jnp.where(is_image[None, :], n_placed, n_text).T

    sig_g, conv_g = exchange(
        grads[:PAIR_SIG].reshape(2, SIG, HALF), grads[PAIR_SIG:].reshape(2, CONV, HALF)
    )

    def tokens_first(x, width):
        return jnp.concatenate([x[0], x[1]], axis=1).T.reshape(slots, tile_tokens, width)

    return normed, tokens_first(sig_g, SIG), tokens_first(conv_g, CONV)


def solution(mesh):
    fine = Mesh(mesh.devices.reshape(SIZES), AXES)
    dp, mp = ("xh", "xl", "zl", "core"), ("y", "zh")
    return jax.shard_map(
        per_device,
        mesh=fine,
        in_specs=(
            P(dp, None, mp),
            P(dp, None, mp),
            P(dp, mp),
            P(mp),
            P(dp, mp),
            P(dp, mp),
            P(dp),
            P(dp, None),
        ),
        out_specs=(P(dp, mp), P(dp, None, mp), P(dp, None, mp)),
        check_vma=False,
    )
```

time: 284 us -> 225 us (0.79)
  waiting for transfers between devices: 96.8 us -> 58.3 us
  local copies, waits for them, and re-layouts: 46.1 us -> 19 us
  blocking collectives: 16.8 us -> 31 us
  starting transfers between devices: 81.3 us -> 78.3 us
    ppermute x8 -> x0, starting transfers between devices: 46.6 us -> none  [swap(): return lax.ppermute(x, ('x', 'zh'), pairs)]
    all_gather x1, waiting for transfers between devices: 44.8 us -> 2.1 us  [per_device(): mine = lax.all_gather(w_x.reshape(DEEP, COLS_PAD), ('zh', 'zl'), axis=0)]
    all_to_all x0 -> x3, starting transfers between devices: none -> 28.8 us  [the longest x2 21.7 us: exchange(): lax.all_to_all(jnp.concatenate([first, second]), ('xh', 'zh'), split_axis...]
    all_to_all x0 -> x3, waiting for transfers between devices: none -> 21.7 us  [the longest x2 15.1 us: exchange(): lax.all_to_all(jnp.concatenate([first, second]), ('xh', 'zh'), split_axis...]
    ppermute x8 -> x0, waiting for transfers between devices: 18.3 us -> none  [swap(): return lax.ppermute(x, ('x', 'zh'), pairs)]
    all_gather x0 -> x1, blocking collectives: none -> 16.2 us  [per_device(): w_x = lax.all_gather(w_own, ('xh', 'xl'), axis=0)]
    ppermute x9 -> x12, starting transfers between devices: 34.6 us -> 49.4 us  [shift(): return lax.ppermute(x, axis, [(i, (i + by) % n) for i in range(n)])]
    ppermute x9 -> x12, waiting for transfers between devices: 8.69 us -> 20 us  [shift(): return lax.ppermute(x, axis, [(i, (i + by) % n) for i in range(n)])]
  transfers between devices with their start and end apart: 19 -> 17, of which waited for: 10 -> 11; matrix products, arithmetic and copies ran while one was open for 13% -> 5% of each run, Pallas kernels for 0% -> 0%
where the time goes in v2:
time: 225 us; the launch traced here: 223 us
  starting transfers between devices  78.3 us (35%)
  waiting for transfers between devices  58.3 us (26%)
  blocking collectives  31 us (14%)
  local copies, waits for them, and re-layouts  19 us (8%)
  between operations  15.3 us (7%)
  Pallas kernels  13.7 us (6%)
  other arithmetic  5.59 us (2%)
    ppermute x12, starting transfers between devices, shift(): return lax.ppermute(x, axis, [(i, (i + by) % n) for i in range(n)])  49.4 us
    all_to_all x2, starting transfers between devices, exchange(): lax.all_to_all(jnp.concatenate([first, second]), ('xh', 'zh'), split_axis...  21.7 us
    ppermute x12, waiting for transfers between devices, shift(): return lax.ppermute(x, axis, [(i, (i + by) % n) for i in range(n)])  20 us
    all_gather x1, blocking collectives, per_device(): w_x = lax.all_gather(w_own, ('xh', 'xl'), axis=0)  16.2 us
    all_to_all x2, waiting for transfers between devices, exchange(): lax.all_to_all(jnp.concatenate([first, second]), ('xh', 'zh'), split_axis...  15.1 us
    psum x1, blocking collectives, per_device(): text_square = lax.psum(text_square, 'y')  14.8 us
    reduce_scatter x1, waiting for transfers between devices, per_device(): lax.psum_scatter(p.reshape(TOTAL, HALF), 'y', scatter_dimension=0, tiled=...  14.5 us
    unnamed x28, local copies, waits for them, and re-layouts  11.8 us
  transfers between devices with their start and end apart: 17, of which 11 were waited for; matrix products, arithmetic and copies ran while one was open for 5% of the time, Pallas kernels for 0%

profile of v2, /device:TPU:6, one launch (start us, length us, event | category | flops | bytes accessed | tf_op | source)
XLA Modules:
  0.0 223.2 jit_solution(10253827040973212590)
XLA Ops:
  8.0 1.0 concatenate.24
  9.0 16.2 %all-gather = bf16[544,512]{1,0:T(8,128)(2,1)} all-gather(bf16[136,512]{1,0:T(8,128)(2,1)S(1)} %pad.15), channel_id=2, replica_groups=mesh['xh'=2,'xl'=2,'zl'=4,'core'=2,'y'=8,'zh'=2] {'xh','xl'}, dimensions={0}, use_global_device_ids=true | all-gather | bytes 696320 | tf_op jit(solution)/shard_map/all_gather | solution.py:218
  25.3 1.1 copy.29
  27.4 11.3 %all-to-all-start = ((bf16[4,192,256]{2,1,0:T(8,128)(2,1)}), bf16[4,192,256]{2,1,0:T(8,128)(2,1)S(1)}, u32[]{:S(2)}, u32[]{:S(2)}) async-start(bf16[4,192,256]{2,1,0:T(8,128)(2,1)} %pad_maximum_fusion), calls=%async_computation | async-start | bytes 786432 | tf_op jit(solution)/shard_map/all_to_all | solution.py:76
  40.2 7.3 %collective-permute-start.8 = (bf16[448,256]{1,0:T(8,128)(2,1)S(1)}, bf16[448,256]{1,0:T(8,128)(2,1)S(1)}, u32[]{:S(2)}, u32[]{:S(2)}) collective-permute-start(bf16[448,256]{1,0:T(8,128)(2,1)S(1)} %dynamic-slice_bitcast_fusion.1), channel_id=1, source_target_pairs={{0,1},{1,0},{2,3},{3,2},{4,5},{5,4},{6,7},{7,6},{8,9},{9,8},{10,11... | collective-permute-start | bytes 688136 | tf_op jit(solution)/shard_map/ppermute | solution.py:39
  47.6 6.6 %all-to-all-done = bf16[4,192,256]{2,1,0:T(8,128)(2,1)S(1)} async-done(((bf16[4,192,256]{2,1,0:T(8,128)(2,1)}), bf16[4,192,256]{2,1,0:T(8,128)(2,1)S(1)}, u32[]{:S(2)}, u32[]{:S(2)}) %all-to-all-start) | async-done | bytes 393248 | tf_op jit(solution)/shard_map/all_to_all | solution.py:76
  54.3 3.6 %collective-permute-start = (bf16[528,256]{1,0:T(8,128)(2,1)S(1)}, bf16[528,256]{1,0:T(8,128)(2,1)S(1)}, u32[]{:S(2)}, u32[]{:S(2)}) collective-permute-start(bf16[528,256]{1,0:T(8,128)(2,1)S(1)} %pad_maximum_fusion.2), channel_id=1, source_target_pairs={{0,2},{2,4},{4,6},{6,8},{8,10},{10,12},{12,14},{14,0},{1,3},{3,5},... | collective-permute-start | bytes 811016 | tf_op jit(solution)/shard_map/ppermute | solution.py:39
  57.9 4.6 %collective-permute-start.1 = (bf16[528,256]{1,0:T(8,128)(2,1)S(1)}, bf16[528,256]{1,0:T(8,128)(2,1)S(1)}, u32[]{:S(2)}, u32[]{:S(2)}) collective-permute-start(bf16[528,256]{1,0:T(8,128)(2,1)S(1)} %pad_maximum_fusion.2), channel_id=1, source_target_pairs={{0,14},{2,0},{4,2},{6,4},{8,6},{10,8},{12,10},{14,12},{1,15},{3,1}... | collective-permute-start | bytes 811016 | tf_op jit(solution)/shard_map/ppermute | solution.py:39
  62.5 2.7 %collective-permute-done.8 = bf16[448,256]{1,0:T(8,128)(2,1)S(1)} collective-permute-done((bf16[448,256]{1,0:T(8,128)(2,1)S(1)}, bf16[448,256]{1,0:T(8,128)(2,1)S(1)}, u32[]{:S(2)}, u32[]{:S(2)}) %collective-permute-start.8) | collective-permute-done | bytes 229408 | tf_op jit(solution)/shard_map/ppermute | solution.py:39
  65.3 0.8 fusion.6.g_ref
  66.3 3.6 %collective-permute-start.2 = (bf16[528,256]{1,0:T(8,128)(2,1)S(1)}, bf16[528,256]{1,0:T(8,128)(2,1)S(1)}, u32[]{:S(2)}, u32[]{:S(2)}) collective-permute-start(bf16[528,256]{1,0:T(8,128)(2,1)S(1)} %collective-permute-done), channel_id=1, source_target_pairs={{0,2},{2,4},{4,6},{6,8},{8,10},{10,12},{12,14},{14,0},{1,3},{3,5},... | collective-permute-start | bytes 811016 | tf_op jit(solution)/shard_map/ppermute | solution.py:39
  69.9 4.5 %collective-permute-start.3 = (bf16[528,256]{1,0:T(8,128)(2,1)S(1)}, bf16[528,256]{1,0:T(8,128)(2,1)S(1)}, u32[]{:S(2)}, u32[]{:S(2)}) collective-permute-start(bf16[528,256]{1,0:T(8,128)(2,1)S(1)} %collective-permute-done.1), channel_id=1, source_target_pairs={{0,14},{2,0},{4,2},{6,4},{8,6},{10,8},{12,10},{14,12},{1,15},{3,1}... | collective-permute-start | bytes 811016 | tf_op jit(solution)/shard_map/ppermute | solution.py:39
  74.5 5.1 %collective-permute-done.2 = bf16[528,256]{1,0:T(8,128)(2,1)S(1)} collective-permute-done((bf16[528,256]{1,0:T(8,128)(2,1)S(1)}, bf16[528,256]{1,0:T(8,128)(2,1)S(1)}, u32[]{:S(2)}, u32[]{:S(2)}) %collective-permute-start.2) | collective-permute-done | bytes 270368 | tf_op jit(solution)/shard_map/ppermute | solution.py:39
  79.6 1.9 collective-permute-start.4
  81.5 5.1 %collective-permute-start.5 = (bf16[528,256]{1,0:T(8,128)(2,1)S(1)}, bf16[528,256]{1,0:T(8,128)(2,1)S(1)}, u32[]{:S(2)}, u32[]{:S(2)}) collective-permute-start(bf16[528,256]{1,0:T(8,128)(2,1)S(1)} %collective-permute-done.3), channel_id=1, source_target_pairs={{0,14},{2,0},{4,2},{6,4},{8,6},{10,8},{12,10},{14,12},{1,15},{3,1}... | collective-permute-start | bytes 811016 | tf_op jit(solution)/shard_map/ppermute | solution.py:39
  86.8 2.9 %collective-permute-done.4 = bf16[528,256]{1,0:T(8,128)(2,1)S(1)} collective-permute-done((bf16[528,256]{1,0:T(8,128)(2,1)S(1)}, bf16[528,256]{1,0:T(8,128)(2,1)S(1)}, u32[]{:S(2)}, u32[]{:S(2)}) %collective-permute-start.4) | collective-permute-done | bytes 270368 | tf_op jit(solution)/shard_map/ppermute | solution.py:39
  89.7 1.9 collective-permute-start.6
  91.7 5.1 %collective-permute-start.7 = (bf16[264,256]{1,0:T(8,128)(2,1)S(1)}, bf16[264,256]{1,0:T(8,128)(2,1)S(1)}, u32[]{:S(2)}, u32[]{:S(2)}) collective-permute-start(bf16[264,256]{1,0:T(8,128)(2,1)S(1)} %slice.115), channel_id=1, source_target_pairs={{0,14},{2,0},{4,2},{6,4},{8,6},{10,8},{12,10},{14,12},{1,15},{3,1}... | collective-permute-start | bytes 405512 | tf_op jit(solution)/shard_map/ppermute | solution.py:39
  96.9 1.0 collective-permute-done.6
  97.8 1.5 collective-permute-done.7
  99.4 2.1 all-gather.3.cloned.1.call-done.mine_ref
  101.5 2.0 collective-permute-start.9
  104.4 6.8 %collective-permute-done.9.other_ref = bf16[8,544,512]{2,1,0:T(8,128)(2,1)} collective-permute-done((bf16[8,544,512]{2,1,0:T(8,128)(2,1)}, bf16[8,544,512]{2,1,0:T(8,128)(2,1)}, u32[]{:S(2)}, u32[]{:S(2)}) %collective-permute-start.9) | collective-permute-done | bytes 4456480 | tf_op jit(solution)/shard_map/ppermute | solution.py:39
  111.2 2.3 %copy-done.1 = bf16[8,544,512]{2,1,0:T(8,128)(2,1)S(1)} copy-done((bf16[8,544,512]{2,1,0:T(8,128)(2,1)S(1)}, bf16[8,544,512]{2,1,0:T(8,128)(2,1)}, u32[]{:S(2)}) %copy-start.1) | copy-done | bytes 4456472
  113.5 1.0 copy-done.3
  114.5 7.1 %forward.1 = (bf16[2,512,256]{2,1,0:T(8,128)(2,1)S(1)}, f32[2,512,256]{2,1,0:T(8,128)S(1)}, f32[2,512,256]{2,1,0:T(8,128)S(1)}, f32[2,256]{1,0:T(2,128)S(1)}) custom-call(s32[1]{0:T(128)} %bitcast.2.at_ref, bf16[8,528,256]{2,1,0:T(8,128)(2,1)S(1)} %bitcast_dynamic-update-slice_fusion.7.feat_ref, bf16[2,512,256]{2,1,0:T(8,128)(2,1)S(1)} %copy-done.3, ...), custom_call_target="tpu_custom_call" | custom-call | tf_op jit(solution)/shard_map/forward/pallas_call | solution.py:139
  121.6 0.9 copy-done.4
  122.5 1.0 copy-done.6
  123.5 0.8 copy-done.8
  124.9 7.1 %all-to-all-start.1 = ((f32[8,2,256]{2,1,0:T(2,128)}), f32[8,2,256]{2,1,0:T(2,128)S(1)}, u32[]{:S(2)}, u32[]{:S(2)}) async-start(f32[8,2,256]{2,1,0:T(2,128)} %broadcast_in_dim.81), calls=%async_computation.1 | async-start | bytes 32768 | tf_op jit(solution)/shard_map/all_to_all | solution.py:259
  132.1 1.2 fusion.3
  133.2 6.6 %all-to-all-done.1.stat_ref = f32[8,2,256]{2,1,0:T(2,128)S(1)} async-done(((f32[8,2,256]{2,1,0:T(2,128)}), f32[8,2,256]{2,1,0:T(2,128)S(1)}, u32[]{:S(2)}, u32[]{:S(2)}) %all-to-all-start.1) | async-done | bytes 16416 | tf_op jit(solution)/shard_map/all_to_all | solution.py:259
  139.8 2.3 %copy-done.2 = bf16[8,544,512]{2,1,0:T(8,128)(2,1)S(1)} copy-done((bf16[8,544,512]{2,1,0:T(8,128)(2,1)S(1)}, bf16[8,544,512]{2,1,0:T(8,128)(2,1)}, u32[]{:S(2)}) %copy-start.2) | copy-done | bytes 4456472
  142.1 1.2 copy-done.5
  143.3 1.2 copy-done.7
  144.5 1.0 copy-done.9
  145.6 6.7 %backward.1 = (bf16[8,528,256]{2,1,0:T(8,128)(2,1)}, bf16[2,512,256]{2,1,0:T(8,128)(2,1)S(1)}) custom-call(s32[1]{0:T(128)} %bitcast.2.at_ref, f32[2,512,256]{2,1,0:T(8,128)S(1)} %copy-done.5, f32[2,512,256]{2,1,0:T(8,128)S(1)} %copy-done.7, bf16[2,512,256]{2,1,0:T(8,128)(2,1)S(1)} %copy-done.9, f32[2,512,1]{2,1,0:T(8,128)S(1)} %add.193.gain_ref, ...), custom_call_target="tpu_custom_call" | custom-call | tf_op jit(solution)/shard_map/backward/pallas_call | solution.py:188
  152.5 14.8 %psum.7 = f32[512]{0:T(512)S(1)} all-reduce(f32[512]{0:T(512)S(1)} %fusion.3), channel_id=1, replica_groups=mesh['xh'=2,'xl'=2,'zl'=4,'core'=2,'y'=8,'zh'=2] {'y'}, use_global_device_ids=true, to_apply=%region_2.3 | all-reduce | flops 512 | bytes 4096 | tf_op jit(solution)/shard_map/psum | solution.py:274
  167.3 3.3 %collective-permute-start.11 = (f32[512]{0:T(512)S(1)}, f32[512]{0:T(512)S(1)}, u32[]{:S(2)}, u32[]{:S(2)}) collective-permute-start(f32[512]{0:T(512)S(1)} %psum.7), channel_id=1, source_target_pairs={{0,1},{1,0},{2,3},{3,2},{4,5},{5,4},{6,7},{7,6},{8,9},{9,8},{10,11... | collective-permute-start | bytes 6152 | tf_op jit(solution)/shard_map/ppermute | solution.py:39
  170.7 6.5 %collective-permute-start.10 = (bf16[448,256]{1,0:T(8,128)(2,1)S(1)}, bf16[448,256]{1,0:T(8,128)(2,1)S(1)}, u32[]{:S(2)}, u32[]{:S(2)}) collective-permute-start(bf16[448,256]{1,0:T(8,128)(2,1)S(1)} %dynamic-slice_bitcast_fusion), channel_id=1, source_target_pairs={{0,1},{1,0},{2,3},{3,2},{4,5},{5,4},{6,7},{7,6},{8,9},{9,8},{10,11... | collective-permute-start | bytes 688136 | tf_op jit(solution)/shard_map/ppermute | solution.py:39
  177.3 14.5 %reduce-scatter.2.cloned.1.call-done = bf16[528,256]{1,0:T(8,128)(2,1)} async-done(((bf16[4224,256]{1,0:T(8,128)(2,1)}), bf16[528,256]{1,0:T(8,128)(2,1)}) %reduce-scatter.2.cloned.1.call-update) | async-done | bytes 270352 | tf_op jit(solution)/shard_map/reduce_scatter | solution.py:265
  191.7 0.9 slice.120
  192.7 0.9 slice.119
  193.6 0.8 pad_maximum_fusion.1
  194.4 10.3 %all-to-all-start.2 = ((bf16[4,192,256]{2,1,0:T(8,128)(2,1)}), bf16[4,192,256]{2,1,0:T(8,128)(2,1)S(1)}, u32[]{:S(2)}, u32[]{:S(2)}) async-start(bf16[4,192,256]{2,1,0:T(8,128)(2,1)} %pad_maximum_fusion.1), calls=%async_computation.3 | async-start | bytes 786432 | tf_op jit(solution)/shard_map/all_to_all | solution.py:76
  204.9 1.3 fusion
  206.2 8.5 %all-to-all-done.2 = bf16[4,192,256]{2,1,0:T(8,128)(2,1)S(1)} async-done(((bf16[4,192,256]{2,1,0:T(8,128)(2,1)}), bf16[4,192,256]{2,1,0:T(8,128)(2,1)S(1)}, u32[]{:S(2)}, u32[]{:S(2)}) %all-to-all-start.2) | async-done | bytes 393248 | tf_op jit(solution)/shard_map/all_to_all | solution.py:76
  214.7 0.8 copy.33
  (81 shorter events, 6.1 us)
Async XLA Ops:
  7.2 32.4 %copy-start = (bf16[512,448]{0,1:T(8,128)(2,1)S(1)}, bf16[512,448]{0,1:T(8,128)(2,1)}, u32[]{:S(2)}) copy-start(bf16[512,448]{0,1:T(8,128)(2,1)} %param.13) | copy-start | bytes 1376260
  7.2 19.2 %copy-start.11 = (bf16[8,64,72]{2,1,0:T(8,128)(2,1)S(1)}, bf16[8,64,72]{2,1,0:T(8,128)(2,1)}, u32[]{:S(2)}) copy-start(bf16[8,64,72]{2,1,0:T(8,128)(2,1)} %param.8) | copy-start | bytes 221188
  7.2 94.3 %all-gather.3.cloned.1.call-start = ((), (), s32[]{:S(2)}) async-start(), calls=%async_computation.4 | async-start | bytes 5013504 | tf_op jit(solution)/shard_map/all_gather | solution.py:220
  25.2 14.1 %copy-start.13 = (s32[1,8]{1,0:T(1,128)S(1)}, s32[1,8]{1,0:T(1,128)}, u32[]{:S(2)}) copy-start(s32[1,8]{1,0:T(1,128)} %param.15) | copy-start | bytes 100
  27.4 26.9 %all-to-all-start = ((bf16[4,192,256]{2,1,0:T(8,128)(2,1)}), bf16[4,192,256]{2,1,0:T(8,128)(2,1)S(1)}, u32[]{:S(2)}, u32[]{:S(2)}) async-start(bf16[4,192,256]{2,1,0:T(8,128)(2,1)} %pad_maximum_fusion), calls=%async_computation | async-start | bytes 786432 | tf_op jit(solution)/shard_map/all_to_all | solution.py:76
  40.2 25.0 %collective-permute-start.8 = (bf16[448,256]{1,0:T(8,128)(2,1)S(1)}, bf16[448,256]{1,0:T(8,128)(2,1)S(1)}, u32[]{:S(2)}, u32[]{:S(2)}) collective-permute-start(bf16[448,256]{1,0:T(8,128)(2,1)S(1)} %dynamic-slice_bitcast_fusion.1), channel_id=1, source_target_pairs={{0,1},{1,0},{2,3},{3,2},{4,5},{5,4},{6,7},{7,6},{8,9},{9,8},{10,11... | collective-permute-start | bytes 688136 | tf_op jit(solution)/shard_map/ppermute | solution.py:39
  54.3 12.0 %collective-permute-start = (bf16[528,256]{1,0:T(8,128)(2,1)S(1)}, bf16[528,256]{1,0:T(8,128)(2,1)S(1)}, u32[]{:S(2)}, u32[]{:S(2)}) collective-permute-start(bf16[528,256]{1,0:T(8,128)(2,1)S(1)} %pad_maximum_fusion.2), channel_id=1, source_target_pairs={{0,2},{2,4},{4,6},{6,8},{8,10},{10,12},{12,14},{14,0},{1,3},{3,5},... | collective-permute-start | bytes 811016 | tf_op jit(solution)/shard_map/ppermute | solution.py:39
  57.9 12.0 %collective-permute-start.1 = (bf16[528,256]{1,0:T(8,128)(2,1)S(1)}, bf16[528,256]{1,0:T(8,128)(2,1)S(1)}, u32[]{:S(2)}, u32[]{:S(2)}) collective-permute-start(bf16[528,256]{1,0:T(8,128)(2,1)S(1)} %pad_maximum_fusion.2), channel_id=1, source_target_pairs={{0,14},{2,0},{4,2},{6,4},{8,6},{10,8},{12,10},{14,12},{1,15},{3,1}... | collective-permute-start | bytes 811016 | tf_op jit(solution)/shard_map/ppermute | solution.py:39
  66.3 13.3 %collective-permute-start.2 = (bf16[528,256]{1,0:T(8,128)(2,1)S(1)}, bf16[528,256]{1,0:T(8,128)(2,1)S(1)}, u32[]{:S(2)}, u32[]{:S(2)}) collective-permute-start(bf16[528,256]{1,0:T(8,128)(2,1)S(1)} %collective-permute-done), channel_id=1, source_target_pairs={{0,2},{2,4},{4,6},{6,8},{8,10},{10,12},{12,14},{14,0},{1,3},{3,5},... | collective-permute-start | bytes 811016 | tf_op jit(solution)/shard_map/ppermute | solution.py:39
  69.9 11.6 %collective-permute-start.3 = (bf16[528,256]{1,0:T(8,128)(2,1)S(1)}, bf16[528,256]{1,0:T(8,128)(2,1)S(1)}, u32[]{:S(2)}, u32[]{:S(2)}) collective-permute-start(bf16[528,256]{1,0:T(8,128)(2,1)S(1)} %collective-permute-done.1), channel_id=1, source_target_pairs={{0,14},{2,0},{4,2},{6,4},{8,6},{10,8},{12,10},{14,12},{1,15},{3,1}... | collective-permute-start | bytes 811016 | tf_op jit(solution)/shard_map/ppermute | solution.py:39
  79.6 10.1 %collective-permute-start.4 = (bf16[528,256]{1,0:T(8,128)(2,1)S(1)}, bf16[528,256]{1,0:T(8,128)(2,1)S(1)}, u32[]{:S(2)}, u32[]{:S(2)}) collective-permute-start(bf16[528,256]{1,0:T(8,128)(2,1)S(1)} %collective-permute-done.2), channel_id=1, source_target_pairs={{0,2},{2,4},{4,6},{6,8},{8,10},{10,12},{12,14},{14,0},{1,3},{3,5},... | collective-permute-start | bytes 811016 | tf_op jit(solution)/shard_map/ppermute | solution.py:39
  81.5 10.1 %collective-permute-start.5 = (bf16[528,256]{1,0:T(8,128)(2,1)S(1)}, bf16[528,256]{1,0:T(8,128)(2,1)S(1)}, u32[]{:S(2)}, u32[]{:S(2)}) collective-permute-start(bf16[528,256]{1,0:T(8,128)(2,1)S(1)} %collective-permute-done.3), channel_id=1, source_target_pairs={{0,14},{2,0},{4,2},{6,4},{8,6},{10,8},{12,10},{14,12},{1,15},{3,1}... | collective-permute-start | bytes 811016 | tf_op jit(solution)/shard_map/ppermute | solution.py:39
  89.7 8.1 %collective-permute-start.6 = (bf16[264,256]{1,0:T(8,128)(2,1)S(1)}, bf16[264,256]{1,0:T(8,128)(2,1)S(1)}, u32[]{:S(2)}, u32[]{:S(2)}) collective-permute-start(bf16[264,256]{1,0:T(8,128)(2,1)S(1)} %slice.114), channel_id=1, source_target_pairs={{0,2},{2,4},{4,6},{6,8},{8,10},{10,12},{12,14},{14,0},{1,3},{3,5},... | collective-permute-start | bytes 405512 | tf_op jit(solution)/shard_map/ppermute | solution.py:39
  91.7 7.7 %collective-permute-start.7 = (bf16[264,256]{1,0:T(8,128)(2,1)S(1)}, bf16[264,256]{1,0:T(8,128)(2,1)S(1)}, u32[]{:S(2)}, u32[]{:S(2)}) collective-permute-start(bf16[264,256]{1,0:T(8,128)(2,1)S(1)} %slice.115), channel_id=1, source_target_pairs={{0,14},{2,0},{4,2},{6,4},{8,6},{10,8},{12,10},{14,12},{1,15},{3,1}... | collective-permute-start | bytes 405512 | tf_op jit(solution)/shard_map/ppermute | solution.py:39
  101.5 9.8 %collective-permute-start.9 = (bf16[8,544,512]{2,1,0:T(8,128)(2,1)}, bf16[8,544,512]{2,1,0:T(8,128)(2,1)}, u32[]{:S(2)}, u32[]{:S(2)}) collective-permute-start(bf16[8,544,512]{2,1,0:T(8,128)(2,1)} %all-gather.3.cloned.1.call-done.mine_ref), channel_id=1, source_target_pairs={{0,16},{16,0},{1,17},{17,1},{2,18},{18,2},{3,19},{19,3},{4,20},{20... | collective-permute-start | bytes 13369352 | tf_op jit(solution)/shard_map/ppermute | solution.py:39
  111.2 2.3 %copy-start.1 = (bf16[8,544,512]{2,1,0:T(8,128)(2,1)S(1)}, bf16[8,544,512]{2,1,0:T(8,128)(2,1)}, u32[]{:S(2)}) copy-start(bf16[8,544,512]{2,1,0:T(8,128)(2,1)} %all-gather.3.cloned.1.call-done.mine_ref) | copy-start | bytes 13369348
  113.5 1.0 copy-start.3
  121.6 1.0 copy-start.4
  122.5 1.0 copy-start.6
  123.5 0.8 copy-start.8
  124.9 14.9 %all-to-all-start.1 = ((f32[8,2,256]{2,1,0:T(2,128)}), f32[8,2,256]{2,1,0:T(2,128)S(1)}, u32[]{:S(2)}, u32[]{:S(2)}) async-start(f32[8,2,256]{2,1,0:T(2,128)} %broadcast_in_dim.81), calls=%async_computation.1 | async-start | bytes 32768 | tf_op jit(solution)/shard_map/all_to_all | solution.py:259
  132.0 59.7 %reduce-scatter.2.cloned.1.call-start = ((), (), s32[]{:S(2)}) async-start(), calls=%async_computation.5 | async-start | bytes 2433024 | tf_op jit(solution)/shard_map/reduce_scatter | solution.py:265
  139.8 2.3 %copy-start.2 = (bf16[8,544,512]{2,1,0:T(8,128)(2,1)S(1)}, bf16[8,544,512]{2,1,0:T(8,128)(2,1)}, u32[]{:S(2)}) copy-start(bf16[8,544,512]{2,1,0:T(8,128)(2,1)} %all-gather.3.cloned.1.call-done.mine_ref) | copy-start | bytes 13369348
  142.1 1.2 copy-start.5
  143.3 1.2 copy-start.7
  144.5 1.0 copy-start.9
  167.3 37.5 %collective-permute-start.11 = (f32[512]{0:T(512)S(1)}, f32[512]{0:T(512)S(1)}, u32[]{:S(2)}, u32[]{:S(2)}) collective-permute-start(f32[512]{0:T(512)S(1)} %psum.7), channel_id=1, source_target_pairs={{0,1},{1,0},{2,3},{3,2},{4,5},{5,4},{6,7},{7,6},{8,9},{9,8},{10,11... | collective-permute-start | bytes 6152 | tf_op jit(solution)/shard_map/ppermute | solution.py:39
  170.7 34.2 %copy-start.10 = (bf16[512,448]{0,1:T(8,128)(2,1)S(1)}, bf16[512,448]{0,1:T(8,128)(2,1)}, u32[]{:S(2)}) copy-start(bf16[512,448]{0,1:T(8,128)(2,1)} %param.12) | copy-start | bytes 1376260
  170.7 34.2 %copy-start.12 = (f32[448]{0:T(512)S(1)}, f32[448]{0:T(512)}, u32[]{:S(2)}) copy-start(f32[448]{0:T(512)} %param.11) | copy-start | bytes 5380
  170.7 34.1 %collective-permute-start.10 = (bf16[448,256]{1,0:T(8,128)(2,1)S(1)}, bf16[448,256]{1,0:T(8,128)(2,1)S(1)}, u32[]{:S(2)}, u32[]{:S(2)}) collective-permute-start(bf16[448,256]{1,0:T(8,128)(2,1)S(1)} %dynamic-slice_bitcast_fusion), channel_id=1, source_target_pairs={{0,1},{1,0},{2,3},{3,2},{4,5},{5,4},{6,7},{7,6},{8,9},{9,8},{10,11... | collective-permute-start | bytes 688136 | tf_op jit(solution)/shard_map/ppermute | solution.py:39
  194.4 20.2 %all-to-all-start.2 = ((bf16[4,192,256]{2,1,0:T(8,128)(2,1)}), bf16[4,192,256]{2,1,0:T(8,128)(2,1)S(1)}, u32[]{:S(2)}, u32[]{:S(2)}) async-start(bf16[4,192,256]{2,1,0:T(8,128)(2,1)} %pad_maximum_fusion.1), calls=%async_computation.3 | async-start | bytes 786432 | tf_op jit(solution)/shard_map/all_to_all | solution.py:76
Sparse Core Ops, SparseCore 0:
  25.4 76.0 all-gather.2
  152.4 39.3 reduce-scatter.1

commit v3 on v2

--- a/solution.py
+++ b/solution.py
@@ -28,7 +28,6 @@
 CONV = 192
 PAIR_SIG, PAIR_CONV = 2 * SIG, 2 * CONV
 PAIR = PAIR_SIG + PAIR_CONV
-VMEM_LIMIT = 34 << 20
 
 VMEM = pl.BlockSpec(memory_space=pltpu.VMEM)
 SMEM = pl.BlockSpec(memory_space=pltpu.SMEM)
@@ -68,25 +67,40 @@
     return full
 
 
-def exchange(sig, conv):
+def exchange(blocks):
     xh = lax.axis_index("xh")
-    sig = jnp.pad(sig, ((0, 0), (0, CONV - SIG), (0, 0)))
-    first = jnp.where(xh == 0, sig, conv)
-    second = jnp.where(xh == 0, conv, sig)
-    got = lax.all_to_all(
-        jnp.concatenate([first, second]), ("xh", "zh"), split_axis=0, concat_axis=0, tiled=True
-    )
-    got = got.reshape((2, 2) + conv.shape[1:])
+    got = lax.all_to_all(blocks, ("xh", "zh"), split_axis=0, concat_axis=0, tiled=True)
+    got = got.reshape((2, 2) + blocks.shape[1:])
     return (
         jnp.where(xh == 0, got[0, :, :SIG], got[1, :, :SIG]),
         jnp.where(xh == 0, got[1], got[0]),
     )
 
 
-def forward_kernel(
-    at_ref, feat_ref, g_ref, gain_ref, mine_ref, other_ref,
-    img_ref, a_ref, b_ref, stat_ref, nat_ref, part_ref, fp_ref, acc_ref,
-):
+def call(kernel, name, limit, out_shape, scratch, flops, *args):
+    moved = sum(x.size * x.dtype.itemsize for x in args)
+    moved += sum(x.size * x.dtype.itemsize for x in out_shape)
+    return pl.pallas_call(
+        kernel,
+        in_specs=[SMEM] + [VMEM] * (len(args) - 1),
+        out_specs=[VMEM] * len(out_shape),
+        out_shape=out_shape,
+        scratch_shapes=scratch,
+        compiler_params=pltpu.CompilerParams(vmem_limit_bytes=limit << 20),
+        cost_estimate=pl.CostEstimate(flops=flops, bytes_accessed=moved, transcendentals=0),
+        name=name,
+    )(*args)
+
+
+def shaped(dtype, *shape):
+    return jax.ShapeDtypeStruct(shape, dtype)
+
+
+def rows_of(x, z, c):
+    return ((x * N_ZL + z) * 2 + c) * ROWS
+
+
+def arrange_kernel(at_ref, feat_ref, mine_ref, other_ref, nat_ref, part_ref):
     for y in range(N_Y):
         nat_ref[PAIR_SIG * y : PAIR_SIG * (y + 1)] = feat_ref[y, :PAIR_SIG].astype(F32)
         base = PAIR_SIG * N_Y + PAIR_CONV * y
@@ -98,24 +112,51 @@
     for c in range(2):
         for z in range(N_ZL):
             for x in range(N_X):
-                row = ((x * N_ZL + z) * 2 + c) * ROWS
+                row = rows_of(x, z, c)
                 part_ref[x * ROWS_PAD : x * ROWS_PAD + ROWS] = nat_ref[row : row + ROWS]
-            fp_ref[c, z] = part_ref[...].astype(BF)
-    core = at_ref[0]
+            part = part_ref[...].astype(BF)
+
+            @pl.when(at_ref[0] == c)
+            def _():
+                mine_ref[z] = part
+
+            @pl.when(at_ref[0] != c)
+            def _():
+                other_ref[z] = part
+
+
+def arrange(at, feats):
+    return call(
+        arrange_kernel,
+        "arrange",
+        16,
+        [shaped(BF, N_ZL, DEEP, HALF)] * 2,
+        [pltpu.VMEM((TOTAL, HALF), F32), pltpu.VMEM((DEEP, HALF), F32)],
+        0,
+        at,
+        feats,
+    )
+
+
+def products(fp_ref, w_ref, c, total):
+    for z in range(N_ZL):
+        term = lax.dot_general(
+            fp_ref[z], w_ref[c * N_ZL + z], (((0,), (0,)), ((), ())), preferred_element_type=F32
+        )
+        total = term if total is None else total + term
+    return total
+
+
+def first_kernel(at_ref, fp_ref, w_ref, acc_ref):
     for c in range(2):
-        for k, (w_ref, which) in enumerate(((mine_ref, core), (other_ref, 1 - core))):
-            for z in range(N_ZL):
-                term = lax.dot_general(
-                    fp_ref[which, z],
-                    w_ref[c * N_ZL + z],
-                    (((0,), (0,)), ((), ())),
-                    preferred_element_type=F32,
-                )
-                if k == 0 and z == 0:
-                    acc_ref[...] = term
-                else:
-                    acc_ref[...] += term
-        v = acc_ref[...].T
+        acc_ref[c] = products(fp_ref, w_ref, c, None)
+
+
+def second_kernel(
+    at_ref, fp_ref, w_ref, acc_ref, g_ref, gain_ref, img_ref, a_ref, b_ref, stat_ref
+):
+    for c in range(2):
+        v = products(fp_ref, w_ref, c, acc_ref[c]).T
         v2 = v * v
         t = jnp.tanh(GELU_K * (v + GELU_C * v2 * v))
         image = (0.5 * v * (1.0 + t)).astype(BF)
@@ -135,33 +176,33 @@
             stat_ref[1:2] += cross
 
 
-def forward(at, feats, g, gain, mine, other):
-    return pl.pallas_call(
-        forward_kernel,
-        in_specs=[SMEM] + [VMEM] * 5,
-        out_specs=[VMEM] * 4,
-        out_shape=[
-            jax.ShapeDtypeStruct((2, COLS_PAD, HALF), BF),
-            jax.ShapeDtypeStruct((2, COLS_PAD, HALF), F32),
-            jax.ShapeDtypeStruct((2, COLS_PAD, HALF), F32),
-            jax.ShapeDtypeStruct((2, HALF), F32),
+def forward(at, fp_mine, fp_other, mine, other, g, gain):
+    flops = HALF * TOTAL * COLS * 2
+    acc = call(
+        first_kernel, "first_half", 14, [shaped(F32, 2, HALF, COLS_PAD)], [], flops,
+        at, fp_mine, mine,
+    )[0]
+    return call(
+        second_kernel,
+        "second_half",
+        18,
+        [
+            shaped(BF, 2, COLS_PAD, HALF),
+            shaped(F32, 2, COLS_PAD, HALF),
+            shaped(F32, 2, COLS_PAD, HALF),
+            shaped(F32, 2, HALF),
         ],
-        scratch_shapes=[
-            pltpu.VMEM((TOTAL, HALF), F32),
-            pltpu.VMEM((DEEP, HALF), F32),
-            pltpu.VMEM((2, N_ZL, DEEP, HALF), BF),
-            pltpu.VMEM((HALF, COLS_PAD), F32),
-        ],
-        compiler_params=pltpu.CompilerParams(vmem_limit_bytes=VMEM_LIMIT),
-        name="forward",
-    )(at, feats, g, gain, mine, other)
+        [],
+        flops,
+        at, fp_other, other, acc, g, gain,
+    )
 
 
 def backward_kernel(
     width, at_ref, a_ref, b_ref, img_ref, gain_ref, stat_ref, mine_ref, other_ref,
-    p_ref, n_ref, gp_ref, pp_ref, nat_ref,
+    sig_ref, conv_ref, n_ref, gp_ref, pp_ref, part_ref,
 ):
-    stat = jnp.sum(stat_ref[...], axis=0)
+    stat = jnp.sum(stat_ref[:, 0:2], axis=0)
     inv = lax.rsqrt(stat[0:1] / width + EPS)
     back = inv * inv * inv * stat[1:2] / width
     for c in range(2):
@@ -173,34 +214,58 @@
             p = jnp.dot(w_ref[z], gp_ref[0], preferred_element_type=F32)
             p += jnp.dot(w_ref[N_ZL + z], gp_ref[1], preferred_element_type=F32)
             pp_ref[which, z] = p
-    for c in range(2):
-        for z in range(N_ZL):
-            for x in range(N_X):
-                row = ((x * N_ZL + z) * 2 + c) * ROWS
-                nat_ref[row : row + ROWS] = pp_ref[c, z, x * ROWS_PAD : x * ROWS_PAD + ROWS]
+
+    def piece(begin, length):
+        done = 0
+        while done < length:
+            owner, skip = divmod(begin + done, ROWS)
+            n = min(ROWS - skip, length - done)
+            c, z, x = owner % 2, owner // 2 % N_ZL, owner // (2 * N_ZL)
+            row = x * ROWS_PAD + skip
+            part_ref[done : done + n] = pp_ref[c, z, row : row + n]
+            done += n
+        return part_ref[:length].astype(BF)
+
     for y in range(N_Y):
-        p_ref[y, :PAIR_SIG] = nat_ref[PAIR_SIG * y : PAIR_SIG * (y + 1)].astype(BF)
-        base = PAIR_SIG * N_Y + PAIR_CONV * y
-        p_ref[y, PAIR_SIG:] = nat_ref[base : base + PAIR_CONV].astype(BF)
+        sig_ref[y] = piece(PAIR_SIG * y, PAIR_SIG)
+        conv_ref[y] = piece(PAIR_SIG * N_Y + PAIR_CONV * y, PAIR_CONV)
 
 
 def backward(at, a, b, image, gain, stat, mine, other, width):
-    return pl.pallas_call(
+    return call(
         functools.partial(backward_kernel, width),
-        in_specs=[SMEM] + [VMEM] * 7,
-        out_specs=[VMEM] * 2,
-        out_shape=[
-            jax.ShapeDtypeStruct((N_Y, PAIR, HALF), BF),
-            jax.ShapeDtypeStruct((2, COLS_PAD, HALF), BF),
+        "backward",
+        24,
+        [
+            shaped(BF, N_Y, PAIR_SIG, HALF),
+            shaped(BF, N_Y, PAIR_CONV, HALF),
+            shaped(BF, 2, COLS_PAD, HALF),
         ],
-        scratch_shapes=[
+        [
             pltpu.VMEM((2, COLS_PAD, HALF), BF),
             pltpu.VMEM((2, N_ZL, DEEP, HALF), F32),
-            pltpu.VMEM((TOTAL, HALF), F32),
+            pltpu.VMEM((PAIR_CONV, HALF), F32),
         ],
-        compiler_params=pltpu.CompilerParams(vmem_limit_bytes=VMEM_LIMIT),
-        name="backward",
-    )(at, a, b, image, gain, stat, mine, other)
+        HALF * TOTAL * COLS * 4,
+        at, a, b, image, gain, stat, mine, other,
+    )
+
+
+def pack_kernel(at_ref, sig_ref, conv_ref, out_ref):
+    sig = sig_ref[0].astype(F32)
+    for y in range(1, N_Y):
+        sig += sig_ref[y].astype(F32)
+    pad = jnp.zeros((CONV - SIG, HALF), F32)
+    for b in range(2):
+        out_ref[at_ref[0], b] = jnp.concatenate([sig[b * SIG : (b + 1) * SIG], pad]).astype(BF)
+        out_ref[1 - at_ref[0], b] = conv_ref[b * CONV : (b + 1) * CONV]
+
+
+def pack(xh, sig, conv):
+    return call(
+        pack_kernel, "pack", 8, [shaped(BF, 2, 2, CONV, HALF)], [], 0,
+        xh.astype(jnp.int32).reshape(1), sig, conv,
+    )[0].reshape(4, CONV, HALF)
 
 
 def per_device(sig_feat, conv_feat, weight, gain, text, grad_out, tile_count, tile_block):
@@ -222,8 +287,12 @@
     def by_half(x):
         return jnp.stack([x[:, :HALF], x[:, HALF:]])
 
+    xh = lax.axis_index("xh")
+    sig = by_half(sig_feat.reshape(tokens, SIG).T)
+    conv = by_half(conv_feat.reshape(tokens, CONV).T)
+    sig = jnp.pad(sig, ((0, 0), (0, CONV - SIG), (0, 0)))
     sig, conv = exchange(
-        by_half(sig_feat.reshape(tokens, SIG).T), by_half(conv_feat.reshape(tokens, CONV).T)
+        jnp.concatenate([jnp.where(xh == 0, sig, conv), jnp.where(xh == 0, conv, sig)])
     )
     feats = gather_y(
         jnp.concatenate([sig.reshape(PAIR_SIG, HALF), conv.reshape(PAIR_CONV, HALF)])
@@ -246,40 +315,43 @@
     grad_slots = lax.dot_general(
         grad_out.T, chooser, (((1,), (1,)), ((), ())), preferred_element_type=F32
     ).astype(BF)
-    grad_got = shift(half_of(grad_slots, 1 - zh), "zh", 1)
-    g = ordered(zh, half_of(grad_slots, zh)[None], grad_got[None], 0)
+    fp_mine, fp_other = arrange(at, feats)
+    mine, fp_mine, fp_other, grad_keep, grad_give = lax.optimization_barrier(
+        (mine, fp_mine, fp_other, half_of(grad_slots, zh), half_of(grad_slots, 1 - zh))
+    )
+    other = shift(mine, "core", 1)
+    grad_got = shift(grad_give, "zh", 1)
+    g = ordered(zh, grad_keep[None], grad_got[None], 0)
     g = jnp.pad(g, ((0, 0), (0, COLS_PAD - COLS), (0, 0)))
-
-    mine, feats, g = lax.optimization_barrier((mine, feats, g))
-    other = shift(mine, "core", 1)
     spare = mine[::N_ZL, ROWS : ROWS + 3].astype(F32)
     gain_pair = (spare[:, 0] + spare[:, 1] + spare[:, 2])[:, :, None]
 
-    image, a, b, stat = forward(at, feats, g, gain_pair, mine, other)
+    image, a, b, stat = forward(at, fp_mine, fp_other, mine, other, g, gain_pair)
+    text_f = text.T.astype(F32)
+    text_square = jnp.sum(text_f * text_f, axis=0).reshape(2, HALF)
+    stat = jnp.concatenate([stat, text_square])
     stat = lax.all_to_all(
         jnp.broadcast_to(stat[None], (N_Y,) + stat.shape), "y", 0, 0, tiled=True
     )
-    p, n_image = backward(at, a, b, image, gain_pair, stat, mine, other, float(model_width))
-    text_f = text.T.astype(F32)
-    text_square, p = lax.optimization_barrier((jnp.sum(text_f * text_f, axis=0), p))
-    grads = lax.psum_scatter(
-        p.reshape(TOTAL, HALF), "y", scatter_dimension=0, tiled=True
-    )
+    sig_p, conv_p, n_image = backward(at, a, b, image, gain_pair, stat, mine, other, float(model_width))
+    stat, sig_p, conv_p = lax.optimization_barrier((stat, sig_p, conv_p))
+    text_square = jnp.sum(stat[:, 2:], axis=0).reshape(tokens)
+    conv_p = lax.psum_scatter(
+        conv_p.reshape(N_Y * PAIR_CONV, HALF), "y", scatter_dimension=0, tiled=True
+    )
+    sig_p = lax.all_to_all(sig_p, "y", 0, 0, tiled=True)
 
     n_image = n_image[:, :COLS]
     n_keep = lax.dynamic_index_in_dim(n_image, zh, 0, keepdims=False)
     n_got = shift(lax.dynamic_index_in_dim(n_image, 1 - zh, 0, keepdims=False), "zh", 1)
     n_slots = ordered(zh, n_keep, n_got, 1)
     n_placed = jnp.dot(n_slots, chooser, preferred_element_type=F32).astype(BF)
-    text_square = lax.psum(text_square, "y")
     text_square = text_square + shift(text_square, "zh", 1)
     inv_text = lax.rsqrt(text_square / model_width + EPS)
     n_text = (text_f * inv_text[None, :] * gain[:, None]).astype(BF)
     normed = jnp.where(is_image[None, :], n_placed, n_text).T
 
-    sig_g, conv_g = exchange(
-        grads[:PAIR_SIG].reshape(2, SIG, HALF), grads[PAIR_SIG:].reshape(2, CONV, HALF)
-    )
+    sig_g, conv_g = exchange(pack(xh, sig_p, conv_p))
 
     def tokens_first(x, width):
         return jnp.concatenate([x[0], x[1]], axis=1).T.reshape(slots, tile_tokens, width)

time: 225 us -> 211 us (0.938)
  starting transfers between devices: 78.3 us -> 66.8 us
  waiting for transfers between devices: 58.3 us -> 69.2 us
  local copies, waits for them, and re-layouts: 19 us -> 8.64 us
  other arithmetic: 5.59 us -> 2.89 us
    psum x1 -> x0, blocking collectives: 14.8 us -> none  [per_device(): text_square = lax.psum(text_square, 'y')]
    all_to_all x0 -> x1, blocking collectives: none -> 14.3 us  [per_device(): lax.all_to_all(jnp.broadcast_to(stat[None], (N_Y,) + stat.shape), 'y', 0,...]
    unnamed x28 -> x19, local copies, waits for them, and re-layouts: 11.8 us -> 3.23 us
    all_to_all x3, starting transfers between devices: 28.8 us -> 22.7 us  [the longest x2 19.2 us: exchange(): lax.all_to_all(blocks, ('xh', 'zh'), split_axis=0, concat_axis=0, tiled=T...]
    ppermute x12, starting transfers between devices: 49.4 us -> 44 us  [shift(): return lax.ppermute(x, axis, [(i, (i + by) % n) for i in range(n)])]
    ppermute x12, waiting for transfers between devices: 20 us -> 25.4 us  [shift(): return lax.ppermute(x, axis, [(i, (i + by) % n) for i in range(n)])]
    all_to_all x3, waiting for transfers between devices: 21.7 us -> 26.8 us  [the longest x2 18.9 us: exchange(): lax.all_to_all(blocks, ('xh', 'zh'), split_axis=0, concat_axis=0, tiled=T...]
    reduce_scatter x1, waiting for transfers between devices: 14.5 us -> 16.9 us  [per_device(): lax.psum_scatter(conv_p.reshape(N_Y * PAIR_CONV, HALF), 'y', scatter_dime...]
  transfers between devices with their start and end apart: 17 -> 17, of which waited for: 11 -> 10; matrix products, arithmetic and copies ran while one was open for 5% -> 3% of each run, Pallas kernels for 0% -> 2%
where the time goes in v3:
time: 211 us; the launch traced here: 210 us
  waiting for transfers between devices  69.2 us (33%)
  starting transfers between devices  66.8 us (32%)
  blocking collectives  30.5 us (14%)
  between operations  15.4 us (7%)
  Pallas kernels  14.8 us (7%)
  local copies, waits for them, and re-layouts  8.64 us (4%)
  other arithmetic  2.89 us (1%)
    ppermute x12, starting transfers between devices, shift(): return lax.ppermute(x, axis, [(i, (i + by) % n) for i in range(n)])  44 us
    ppermute x12, waiting for transfers between devices, shift(): return lax.ppermute(x, axis, [(i, (i + by) % n) for i in range(n)])  25.4 us
    all_to_all x2, starting transfers between devices, exchange(): lax.all_to_all(blocks, ('xh', 'zh'), split_axis=0, concat_axis=0, tiled=T...  19.2 us
    all_to_all x2, waiting for transfers between devices, exchange(): lax.all_to_all(blocks, ('xh', 'zh'), split_axis=0, concat_axis=0, tiled=T...  18.9 us
    reduce_scatter x1, waiting for transfers between devices, per_device(): lax.psum_scatter(conv_p.reshape(N_Y * PAIR_CONV, HALF), 'y', scatter_dime...  16.9 us
    all_gather x1, blocking collectives, per_device(): w_x = lax.all_gather(w_own, ('xh', 'xl'), axis=0)  16.2 us
    pallas_call x5, Pallas kernels, call(): pl.pallas_call(kernel, in_specs=[SMEM] + [VMEM] * (len(args) - 1), out_sp...  14.8 us
    all_to_all x1, blocking collectives, per_device(): lax.all_to_all(jnp.broadcast_to(stat[None], (N_Y,) + stat.shape), 'y', 0,...  14.3 us
  transfers between devices with their start and end apart: 17, of which 10 were waited for; matrix products, arithmetic and copies ran while one was open for 3% of the time, Pallas kernels for 2%

profile of v3, /device:TPU:6, one launch (start us, length us, event | category | flops | bytes accessed | tf_op | source)
XLA Modules:
  0.0 210.2 jit_solution(13604696150578137771)
XLA Ops:
  7.2 0.8 subtract_convert_fusion
  8.0 1.0 concatenate.24
  9.0 16.2 %all-gather = bf16[544,512]{1,0:T(8,128)(2,1)} all-gather(bf16[136,512]{1,0:T(8,128)(2,1)S(1)} %pad.12), channel_id=2, replica_groups=mesh['xh'=2,'xl'=2,'zl'=4,'core'=2,'y'=8,'zh'=2] {'xh','xl'}, dimensions={0}, use_global_device_ids=true | all-gather | bytes 696320 | tf_op jit(solution)/shard_map/all_gather | solution.py:283
  25.3 1.0 copy.28
  26.3 0.1 copy.29
  26.5 0.8 pad_maximum_fusion
  27.3 11.3 %all-to-all-start = ((bf16[4,192,256]{2,1,0:T(8,128)(2,1)}), bf16[4,192,256]{2,1,0:T(8,128)(2,1)S(1)}, u32[]{:S(2)}, u32[]{:S(2)}) async-start(bf16[4,192,256]{2,1,0:T(8,128)(2,1)} %pad_maximum_fusion), calls=%async_computation | async-start | bytes 786432 | tf_op jit(solution)/shard_map/all_to_all | solution.py:72
  39.5 8.9 %all-to-all-done = bf16[4,192,256]{2,1,0:T(8,128)(2,1)S(1)} async-done(((bf16[4,192,256]{2,1,0:T(8,128)(2,1)}), bf16[4,192,256]{2,1,0:T(8,128)(2,1)S(1)}, u32[]{:S(2)}, u32[]{:S(2)}) %all-to-all-start) | async-done | bytes 393248 | tf_op jit(solution)/shard_map/all_to_all | solution.py:72
  48.5 3.5 %collective-permute-start = (bf16[528,256]{1,0:T(8,128)(2,1)S(1)}, bf16[528,256]{1,0:T(8,128)(2,1)S(1)}, u32[]{:S(2)}, u32[]{:S(2)}) collective-permute-start(bf16[528,256]{1,0:T(8,128)(2,1)S(1)} %pad_maximum_fusion.1), channel_id=1, source_target_pairs={{0,2},{2,4},{4,6},{6,8},{8,10},{10,12},{12,14},{14,0},{1,3},{3,5},... | collective-permute-start | bytes 811016 | tf_op jit(solution)/shard_map/ppermute | solution.py:38
  52.0 5.4 %collective-permute-start.1 = (bf16[528,256]{1,0:T(8,128)(2,1)S(1)}, bf16[528,256]{1,0:T(8,128)(2,1)S(1)}, u32[]{:S(2)}, u32[]{:S(2)}) collective-permute-start(bf16[528,256]{1,0:T(8,128)(2,1)S(1)} %pad_maximum_fusion.1), channel_id=1, source_target_pairs={{0,14},{2,0},{4,2},{6,4},{8,6},{10,8},{12,10},{14,12},{1,15},{3,1}... | collective-permute-start | bytes 811016 | tf_op jit(solution)/shard_map/ppermute | solution.py:38
  57.5 0.6 convolution_convert_fusion.1
  58.2 0.7 dynamic-slice_bitcast_fusion.1
  58.9 0.1 broadcast_in_dim.71
  59.1 2.9 %collective-permute-done = bf16[528,256]{1,0:T(8,128)(2,1)S(1)} collective-permute-done((bf16[528,256]{1,0:T(8,128)(2,1)S(1)}, bf16[528,256]{1,0:T(8,128)(2,1)S(1)}, u32[]{:S(2)}, u32[]{:S(2)}) %collective-permute-start) | collective-permute-done | bytes 270368 | tf_op jit(solution)/shard_map/ppermute | solution.py:38
  62.0 1.9 collective-permute-start.2
  64.0 5.4 %collective-permute-start.3 = (bf16[528,256]{1,0:T(8,128)(2,1)S(1)}, bf16[528,256]{1,0:T(8,128)(2,1)S(1)}, u32[]{:S(2)}, u32[]{:S(2)}) collective-permute-start(bf16[528,256]{1,0:T(8,128)(2,1)S(1)} %collective-permute-done.1), channel_id=1, source_target_pairs={{0,14},{2,0},{4,2},{6,4},{8,6},{10,8},{12,10},{14,12},{1,15},{3,1}... | collective-permute-start | bytes 811016 | tf_op jit(solution)/shard_map/ppermute | solution.py:38
  69.5 5.0 %collective-permute-done.2 = bf16[528,256]{1,0:T(8,128)(2,1)S(1)} collective-permute-done((bf16[528,256]{1,0:T(8,128)(2,1)S(1)}, bf16[528,256]{1,0:T(8,128)(2,1)S(1)}, u32[]{:S(2)}, u32[]{:S(2)}) %collective-permute-start.2) | collective-permute-done | bytes 270368 | tf_op jit(solution)/shard_map/ppermute | solution.py:38
  74.4 1.9 collective-permute-start.4
  76.4 5.2 %collective-permute-start.5 = (bf16[528,256]{1,0:T(8,128)(2,1)S(1)}, bf16[528,256]{1,0:T(8,128)(2,1)S(1)}, u32[]{:S(2)}, u32[]{:S(2)}) collective-permute-start(bf16[528,256]{1,0:T(8,128)(2,1)S(1)} %collective-permute-done.3), channel_id=1, source_target_pairs={{0,14},{2,0},{4,2},{6,4},{8,6},{10,8},{12,10},{14,12},{1,15},{3,1}... | collective-permute-start | bytes 811016 | tf_op jit(solution)/shard_map/ppermute | solution.py:38
  81.7 3.1 %collective-permute-done.4 = bf16[528,256]{1,0:T(8,128)(2,1)S(1)} collective-permute-done((bf16[528,256]{1,0:T(8,128)(2,1)S(1)}, bf16[528,256]{1,0:T(8,128)(2,1)S(1)}, u32[]{:S(2)}, u32[]{:S(2)}) %collective-permute-start.4) | collective-permute-done | bytes 270368 | tf_op jit(solution)/shard_map/ppermute | solution.py:38
  84.8 1.9 collective-permute-start.6
  86.7 5.1 %collective-permute-start.7 = (bf16[264,256]{1,0:T(8,128)(2,1)S(1)}, bf16[264,256]{1,0:T(8,128)(2,1)S(1)}, u32[]{:S(2)}, u32[]{:S(2)}) collective-permute-start(bf16[264,256]{1,0:T(8,128)(2,1)S(1)} %slice.111), channel_id=1, source_target_pairs={{0,14},{2,0},{4,2},{6,4},{8,6},{10,8},{12,10},{14,12},{1,15},{3,1}... | collective-permute-start | bytes 405512 | tf_op jit(solution)/shard_map/ppermute | solution.py:38
  91.9 1.0 collective-permute-done.6
  92.9 1.5 collective-permute-done.7
  94.4 0.8 arrange.1
  95.3 1.9 collective-permute-start.8
  97.2 0.1 fusion.3
  97.4 1.9 collective-permute-start.9
  99.3 0.7 slice_convert_fusion
  100.0 0.2 add.189.gain_ref
  100.2 2.3 %copy-done.1 = bf16[8,544,512]{2,1,0:T(8,128)(2,1)S(1)} copy-done((bf16[8,544,512]{2,1,0:T(8,128)(2,1)S(1)}, bf16[8,544,512]{2,1,0:T(8,128)(2,1)}, u32[]{:S(2)}) %copy-start.1) | copy-done | bytes 4456472
  102.5 1.8 first_half.1.acc_ref
  104.3 12.0 %collective-permute-done.9 = bf16[448,256]{1,0:T(8,128)(2,1)S(1)} collective-permute-done((bf16[448,256]{1,0:T(8,128)(2,1)}, bf16[448,256]{1,0:T(8,128)(2,1)S(1)}, u32[]{:S(2)}, u32[]{:S(2)}) %collective-permute-start.9) | collective-permute-done | bytes 229408 | tf_op jit(solution)/shard_map/ppermute | solution.py:38
  116.4 4.9 %second_half.1 = (bf16[2,512,256]{2,1,0:T(8,128)(2,1)S(1)}, f32[2,512,256]{2,1,0:T(8,128)S(1)}, f32[2,512,256]{2,1,0:T(8,128)S(1)}, f32[2,256]{1,0:T(2,128)S(1)}) custom-call(s32[1]{0:T(128)} %bitcast.2.at_ref, bf16[4,544,256]{2,1,0:T(8,128)(2,1)S(1)} %get-tuple-element.28.fp_ref, bf16[8,544,512]{2,1,0:T(8,128)(2,1)} %collective-permute-done.8.w_ref.other_ref, ...), custom_call_target="tpu_custom_call" | custom-call | flops 968884224 | bytes 9771012 | tf_op jit(solution)/shard_map/second_half/pallas_call | solution.py:83
  121.4 14.3 %all_to_all.20.stat_ref = f32[8,4,256]{2,1,0:T(4,128)S(1)} all-to-all(f32[8,4,256]{2,1,0:T(4,128)S(1)} %broadcast_in_dim.81), channel_id=1, replica_groups=mesh['xh'=2,'xl'=2,'zl'=4,'core'=2,'y'=8,'zh'=2] {'y'}, dimensions={0} | all-to-all | bytes 65536 | tf_op jit(solution)/shard_map/all_to_all | solution.py:333
  135.7 6.4 %backward.1 = (bf16[8,144,256]{2,1,0:T(8,128)(2,1)}, bf16[8,384,256]{2,1,0:T(8,128)(2,1)}, bf16[2,512,256]{2,1,0:T(8,128)(2,1)S(1)}) custom-call(s32[1]{0:T(128)} %bitcast.2.at_ref, f32[2,512,256]{2,1,0:T(8,128)S(1)} %get-tuple-element.33.a_ref, f32[2,512,256]{2,1,0:T(8,128)S(1)} %get-tuple-element.34.b_ref, ...), custom_call_target="tpu_custom_call" | custom-call | flops 1937768448 | bytes 14258180 | tf_op jit(solution)/shard_map/backward/pallas_call | solution.py:83
  142.1 3.5 %all-to-all-start.2 = ((bf16[8,144,256]{2,1,0:T(8,128)(2,1)}), bf16[8,144,256]{2,1,0:T(8,128)(2,1)S(1)}, u32[]{:S(2)}, u32[]{:S(2)}) async-start(bf16[8,144,256]{2,1,0:T(8,128)(2,1)} %get-tuple-element.41), calls=%async_computation.2 | async-start | bytes 1179648 | tf_op jit(solution)/shard_map/all_to_all | solution.py:342
  145.7 1.9 collective-permute-start.11
  147.7 7.8 %collective-permute-start.10 = (bf16[448,256]{1,0:T(8,128)(2,1)S(1)}, bf16[448,256]{1,0:T(8,128)(2,1)S(1)}, u32[]{:S(2)}, u32[]{:S(2)}) collective-permute-start(bf16[448,256]{1,0:T(8,128)(2,1)S(1)} %dynamic-slice_bitcast_fusion), channel_id=1, source_target_pairs={{0,1},{1,0},{2,3},{3,2},{4,5},{5,4},{6,7},{7,6},{8,9},{9,8},{10,11... | collective-permute-start | bytes 688136 | tf_op jit(solution)/shard_map/ppermute | solution.py:38
  155.8 8.0 %all-to-all-done.2.sig_ref = bf16[8,144,256]{2,1,0:T(8,128)(2,1)S(1)} async-done(((bf16[8,144,256]{2,1,0:T(8,128)(2,1)}), bf16[8,144,256]{2,1,0:T(8,128)(2,1)S(1)}, u32[]{:S(2)}, u32[]{:S(2)}) %all-to-all-start.2) | async-done | bytes 589856 | tf_op jit(solution)/shard_map/all_to_all | solution.py:342
  163.8 16.9 %reduce-scatter.2.cloned.1.call-done.conv_ref = bf16[384,256]{1,0:T(8,128)(2,1)} async-done(((bf16[3072,256]{1,0:T(8,128)(2,1)}), bf16[384,256]{1,0:T(8,128)(2,1)}) %reduce-scatter.2.cloned.1.call-update) | async-done | bytes 196624 | tf_op jit(solution)/shard_map/reduce_scatter | solution.py:339
  180.7 0.9 copy-done.2
  181.6 0.8 pack.1
  182.4 7.8 %all-to-all-start.3 = ((bf16[4,192,256]{2,1,0:T(8,128)(2,1)}), bf16[4,192,256]{2,1,0:T(8,128)(2,1)S(1)}, u32[]{:S(2)}, u32[]{:S(2)}) async-start(bf16[4,192,256]{2,1,0:T(8,128)(2,1)} %bitcast.33), calls=%async_computation.4 | async-start | bytes 786432 | tf_op jit(solution)/shard_map/all_to_all | solution.py:72
  190.3 1.3 fusion
  191.7 9.9 %all-to-all-done.3 = bf16[4,192,256]{2,1,0:T(8,128)(2,1)S(1)} async-done(((bf16[4,192,256]{2,1,0:T(8,128)(2,1)}), bf16[4,192,256]{2,1,0:T(8,128)(2,1)S(1)}, u32[]{:S(2)}, u32[]{:S(2)}) %all-to-all-start.3) | async-done | bytes 393248 | tf_op jit(solution)/shard_map/all_to_all | solution.py:72
  201.7 0.8 copy.32
  202.5 0.8 copy.33
  (75 shorter events, 1.3 us)
Async XLA Ops:
  7.2 50.3 %copy-start = (bf16[512,448]{0,1:T(8,128)(2,1)S(1)}, bf16[512,448]{0,1:T(8,128)(2,1)}, u32[]{:S(2)}) copy-start(bf16[512,448]{0,1:T(8,128)(2,1)} %param.13) | copy-start | bytes 1376260
  7.2 19.1 %copy-start.4 = (bf16[8,64,192]{2,1,0:T(8,128)(2,1)S(1)}, bf16[8,64,192]{2,1,0:T(8,128)(2,1)}, u32[]{:S(2)}) copy-start(bf16[8,64,192]{2,1,0:T(8,128)(2,1)} %param.9) | copy-start | bytes 589828
  7.2 88.1 %all-gather.3.cloned.1.call-start = ((), (), s32[]{:S(2)}) async-start(), calls=%async_computation.5 | async-start | bytes 5013504 | tf_op jit(solution)/shard_map/all_gather | solution.py:285
  25.3 14.1 %copy-start.6 = (s32[1,8]{1,0:T(1,128)S(1)}, s32[1,8]{1,0:T(1,128)}, u32[]{:S(2)}) copy-start(s32[1,8]{1,0:T(1,128)} %param.15) | copy-start | bytes 100
  27.3 21.1 %all-to-all-start = ((bf16[4,192,256]{2,1,0:T(8,128)(2,1)}), bf16[4,192,256]{2,1,0:T(8,128)(2,1)S(1)}, u32[]{:S(2)}, u32[]{:S(2)}) async-start(bf16[4,192,256]{2,1,0:T(8,128)(2,1)} %pad_maximum_fusion), calls=%async_computation | async-start | bytes 786432 | tf_op jit(solution)/shard_map/all_to_all | solution.py:72
  38.7 142.0 %reduce-scatter.2.cloned.1.call-start = ((), (), s32[]{:S(2)}) async-start(), calls=%async_computation.6 | async-start | bytes 1769472 | tf_op jit(solution)/shard_map/reduce_scatter | solution.py:339
  48.5 13.5 %collective-permute-start = (bf16[528,256]{1,0:T(8,128)(2,1)S(1)}, bf16[528,256]{1,0:T(8,128)(2,1)S(1)}, u32[]{:S(2)}, u32[]{:S(2)}) collective-permute-start(bf16[528,256]{1,0:T(8,128)(2,1)S(1)} %pad_maximum_fusion.1), channel_id=1, source_target_pairs={{0,2},{2,4},{4,6},{6,8},{8,10},{10,12},{12,14},{14,0},{1,3},{3,5},... | collective-permute-start | bytes 811016 | tf_op jit(solution)/shard_map/ppermute | solution.py:38
  52.0 11.9 %collective-permute-start.1 = (bf16[528,256]{1,0:T(8,128)(2,1)S(1)}, bf16[528,256]{1,0:T(8,128)(2,1)S(1)}, u32[]{:S(2)}, u32[]{:S(2)}) collective-permute-start(bf16[528,256]{1,0:T(8,128)(2,1)S(1)} %pad_maximum_fusion.1), channel_id=1, source_target_pairs={{0,14},{2,0},{4,2},{6,4},{8,6},{10,8},{12,10},{14,12},{1,15},{3,1}... | collective-permute-start | bytes 811016 | tf_op jit(solution)/shard_map/ppermute | solution.py:38
  62.0 12.4 %collective-permute-start.2 = (bf16[528,256]{1,0:T(8,128)(2,1)S(1)}, bf16[528,256]{1,0:T(8,128)(2,1)S(1)}, u32[]{:S(2)}, u32[]{:S(2)}) collective-permute-start(bf16[528,256]{1,0:T(8,128)(2,1)S(1)} %collective-permute-done), channel_id=1, source_target_pairs={{0,2},{2,4},{4,6},{6,8},{8,10},{10,12},{12,14},{14,0},{1,3},{3,5},... | collective-permute-start | bytes 811016 | tf_op jit(solution)/shard_map/ppermute | solution.py:38
  64.0 12.4 %collective-permute-start.3 = (bf16[528,256]{1,0:T(8,128)(2,1)S(1)}, bf16[528,256]{1,0:T(8,128)(2,1)S(1)}, u32[]{:S(2)}, u32[]{:S(2)}) collective-permute-start(bf16[528,256]{1,0:T(8,128)(2,1)S(1)} %collective-permute-done.1), channel_id=1, source_target_pairs={{0,14},{2,0},{4,2},{6,4},{8,6},{10,8},{12,10},{14,12},{1,15},{3,1}... | collective-permute-start | bytes 811016 | tf_op jit(solution)/shard_map/ppermute | solution.py:38
  74.4 10.3 %collective-permute-start.4 = (bf16[528,256]{1,0:T(8,128)(2,1)S(1)}, bf16[528,256]{1,0:T(8,128)(2,1)S(1)}, u32[]{:S(2)}, u32[]{:S(2)}) collective-permute-start(bf16[528,256]{1,0:T(8,128)(2,1)S(1)} %collective-permute-done.2), channel_id=1, source_target_pairs={{0,2},{2,4},{4,6},{6,8},{8,10},{10,12},{12,14},{14,0},{1,3},{3,5},... | collective-permute-start | bytes 811016 | tf_op jit(solution)/shard_map/ppermute | solution.py:38
  76.4 10.3 %collective-permute-start.5 = (bf16[528,256]{1,0:T(8,128)(2,1)S(1)}, bf16[528,256]{1,0:T(8,128)(2,1)S(1)}, u32[]{:S(2)}, u32[]{:S(2)}) collective-permute-start(bf16[528,256]{1,0:T(8,128)(2,1)S(1)} %collective-permute-done.3), channel_id=1, source_target_pairs={{0,14},{2,0},{4,2},{6,4},{8,6},{10,8},{12,10},{14,12},{1,15},{3,1}... | collective-permute-start | bytes 811016 | tf_op jit(solution)/shard_map/ppermute | solution.py:38
  81.7 15.5 %copy-start.3 = (bf16[512,448]{0,1:T(8,128)(2,1)S(1)}, bf16[512,448]{0,1:T(8,128)(2,1)}, u32[]{:S(2)}) copy-start(bf16[512,448]{0,1:T(8,128)(2,1)} %param.12) | copy-start | bytes 1376260
  84.8 8.1 %collective-permute-start.6 = (bf16[264,256]{1,0:T(8,128)(2,1)S(1)}, bf16[264,256]{1,0:T(8,128)(2,1)S(1)}, u32[]{:S(2)}, u32[]{:S(2)}) collective-permute-start(bf16[264,256]{1,0:T(8,128)(2,1)S(1)} %slice.110), channel_id=1, source_target_pairs={{0,2},{2,4},{4,6},{6,8},{8,10},{10,12},{12,14},{14,0},{1,3},{3,5},... | collective-permute-start | bytes 405512 | tf_op jit(solution)/shard_map/ppermute | solution.py:38
  86.7 7.7 %collective-permute-start.7 = (bf16[264,256]{1,0:T(8,128)(2,1)S(1)}, bf16[264,256]{1,0:T(8,128)(2,1)S(1)}, u32[]{:S(2)}, u32[]{:S(2)}) collective-permute-start(bf16[264,256]{1,0:T(8,128)(2,1)S(1)} %slice.111), channel_id=1, source_target_pairs={{0,14},{2,0},{4,2},{6,4},{8,6},{10,8},{12,10},{14,12},{1,15},{3,1}... | collective-permute-start | bytes 405512 | tf_op jit(solution)/shard_map/ppermute | solution.py:38
  95.3 21.1 %collective-permute-start.8 = (bf16[8,544,512]{2,1,0:T(8,128)(2,1)}, bf16[8,544,512]{2,1,0:T(8,128)(2,1)}, u32[]{:S(2)}, u32[]{:S(2)}) collective-permute-start(bf16[8,544,512]{2,1,0:T(8,128)(2,1)} %all-gather.3.cloned.1.call-done.w_ref.mine_ref), channel_id=1, source_target_pairs={{0,16},{16,0},{1,17},{17,1},{2,18},{18,2},{3,19},{19,3},{4,20},{20... | collective-permute-start | bytes 13369352 | tf_op jit(solution)/shard_map/ppermute | solution.py:38
  97.4 18.9 %collective-permute-start.9 = (bf16[448,256]{1,0:T(8,128)(2,1)}, bf16[448,256]{1,0:T(8,128)(2,1)S(1)}, u32[]{:S(2)}, u32[]{:S(2)}) collective-permute-start(bf16[448,256]{1,0:T(8,128)(2,1)} %get-tuple-element.32), channel_id=1, source_target_pairs={{0,1},{1,0},{2,3},{3,2},{4,5},{5,4},{6,7},{7,6},{8,9},{9,8},{10,11... | collective-permute-start | bytes 688136 | tf_op jit(solution)/shard_map/ppermute | solution.py:38
  100.2 2.3 %copy-start.1 = (bf16[8,544,512]{2,1,0:T(8,128)(2,1)S(1)}, bf16[8,544,512]{2,1,0:T(8,128)(2,1)}, u32[]{:S(2)}) copy-start(bf16[8,544,512]{2,1,0:T(8,128)(2,1)} %all-gather.3.cloned.1.call-done.w_ref.mine_ref) | copy-start | bytes 13369348
  116.3 19.3 %slice-start = ((s8[4456448]{0:T(1024)(128)(4,1)}), s8[4194304]{0:T(1024)(128)(4,1)S(1)}, s32[]{:S(2)}) async-start(s8[4456448]{0:T(1024)(128)(4,1)} %bitcast.74), calls=%async_computation.7 | async-start | bytes 8388608
  116.4 19.3 %slice-start.1 = ((s8[4456448]{0:T(1024)(128)(4,1)}), s8[262144]{0:T(1024)(128)(4,1)S(1)}, s32[]{:S(2)}) async-start(s8[4456448]{0:T(1024)(128)(4,1)} %bitcast.74), calls=%async_computation.8 | async-start | bytes 524288
  142.1 21.7 %all-to-all-start.2 = ((bf16[8,144,256]{2,1,0:T(8,128)(2,1)}), bf16[8,144,256]{2,1,0:T(8,128)(2,1)S(1)}, u32[]{:S(2)}, u32[]{:S(2)}) async-start(bf16[8,144,256]{2,1,0:T(8,128)(2,1)} %get-tuple-element.41), calls=%async_computation.2 | async-start | bytes 1179648 | tf_op jit(solution)/shard_map/all_to_all | solution.py:342
  145.6 44.7 %copy-start.5 = (f32[448]{0:T(512)S(1)}, f32[448]{0:T(512)}, u32[]{:S(2)}) copy-start(f32[448]{0:T(512)} %param.11) | copy-start | bytes 5380
  145.7 44.5 %collective-permute-start.11 = (f32[512]{0:T(512)S(1)}, f32[512]{0:T(512)S(1)}, u32[]{:S(2)}, u32[]{:S(2)}) collective-permute-start(f32[512]{0:T(512)S(1)} %bitcast.89), channel_id=1, source_target_pairs={{0,1},{1,0},{2,3},{3,2},{4,5},{5,4},{6,7},{7,6},{8,9},{9,8},{10,11... | collective-permute-start | bytes 6152 | tf_op jit(solution)/shard_map/ppermute | solution.py:38
  147.7 42.6 %collective-permute-start.10 = (bf16[448,256]{1,0:T(8,128)(2,1)S(1)}, bf16[448,256]{1,0:T(8,128)(2,1)S(1)}, u32[]{:S(2)}, u32[]{:S(2)}) collective-permute-start(bf16[448,256]{1,0:T(8,128)(2,1)S(1)} %dynamic-slice_bitcast_fusion), channel_id=1, source_target_pairs={{0,1},{1,0},{2,3},{3,2},{4,5},{5,4},{6,7},{7,6},{8,9},{9,8},{10,11... | collective-permute-start | bytes 688136 | tf_op jit(solution)/shard_map/ppermute | solution.py:38
  180.7 0.9 copy-start.2
  182.4 19.2 %all-to-all-start.3 = ((bf16[4,192,256]{2,1,0:T(8,128)(2,1)}), bf16[4,192,256]{2,1,0:T(8,128)(2,1)S(1)}, u32[]{:S(2)}, u32[]{:S(2)}) async-start(bf16[4,192,256]{2,1,0:T(8,128)(2,1)} %bitcast.33), calls=%async_computation.4 | async-start | bytes 786432 | tf_op jit(solution)/shard_map/all_to_all | solution.py:72
Sparse Core Ops, SparseCore 0:
  25.4 66.9 all-gather.2
  142.2 38.4 reduce-scatter.1

commit v4 on v3

--- a/solution.py
+++ b/solution.py
@@ -18,8 +18,9 @@
 SIZES = (2, 2, 4, 2, 8, 2)
 N_X, N_ZL, N_Y = 4, 4, 8
 ROWS = 132
-ROWS_PAD = 136
-DEEP = N_X * ROWS_PAD
+DEEP = 2 * ROWS
+WIDE = 896
+RIGHT = 384
 TOTAL = 4224
 COLS = 448
 COLS_PAD = 512
@@ -44,27 +45,20 @@
     return jnp.concatenate([first, second], axis=axis)
 
 
-def gather_y(block):
-    n = lax.axis_size("y")
+def put(full, part, owner):
+    return lax.dynamic_update_slice(full, part[None], (owner % N_Y, 0, 0))
+
+
+def ring_y(block):
     me = lax.axis_index("y")
-    rows = block.shape[0]
-    full = jnp.zeros((n,) + block.shape, block.dtype)
-
-    def put(full, part, owner, row=0):
-        return lax.dynamic_update_slice(full, part[None], (owner % n, row, 0))
-
-    full = put(full, block, me)
+    full = put(jnp.zeros((N_Y,) + block.shape, block.dtype), block, me)
     right = left = block
-    for step in range(1, n // 2):
+    for step in range(1, N_Y // 2):
         right = shift(right, "y", 1)
         left = shift(left, "y", -1)
-        full = put(full, right, me - step + n)
+        full = put(full, right, me - step + N_Y)
         full = put(full, left, me + step)
-    half = rows // 2
-    far = me + n // 2
-    full = put(full, shift(right[:half], "y", 1), far)
-    full = put(full, shift(left[half:], "y", -1), far, half)
-    return full
+    return full, right
 
 
 def exchange(blocks):
@@ -100,21 +94,22 @@
     return ((x * N_ZL + z) * 2 + c) * ROWS
 
 
-def arrange_kernel(at_ref, feat_ref, mine_ref, other_ref, nat_ref, part_ref):
+def arrange_kernel(at_ref, feat_ref, far_ref, mine_ref, other_ref, nat_ref, part_ref):
     for y in range(N_Y):
         nat_ref[PAIR_SIG * y : PAIR_SIG * (y + 1)] = feat_ref[y, :PAIR_SIG].astype(F32)
         base = PAIR_SIG * N_Y + PAIR_CONV * y
         nat_ref[base : base + PAIR_CONV] = feat_ref[y, PAIR_SIG:].astype(F32)
-    for x in range(N_X):
-        part_ref[x * ROWS_PAD + ROWS : (x + 1) * ROWS_PAD] = jnp.zeros(
-            (ROWS_PAD - ROWS, HALF), F32
-        )
+    far = lax.rem(at_ref[1] + N_Y // 2, N_Y)
+    row = pl.multiple_of(PAIR_SIG * far, 16)
+    nat_ref[pl.ds(row, PAIR_SIG)] = far_ref[:PAIR_SIG].astype(F32)
+    row = pl.multiple_of(PAIR_SIG * N_Y + PAIR_CONV * far, 16)
+    nat_ref[pl.ds(row, PAIR_CONV)] = far_ref[PAIR_SIG:].astype(F32)
     for c in range(2):
         for z in range(N_ZL):
             for x in range(N_X):
                 row = rows_of(x, z, c)
-                part_ref[x * ROWS_PAD : x * ROWS_PAD + ROWS] = nat_ref[row : row + ROWS]
-            part = part_ref[...].astype(BF)
+                part_ref[x * ROWS : (x + 1) * ROWS] = nat_ref[row : row + ROWS]
+            part = part_ref[...].astype(BF).reshape(2, DEEP, HALF)
 
             @pl.when(at_ref[0] == c)
             def _():
@@ -125,58 +120,66 @@
                 other_ref[z] = part
 
 
-def arrange(at, feats):
+def arrange(at, feats, far):
     return call(
         arrange_kernel,
         "arrange",
         16,
-        [shaped(BF, N_ZL, DEEP, HALF)] * 2,
-        [pltpu.VMEM((TOTAL, HALF), F32), pltpu.VMEM((DEEP, HALF), F32)],
+        [shaped(BF, N_ZL, 2, DEEP, HALF)] * 2,
+        [pltpu.VMEM((TOTAL, HALF), F32), pltpu.VMEM((2 * DEEP, HALF), F32)],
         0,
         at,
         feats,
-    )
-
-
-def products(fp_ref, w_ref, c, total):
+        far,
+    )
+
+
+def weight_kernel(at_ref, w_ref, out_ref):
+    w = w_ref[...].astype(F32)
+    left = jnp.concatenate([w[0], w[1]], axis=0)
+    right = jnp.concatenate([w[2], w[3]], axis=0)
+    out_ref[...] = jnp.concatenate([left, right], axis=1).astype(BF)
+
+
+def side_by_side(at, w):
+    return call(weight_kernel, "side_by_side", 8, [shaped(BF, DEEP, WIDE)], [], 0, at, w)[0]
+
+
+def products(fp_ref, w_ref, c):
+    left = right = None
     for z in range(N_ZL):
-        term = lax.dot_general(
-            fp_ref[z], w_ref[c * N_ZL + z], (((0,), (0,)), ((), ())), preferred_element_type=F32
-        )
-        total = term if total is None else total + term
-    return total
+        w = w_ref[c * N_ZL + z]
+        dims = (((0,), (0,)), ((), ()))
+        one = lax.dot_general(fp_ref[z, 0], w[:, :COLS_PAD], dims, preferred_element_type=F32)
+        two = lax.dot_general(fp_ref[z, 1], w[:, RIGHT:], dims, preferred_element_type=F32)
+        left = one if left is None else left + one
+        right = two if right is None else right + two
+    return left + pltpu.roll(right, COLS_PAD - (COLS - RIGHT), axis=1)
 
 
 def first_kernel(at_ref, fp_ref, w_ref, acc_ref):
     for c in range(2):
-        acc_ref[c] = products(fp_ref, w_ref, c, None)
-
-
-def second_kernel(
-    at_ref, fp_ref, w_ref, acc_ref, g_ref, gain_ref, img_ref, a_ref, b_ref, stat_ref
-):
+        acc_ref[c] = products(fp_ref, w_ref, c)
+
+
+def second_kernel(at_ref, fp_ref, w_ref, acc_ref, img_ref, slope_ref, square_ref):
+    square = jnp.zeros((1, HALF), F32)
     for c in range(2):
-        v = products(fp_ref, w_ref, c, acc_ref[c]).T
+        v = (acc_ref[c] + products(fp_ref, w_ref, c)).T
+        v = jnp.where(lax.broadcasted_iota(jnp.int32, v.shape, 0) < COLS, v, 0.0)
         v2 = v * v
         t = jnp.tanh(GELU_K * (v + GELU_C * v2 * v))
         image = (0.5 * v * (1.0 + t)).astype(BF)
-        slope = 0.5 * (1.0 + t) + 0.5 * v * (1.0 - t * t) * GELU_K * (1.0 + 3.0 * GELU_C * v2)
         img_ref[c] = image
+        slope_ref[c] = 0.5 * (1.0 + t) + 0.5 * v * (1.0 - t * t) * GELU_K * (
+            1.0 + 3.0 * GELU_C * v2
+        )
         m = image.astype(F32)
-        cot = g_ref[c].astype(F32) * gain_ref[c]
-        square = jnp.sum(m * m, axis=0, keepdims=True)
-        cross = jnp.sum(cot * m, axis=0, keepdims=True)
-        a_ref[c] = slope * cot
-        b_ref[c] = slope * m
-        if c == 0:
-            stat_ref[0:1] = square
-            stat_ref[1:2] = cross
-        else:
-            stat_ref[0:1] += square
-            stat_ref[1:2] += cross
-
-
-def forward(at, fp_mine, fp_other, mine, other, g, gain):
+        square += jnp.sum(m * m, axis=0, keepdims=True)
+    square_ref[...] = square
+
+
+def forward(at, fp_mine, fp_other, mine, other):
     flops = HALF * TOTAL * COLS * 2
     acc = call(
         first_kernel, "first_half", 14, [shaped(F32, 2, HALF, COLS_PAD)], [], flops,
@@ -189,31 +192,76 @@
         [
             shaped(BF, 2, COLS_PAD, HALF),
             shaped(F32, 2, COLS_PAD, HALF),
-            shaped(F32, 2, COLS_PAD, HALF),
-            shaped(F32, 2, HALF),
+            shaped(F32, 1, HALF),
         ],
         [],
         flops,
-        at, fp_other, other, acc, g, gain,
+        at, fp_other, other, acc,
+    )
+
+
+def sums_kernel(
+    at_ref, img_ref, keep_ref, got_ref, gain_ref, square_ref, text_ref,
+    stat_ref, cot_ref, gains_ref,
+):
+    zh = at_ref[0]
+    terms = got_ref[COLS : COLS + 16].astype(F32)
+    row = terms[0:2] + terms[2:4] + terms[4:6]
+    other = jnp.concatenate(
+        [jnp.broadcast_to(row[i : i + 1], (8, HALF)).T[:, :1] for i in range(2)]
+    )
+    gains_ref[zh] = gain_ref[...]
+    gains_ref[1 - zh] = other
+    rest = jnp.zeros((COLS_PAD - COLS, HALF), F32)
+    cot_ref[zh, :COLS] = keep_ref[...].astype(F32) * gain_ref[:COLS]
+    cot_ref[zh, COLS:] = rest
+    cot_ref[1 - zh, :COLS] = got_ref[:COLS].astype(F32) * other[:COLS]
+    cot_ref[1 - zh, COLS:] = rest
+    cross = jnp.zeros((1, HALF), F32)
+    for c in range(2):
+        cross += jnp.sum(cot_ref[c] * img_ref[c].astype(F32), axis=0, keepdims=True)
+    for y in range(N_Y):
+        stat_ref[y, 0:1] = square_ref[...]
+        stat_ref[y, 1:2] = cross
+        stat_ref[y, 2:4] = text_ref[...]
+
+
+def sums(zh, image, keep, got, gain, square, text):
+    return call(
+        sums_kernel,
+        "sums",
+        14,
+        [
+            shaped(F32, N_Y, 4, HALF),
+            shaped(F32, 2, COLS_PAD, HALF),
+            shaped(F32, 2, COLS_PAD, 1),
+        ],
+        [],
+        0,
+        zh, image, keep, got, gain, square, text,
     )
 
 
 def backward_kernel(
-    width, at_ref, a_ref, b_ref, img_ref, gain_ref, stat_ref, mine_ref, other_ref,
+    width, at_ref, slope_ref, img_ref, cot_ref, gain_ref, stat_ref, mine_ref, other_ref,
     sig_ref, conv_ref, n_ref, gp_ref, pp_ref, part_ref,
 ):
     stat = jnp.sum(stat_ref[:, 0:2], axis=0)
     inv = lax.rsqrt(stat[0:1] / width + EPS)
     back = inv * inv * inv * stat[1:2] / width
     for c in range(2):
-        gp_ref[c] = (inv * a_ref[c] - back * b_ref[c]).astype(BF)
-        n_ref[c] = (img_ref[c].astype(F32) * inv * gain_ref[c]).astype(BF)
+        m = img_ref[c].astype(F32)
+        gp = (slope_ref[c] * (inv * cot_ref[c] - back * m)).astype(BF)
+        gp_ref[c, 0] = gp
+        gp_ref[c, 1] = jnp.concatenate([jnp.zeros((COLS - RIGHT, HALF), BF), gp[:COLS]])
+        n_ref[c] = (m * inv * gain_ref[c]).astype(BF)
     core = at_ref[0]
     for w_ref, which in ((mine_ref, core), (other_ref, 1 - core)):
         for z in range(N_ZL):
-            p = jnp.dot(w_ref[z], gp_ref[0], preferred_element_type=F32)
-            p += jnp.dot(w_ref[N_ZL + z], gp_ref[1], preferred_element_type=F32)
-            pp_ref[which, z] = p
+            for h, cols in ((0, slice(0, COLS_PAD)), (1, slice(RIGHT, WIDE))):
+                p = jnp.dot(w_ref[z, :, cols], gp_ref[0, h], preferred_element_type=F32)
+                p += jnp.dot(w_ref[N_ZL + z, :, cols], gp_ref[1, h], preferred_element_type=F32)
+                pp_ref[which, z, h] = p
 
     def piece(begin, length):
         done = 0
@@ -221,8 +269,8 @@
             owner, skip = divmod(begin + done, ROWS)
             n = min(ROWS - skip, length - done)
             c, z, x = owner % 2, owner // 2 % N_ZL, owner // (2 * N_ZL)
-            row = x * ROWS_PAD + skip
-            part_ref[done : done + n] = pp_ref[c, z, row : row + n]
+            row = x % 2 * ROWS + skip
+            part_ref[done : done + n] = pp_ref[c, z, x // 2, row : row + n]
             done += n
         return part_ref[:length].astype(BF)
 
@@ -231,7 +279,7 @@
         conv_ref[y] = piece(PAIR_SIG * N_Y + PAIR_CONV * y, PAIR_CONV)
 
 
-def backward(at, a, b, image, gain, stat, mine, other, width):
+def backward(at, slope, image, cot, gain, stat, mine, other, width):
     return call(
         functools.partial(backward_kernel, width),
         "backward",
@@ -242,12 +290,12 @@
             shaped(BF, 2, COLS_PAD, HALF),
         ],
         [
-            pltpu.VMEM((2, COLS_PAD, HALF), BF),
-            pltpu.VMEM((2, N_ZL, DEEP, HALF), F32),
+            pltpu.VMEM((2, 2, COLS_PAD, HALF), BF),
+            pltpu.VMEM((2, N_ZL, 2, DEEP, HALF), F32),
             pltpu.VMEM((PAIR_CONV, HALF), F32),
         ],
         HALF * TOTAL * COLS * 4,
-        at, a, b, image, gain, stat, mine, other,
+        at, slope, image, cot, gain, stat, mine, other,
     )
 
 
@@ -273,16 +321,11 @@
     slots, tile_tokens = sig_feat.shape[:2]
     tokens = slots * tile_tokens
     model_width = COLS * N_Y * 2
-    at = lax.axis_index("core").astype(jnp.int32).reshape(1)
-
-    g0 = gain.astype(BF)
-    g1 = (gain - g0.astype(F32)).astype(BF)
-    g2 = (gain - g0.astype(F32) - g1.astype(F32)).astype(BF)
-    spare = jnp.stack([g0, g1, g2, jnp.zeros_like(g0)])
-    w_own = jnp.pad(jnp.concatenate([weight, spare]), ((0, 0), (0, COLS_PAD - COLS)))
-    w_x = lax.all_gather(w_own, ("xh", "xl"), axis=0)
+    at = jnp.stack([lax.axis_index("core"), lax.axis_index("y")]).astype(jnp.int32)
+
+    w_x = lax.all_gather(weight, ("xh", "xl"), axis=0)
     w_x, sig_feat, conv_feat = lax.optimization_barrier((w_x, sig_feat, conv_feat))
-    mine = lax.all_gather(w_x.reshape(DEEP, COLS_PAD), ("zh", "zl"), axis=0)
+    mine = lax.all_gather(side_by_side(at, w_x), ("zh", "zl"), axis=0)
 
     def by_half(x):
         return jnp.stack([x[:, :HALF], x[:, HALF:]])
@@ -294,7 +337,7 @@
     sig, conv = exchange(
         jnp.concatenate([jnp.where(xh == 0, sig, conv), jnp.where(xh == 0, conv, sig)])
     )
-    feats = gather_y(
+    feats, right = ring_y(
         jnp.concatenate([sig.reshape(PAIR_SIG, HALF), conv.reshape(PAIR_CONV, HALF)])
     )
 
@@ -315,25 +358,32 @@
     grad_slots = lax.dot_general(
         grad_out.T, chooser, (((1,), (1,)), ((), ())), preferred_element_type=F32
     ).astype(BF)
-    fp_mine, fp_other = arrange(at, feats)
-    mine, fp_mine, fp_other, grad_keep, grad_give = lax.optimization_barrier(
-        (mine, fp_mine, fp_other, half_of(grad_slots, zh), half_of(grad_slots, 1 - zh))
+    g0 = gain.astype(BF)
+    g1 = (gain - g0.astype(F32)).astype(BF)
+    g2 = (gain - g0.astype(F32) - g1.astype(F32)).astype(BF)
+    terms = jnp.pad(jnp.stack([g0, g1, g2]), ((0, 0), (0, COLS_PAD - COLS))).reshape(6, HALF)
+    give = jnp.concatenate([half_of(grad_slots, 1 - zh), jnp.pad(terms, ((0, 10), (0, 0)))])
+    keep = half_of(grad_slots, zh)
+
+    mine, feats, right, give, keep = lax.optimization_barrier(
+        (mine, feats, right, give, keep)
     )
     other = shift(mine, "core", 1)
-    grad_got = shift(grad_give, "zh", 1)
-    g = ordered(zh, grad_keep[None], grad_got[None], 0)
-    g = jnp.pad(g, ((0, 0), (0, COLS_PAD - COLS), (0, 0)))
-    spare = mine[::N_ZL, ROWS : ROWS + 3].astype(F32)
-    gain_pair = (spare[:, 0] + spare[:, 1] + spare[:, 2])[:, :, None]
-
-    image, a, b, stat = forward(at, fp_mine, fp_other, mine, other, g, gain_pair)
+    fp_mine, fp_other = arrange(at, feats, shift(right, "y", 1))
+    got = shift(give, "zh", 1)
+
+    image, slope, square = forward(at, fp_mine, fp_other, mine, other)
+    image, slope, square, got = lax.optimization_barrier((image, slope, square, got))
     text_f = text.T.astype(F32)
     text_square = jnp.sum(text_f * text_f, axis=0).reshape(2, HALF)
-    stat = jnp.concatenate([stat, text_square])
-    stat = lax.all_to_all(
-        jnp.broadcast_to(stat[None], (N_Y,) + stat.shape), "y", 0, 0, tiled=True
-    )
-    sig_p, conv_p, n_image = backward(at, a, b, image, gain_pair, stat, mine, other, float(model_width))
+    gain_own = jnp.pad(gain, (0, COLS_PAD - COLS))[:, None]
+    stat, cot, gain_pair = sums(
+        zh.astype(jnp.int32).reshape(1), image, keep, got, gain_own, square, text_square
+    )
+    stat = lax.all_to_all(stat, "y", 0, 0, tiled=True)
+    sig_p, conv_p, n_image = backward(
+        at, slope, image, cot, gain_pair, stat, mine, other, float(model_width)
+    )
     stat, sig_p, conv_p = lax.optimization_barrier((stat, sig_p, conv_p))
     text_square = jnp.sum(stat[:, 2:], axis=0).reshape(tokens)
     conv_p = lax.psum_scatter(

time: 211 us -> 205 us (0.972)
  waiting for transfers between devices: 69.2 us -> 63.3 us
  Pallas kernels: 14.8 us -> 19.5 us
  starting transfers between devices: 66.8 us -> 62.7 us
    ppermute x12 -> x11, waiting for transfers between devices: 25.4 us -> 12.4 us  [shift(): return lax.ppermute(x, axis, [(i, (i + by) % n) for i in range(n)])]
    all_gather x1, waiting for transfers between devices: 0.02 us -> 4.9 us  [per_device(): mine = lax.all_gather(side_by_side(at, w_x), ('zh', 'zl'), axis=0)]
    pallas_call x5 -> x7, Pallas kernels: 14.8 us -> 19.5 us  [call(): pl.pallas_call(kernel, in_specs=[SMEM] + [VMEM] * (len(args) - 1), out_sp...]
    ppermute x12 -> x11, starting transfers between devices: 44 us -> 40 us  [shift(): return lax.ppermute(x, axis, [(i, (i + by) % n) for i in range(n)])]
    all_to_all x1, waiting for transfers between devices: 7.97 us -> 11.5 us  [per_device(): sig_p = lax.all_to_all(sig_p, 'y', 0, 0, tiled=True)]
  transfers between devices with their start and end apart: 17 -> 16, of which waited for: 10 -> 12; matrix products, arithmetic and copies ran while one was open for 3% -> 4% of each run, Pallas kernels for 2% -> 5%
where the time goes in v4:
time: 205 us
  waiting for transfers between devices  63.3 us (31%)
  starting transfers between devices  62.7 us (31%)
  blocking collectives  30.3 us (15%)
  Pallas kernels  19.5 us (10%)
  between operations  15.3 us (7%)
  local copies, waits for them, and re-layouts  7.71 us (4%)
  other arithmetic  3.81 us (2%)
    ppermute x11, starting transfers between devices, shift(): return lax.ppermute(x, axis, [(i, (i + by) % n) for i in range(n)])  40 us
    pallas_call x7, Pallas kernels, call(): pl.pallas_call(kernel, in_specs=[SMEM] + [VMEM] * (len(args) - 1), out_sp...  19.5 us
    all_to_all x2, starting transfers between devices, exchange(): lax.all_to_all(blocks, ('xh', 'zh'), split_axis=0, concat_axis=0, tiled=T...  19.1 us
    all_to_all x2, waiting for transfers between devices, exchange(): lax.all_to_all(blocks, ('xh', 'zh'), split_axis=0, concat_axis=0, tiled=T...  17.7 us
    reduce_scatter x1, waiting for transfers between devices, per_device(): lax.psum_scatter(conv_p.reshape(N_Y * PAIR_CONV, HALF), 'y', scatter_dime...  16.8 us
    all_gather x1, blocking collectives, per_device(): w_x = lax.all_gather(weight, ('xh', 'xl'), axis=0)  15.9 us
    all_to_all x1, blocking collectives, per_device(): stat = lax.all_to_all(stat, 'y', 0, 0, tiled=True)  14.4 us
    ppermute x11, waiting for transfers between devices, shift(): return lax.ppermute(x, axis, [(i, (i + by) % n) for i in range(n)])  12.4 us
  transfers between devices with their start and end apart: 16, of which 12 were waited for; matrix products, arithmetic and copies ran while one was open for 4% of the time, Pallas kernels for 5%

profile of v4, /device:TPU:6, one launch (start us, length us, event | category | flops | bytes accessed | tf_op | source)
XLA Modules:
  0.0 204.5 jit_solution(12070032233050210825)
XLA Ops:
  7.3 15.9 %all-gather.2.w_ref = bf16[4,132,448]{2,1,0:T(8,128)(2,1)S(1)} all-gather(bf16[1,132,448]{2,1,0:T(8,128)(2,1)} %bitcast.82), channel_id=2, replica_groups=mesh['xh'=2,'xl'=2,'zl'=4,'core'=2,'y'=8,'zh'=2] {'xh','xl'}, dimensions={0}, use_global_device_ids=true | all-gather | bytes 591360 | tf_op jit(solution)/shard_map/all_gather | solution.py:326
  23.2 1.5 side_by_side.1
  25.1 0.8 pad_maximum_fusion
  25.9 11.2 %all-to-all-start = ((bf16[4,192,256]{2,1,0:T(8,128)(2,1)}), bf16[4,192,256]{2,1,0:T(8,128)(2,1)S(1)}, u32[]{:S(2)}, u32[]{:S(2)}) async-start(bf16[4,192,256]{2,1,0:T(8,128)(2,1)} %pad_maximum_fusion), calls=%async_computation | async-start | bytes 786432 | tf_op jit(solution)/shard_map/all_to_all | solution.py:66
  38.0 0.6 convolution_convert_fusion.1
  38.7 7.9 %all-to-all-done = bf16[4,192,256]{2,1,0:T(8,128)(2,1)S(1)} async-done(((bf16[4,192,256]{2,1,0:T(8,128)(2,1)}), bf16[4,192,256]{2,1,0:T(8,128)(2,1)S(1)}, u32[]{:S(2)}, u32[]{:S(2)}) %all-to-all-start) | async-done | bytes 393248 | tf_op jit(solution)/shard_map/all_to_all | solution.py:66
  46.6 0.7 pad_maximum_fusion.1
  47.3 3.5 %collective-permute-start = (bf16[528,256]{1,0:T(8,128)(2,1)}, bf16[528,256]{1,0:T(8,128)(2,1)}, u32[]{:S(2)}, u32[]{:S(2)}) collective-permute-start(bf16[528,256]{1,0:T(8,128)(2,1)} %pad_maximum_fusion.1), channel_id=1, source_target_pairs={{0,2},{2,4},{4,6},{6,8},{8,10},{10,12},{12,14},{14,0},{1,3},{3,5},... | collective-permute-start | bytes 811016 | tf_op jit(solution)/shard_map/ppermute | solution.py:39
  50.8 3.8 %collective-permute-start.1 = (bf16[528,256]{1,0:T(8,128)(2,1)}, bf16[528,256]{1,0:T(8,128)(2,1)}, u32[]{:S(2)}, u32[]{:S(2)}) collective-permute-start(bf16[528,256]{1,0:T(8,128)(2,1)} %pad_maximum_fusion.1), channel_id=1, source_target_pairs={{0,14},{2,0},{4,2},{6,4},{8,6},{10,8},{12,10},{14,12},{1,15},{3,1}... | collective-permute-start | bytes 811016 | tf_op jit(solution)/shard_map/ppermute | solution.py:39
  54.8 0.7 fusion.18
  55.7 1.8 collective-permute-done
  57.4 2.8 %collective-permute-start.2 = (bf16[528,256]{1,0:T(8,128)(2,1)}, bf16[528,256]{1,0:T(8,128)(2,1)S(1)}, u32[]{:S(2)}, u32[]{:S(2)}) collective-permute-start(bf16[528,256]{1,0:T(8,128)(2,1)} %collective-permute-done), channel_id=1, source_target_pairs={{0,2},{2,4},{4,6},{6,8},{8,10},{10,12},{12,14},{14,0},{1,3},{3,5},... | collective-permute-start | bytes 811016 | tf_op jit(solution)/shard_map/ppermute | solution.py:39
  60.2 0.3 collective-permute-done.1
  60.5 4.0 %collective-permute-start.3 = (bf16[528,256]{1,0:T(8,128)(2,1)}, bf16[528,256]{1,0:T(8,128)(2,1)S(1)}, u32[]{:S(2)}, u32[]{:S(2)}) collective-permute-start(bf16[528,256]{1,0:T(8,128)(2,1)} %collective-permute-done.1), channel_id=1, source_target_pairs={{0,14},{2,0},{4,2},{6,4},{8,6},{10,8},{12,10},{14,12},{1,15},{3,1}... | collective-permute-start | bytes 811016 | tf_op jit(solution)/shard_map/ppermute | solution.py:39
  64.5 1.0 bitcast_dynamic-update-slice_fusion.5
  65.5 1.0 bitcast_dynamic-update-slice_fusion.4
  66.5 1.6 collective-permute-done.2
  68.1 2.6 %collective-permute-start.4 = (bf16[528,256]{1,0:T(8,128)(2,1)S(1)}, bf16[528,256]{1,0:T(8,128)(2,1)S(1)}, u32[]{:S(2)}, u32[]{:S(2)}) collective-permute-start(bf16[528,256]{1,0:T(8,128)(2,1)S(1)} %collective-permute-done.2), channel_id=1, source_target_pairs={{0,2},{2,4},{4,6},{6,8},{8,10},{10,12},{12,14},{14,0},{1,3},{3,5},... | collective-permute-start | bytes 811016 | tf_op jit(solution)/shard_map/ppermute | solution.py:39
  70.8 0.3 collective-permute-done.3
  71.1 4.6 %collective-permute-start.5 = (bf16[528,256]{1,0:T(8,128)(2,1)S(1)}, bf16[528,256]{1,0:T(8,128)(2,1)S(1)}, u32[]{:S(2)}, u32[]{:S(2)}) collective-permute-start(bf16[528,256]{1,0:T(8,128)(2,1)S(1)} %collective-permute-done.3), channel_id=1, source_target_pairs={{0,14},{2,0},{4,2},{6,4},{8,6},{10,8},{12,10},{14,12},{1,15},{3,1}... | collective-permute-start | bytes 811016 | tf_op jit(solution)/shard_map/ppermute | solution.py:39
  75.7 2.2 %collective-permute-done.4 = bf16[528,256]{1,0:T(8,128)(2,1)S(1)} collective-permute-done((bf16[528,256]{1,0:T(8,128)(2,1)S(1)}, bf16[528,256]{1,0:T(8,128)(2,1)S(1)}, u32[]{:S(2)}, u32[]{:S(2)}) %collective-permute-start.4) | collective-permute-done | bytes 270368 | tf_op jit(solution)/shard_map/ppermute | solution.py:39
  78.0 1.6 collective-permute-done.5
  79.6 4.9 %all-gather.5.cloned.1.call-done = bf16[2112,896]{1,0:T(8,128)(2,1)} async-done(((bf16[264,896]{1,0:T(8,128)(2,1)}), bf16[2112,896]{1,0:T(8,128)(2,1)}) %all-gather.5.cloned.1.call-update) | async-done | bytes 3784720 | tf_op jit(solution)/shard_map/all_gather | solution.py:328
  84.5 2.0 collective-permute-start.7
  86.5 3.5 %collective-permute-start.6 = (bf16[528,256]{1,0:T(8,128)(2,1)}, bf16[528,256]{1,0:T(8,128)(2,1)S(1)}, u32[]{:S(2)}, u32[]{:S(2)}) collective-permute-start(bf16[528,256]{1,0:T(8,128)(2,1)} %copy-done.5), channel_id=1, source_target_pairs={{0,2},{2,4},{4,6},{6,8},{8,10},{10,12},{12,14},{14,0},{1,3},{3,5},... | collective-permute-start | bytes 811016 | tf_op jit(solution)/shard_map/ppermute | solution.py:39
  90.0 3.4 %collective-permute-start.8 = (bf16[464,256]{1,0:T(8,128)(2,1)}, bf16[464,256]{1,0:T(8,128)(2,1)}, u32[]{:S(2)}, u32[]{:S(2)}) collective-permute-start(bf16[464,256]{1,0:T(8,128)(2,1)} %fusion.18), channel_id=1, source_target_pairs={{0,1},{1,0},{2,3},{3,2},{4,5},{5,4},{6,7},{7,6},{8,9},{9,8},{10,11... | collective-permute-start | bytes 712712 | tf_op jit(solution)/shard_map/ppermute | solution.py:39
  93.3 1.2 fusion.1
  94.5 0.1 copy.27.gain_ref
  94.7 4.5 %collective-permute-done.6.far_ref = bf16[528,256]{1,0:T(8,128)(2,1)S(1)} collective-permute-done((bf16[528,256]{1,0:T(8,128)(2,1)}, bf16[528,256]{1,0:T(8,128)(2,1)S(1)}, u32[]{:S(2)}, u32[]{:S(2)}) %collective-permute-start.6) | collective-permute-done | bytes 270368 | tf_op jit(solution)/shard_map/ppermute | solution.py:39
  99.2 1.3 arrange.1
  100.5 2.1 %copy-done.1 = bf16[2112,896]{1,0:T(8,128)(2,1)S(1)} copy-done((bf16[2112,896]{1,0:T(8,128)(2,1)S(1)}, bf16[2112,896]{1,0:T(8,128)(2,1)}, u32[]{:S(2)}) %copy-start.1) | copy-done | bytes 3784728
  102.6 3.0 %first_half.1.acc_ref = f32[2,256,512]{2,1,0:T(8,128)S(1)} custom-call(s32[2]{0:T(128)S(1)} %pad_add_fusion.at_ref, bf16[4,2,264,256]{3,2,1,0:T(8,128)(2,1)S(1)} %get-tuple-element.36.fp_ref, bf16[8,264,896]{2,1,0:T(8,128)(2,1)S(1)} %bitcast.70), custom_call_target="tpu_custom_call" | custom-call | flops 968884224 | bytes 5914632 | tf_op jit(solution)/shard_map/first_half/pallas_call | solution.py:77
  105.7 5.1 %second_half.1 = (bf16[2,512,256]{2,1,0:T(8,128)(2,1)S(1)}, f32[2,512,256]{2,1,0:T(8,128)S(1)}, f32[1,256]{1,0:T(1,128)S(1)}) custom-call(s32[2]{0:T(128)S(1)} %pad_add_fusion.at_ref, bf16[4,2,264,256]{3,2,1,0:T(8,128)(2,1)S(1)} %get-tuple-element.34.fp_ref, bf16[8,264,896]{2,1,0:T(8,128)(2,1)} %collective-permute-done.7.w_ref.other_ref, ...), custom_call_target="tpu_custom_call" | custom-call | flops 968884224 | bytes 7488520 | tf_op jit(solution)/shard_map/second_half/pallas_call | solution.py:77
  110.8 1.4 sums.1
  112.2 14.4 %all_to_all.20.stat_ref = f32[8,4,256]{2,1,0:T(4,128)S(1)} all-to-all(f32[8,4,256]{2,1,0:T(4,128)S(1)} %get-tuple-element.48), channel_id=1, replica_groups=mesh['xh'=2,'xl'=2,'zl'=4,'core'=2,'y'=8,'zh'=2] {'y'}, dimensions={0} | all-to-all | bytes 65536 | tf_op jit(solution)/shard_map/all_to_all | solution.py:383
  126.6 6.3 %backward.1 = (bf16[8,144,256]{2,1,0:T(8,128)(2,1)}, bf16[8,384,256]{2,1,0:T(8,128)(2,1)}, bf16[2,512,256]{2,1,0:T(8,128)(2,1)S(1)}) custom-call(s32[2]{0:T(128)S(1)} %pad_add_fusion.at_ref, f32[2,512,256]{2,1,0:T(8,128)S(1)} %get-tuple-element.41.slope_ref, bf16[2,512,256]{2,1,0:T(8,128)(2,1)S(1)} %get-tuple-element.42.img_ref, ...), custom_call_target="tpu_custom_call" | custom-call | flops 1937768448 | bytes 12914696 | tf_op jit(solution)/shard_map/backward/pallas_call | solution.py:77
  132.9 3.5 %all-to-all-start.2 = ((bf16[8,144,256]{2,1,0:T(8,128)(2,1)}), bf16[8,144,256]{2,1,0:T(8,128)(2,1)S(1)}, u32[]{:S(2)}, u32[]{:S(2)}) async-start(bf16[8,144,256]{2,1,0:T(8,128)(2,1)} %get-tuple-element.53), calls=%async_computation.2 | async-start | bytes 1179648 | tf_op jit(solution)/shard_map/all_to_all | solution.py:392
  136.5 3.5 %collective-permute-start.10 = (f32[512]{0:T(512)S(1)}, f32[512]{0:T(512)S(1)}, u32[]{:S(2)}, u32[]{:S(2)}) collective-permute-start(f32[512]{0:T(512)S(1)} %bitcast.86), channel_id=1, source_target_pairs={{0,1},{1,0},{2,3},{3,2},{4,5},{5,4},{6,7},{7,6},{8,9},{9,8},{10,11... | collective-permute-start | bytes 6152 | tf_op jit(solution)/shard_map/ppermute | solution.py:39
  140.1 6.4 %collective-permute-start.9 = (bf16[448,256]{1,0:T(8,128)(2,1)S(1)}, bf16[448,256]{1,0:T(8,128)(2,1)S(1)}, u32[]{:S(2)}, u32[]{:S(2)}) collective-permute-start(bf16[448,256]{1,0:T(8,128)(2,1)S(1)} %dynamic-slice_bitcast_fusion), channel_id=1, source_target_pairs={{0,1},{1,0},{2,3},{3,2},{4,5},{5,4},{6,7},{7,6},{8,9},{9,8},{10,11... | collective-permute-start | bytes 688136 | tf_op jit(solution)/shard_map/ppermute | solution.py:39
  146.7 11.5 %all-to-all-done.2.sig_ref = bf16[8,144,256]{2,1,0:T(8,128)(2,1)S(1)} async-done(((bf16[8,144,256]{2,1,0:T(8,128)(2,1)}), bf16[8,144,256]{2,1,0:T(8,128)(2,1)S(1)}, u32[]{:S(2)}, u32[]{:S(2)}) %all-to-all-start.2) | async-done | bytes 589856 | tf_op jit(solution)/shard_map/all_to_all | solution.py:392
  158.2 16.8 %reduce-scatter.2.cloned.1.call-done.conv_ref = bf16[384,256]{1,0:T(8,128)(2,1)} async-done(((bf16[3072,256]{1,0:T(8,128)(2,1)}), bf16[384,256]{1,0:T(8,128)(2,1)}) %reduce-scatter.2.cloned.1.call-update) | async-done | bytes 196624 | tf_op jit(solution)/shard_map/reduce_scatter | solution.py:389
  175.0 0.9 copy-done.3
  175.9 0.8 pack.1
  176.8 7.9 %all-to-all-start.3 = ((bf16[4,192,256]{2,1,0:T(8,128)(2,1)}), bf16[4,192,256]{2,1,0:T(8,128)(2,1)S(1)}, u32[]{:S(2)}, u32[]{:S(2)}) async-start(bf16[4,192,256]{2,1,0:T(8,128)(2,1)} %bitcast.32), calls=%async_computation.4 | async-start | bytes 786432 | tf_op jit(solution)/shard_map/all_to_all | solution.py:66
  184.7 1.3 fusion
  186.1 9.9 %all-to-all-done.3 = bf16[4,192,256]{2,1,0:T(8,128)(2,1)S(1)} async-done(((bf16[4,192,256]{2,1,0:T(8,128)(2,1)}), bf16[4,192,256]{2,1,0:T(8,128)(2,1)S(1)}, u32[]{:S(2)}, u32[]{:S(2)}) %all-to-all-start.3) | async-done | bytes 393248 | tf_op jit(solution)/shard_map/all_to_all | solution.py:66
  196.1 0.8 copy.29
  196.9 0.8 copy.28
  (68 shorter events, 1.5 us)
Async XLA Ops:
  7.2 30.8 %copy-start = (bf16[512,448]{0,1:T(8,128)(2,1)S(1)}, bf16[512,448]{0,1:T(8,128)(2,1)}, u32[]{:S(2)}) copy-start(bf16[512,448]{0,1:T(8,128)(2,1)} %param.13) | copy-start | bytes 1376260
  7.2 17.7 %copy-start.7 = (bf16[8,64,72]{2,1,0:T(8,128)(2,1)S(1)}, bf16[8,64,72]{2,1,0:T(8,128)(2,1)}, u32[]{:S(2)}) copy-start(bf16[8,64,72]{2,1,0:T(8,128)(2,1)} %param.8) | copy-start | bytes 221188
  7.2 17.5 %copy-start.6 = (bf16[8,64,192]{2,1,0:T(8,128)(2,1)S(1)}, bf16[8,64,192]{2,1,0:T(8,128)(2,1)}, u32[]{:S(2)}) copy-start(bf16[8,64,192]{2,1,0:T(8,128)(2,1)} %param.9) | copy-start | bytes 589828
  7.2 77.3 %all-gather.5.cloned.1.call-start = ((), (), s32[]{:S(2)}) async-start(), calls=%async_computation.6 | async-start | bytes 4257792 | tf_op jit(solution)/shard_map/all_gather | solution.py:328
  24.7 13.0 %copy-start.8 = (f32[448]{0:T(512)S(1)}, f32[448]{0:T(512)}, u32[]{:S(2)}) copy-start(f32[448]{0:T(512)} %param.11) | copy-start | bytes 5380
  24.7 13.1 %copy-start.9 = (s32[1,8]{1,0:T(1,128)S(1)}, s32[1,8]{1,0:T(1,128)}, u32[]{:S(2)}) copy-start(s32[1,8]{1,0:T(1,128)} %param.15) | copy-start | bytes 100
  25.9 20.6 %all-to-all-start = ((bf16[4,192,256]{2,1,0:T(8,128)(2,1)}), bf16[4,192,256]{2,1,0:T(8,128)(2,1)S(1)}, u32[]{:S(2)}, u32[]{:S(2)}) async-start(bf16[4,192,256]{2,1,0:T(8,128)(2,1)} %pad_maximum_fusion), calls=%async_computation | async-start | bytes 786432 | tf_op jit(solution)/shard_map/all_to_all | solution.py:66
  37.1 137.9 %reduce-scatter.2.cloned.1.call-start = ((), (), s32[]{:S(2)}) async-start(), calls=%async_computation.5 | async-start | bytes 1769472 | tf_op jit(solution)/shard_map/reduce_scatter | solution.py:389
  47.3 10.1 %collective-permute-start = (bf16[528,256]{1,0:T(8,128)(2,1)}, bf16[528,256]{1,0:T(8,128)(2,1)}, u32[]{:S(2)}, u32[]{:S(2)}) collective-permute-start(bf16[528,256]{1,0:T(8,128)(2,1)} %pad_maximum_fusion.1), channel_id=1, source_target_pairs={{0,2},{2,4},{4,6},{6,8},{8,10},{10,12},{12,14},{14,0},{1,3},{3,5},... | collective-permute-start | bytes 811016 | tf_op jit(solution)/shard_map/ppermute | solution.py:39
  50.8 9.7 %collective-permute-start.1 = (bf16[528,256]{1,0:T(8,128)(2,1)}, bf16[528,256]{1,0:T(8,128)(2,1)}, u32[]{:S(2)}, u32[]{:S(2)}) collective-permute-start(bf16[528,256]{1,0:T(8,128)(2,1)} %pad_maximum_fusion.1), channel_id=1, source_target_pairs={{0,14},{2,0},{4,2},{6,4},{8,6},{10,8},{12,10},{14,12},{1,15},{3,1}... | collective-permute-start | bytes 811016 | tf_op jit(solution)/shard_map/ppermute | solution.py:39
  57.4 10.7 %collective-permute-start.2 = (bf16[528,256]{1,0:T(8,128)(2,1)}, bf16[528,256]{1,0:T(8,128)(2,1)S(1)}, u32[]{:S(2)}, u32[]{:S(2)}) collective-permute-start(bf16[528,256]{1,0:T(8,128)(2,1)} %collective-permute-done), channel_id=1, source_target_pairs={{0,2},{2,4},{4,6},{6,8},{8,10},{10,12},{12,14},{14,0},{1,3},{3,5},... | collective-permute-start | bytes 811016 | tf_op jit(solution)/shard_map/ppermute | solution.py:39
  60.5 10.6 %collective-permute-start.3 = (bf16[528,256]{1,0:T(8,128)(2,1)}, bf16[528,256]{1,0:T(8,128)(2,1)S(1)}, u32[]{:S(2)}, u32[]{:S(2)}) collective-permute-start(bf16[528,256]{1,0:T(8,128)(2,1)} %collective-permute-done.1), channel_id=1, source_target_pairs={{0,14},{2,0},{4,2},{6,4},{8,6},{10,8},{12,10},{14,12},{1,15},{3,1}... | collective-permute-start | bytes 811016 | tf_op jit(solution)/shard_map/ppermute | solution.py:39
  68.1 9.8 %collective-permute-start.4 = (bf16[528,256]{1,0:T(8,128)(2,1)S(1)}, bf16[528,256]{1,0:T(8,128)(2,1)S(1)}, u32[]{:S(2)}, u32[]{:S(2)}) collective-permute-start(bf16[528,256]{1,0:T(8,128)(2,1)S(1)} %collective-permute-done.2), channel_id=1, source_target_pairs={{0,2},{2,4},{4,6},{6,8},{8,10},{10,12},{12,14},{14,0},{1,3},{3,5},... | collective-permute-start | bytes 811016 | tf_op jit(solution)/shard_map/ppermute | solution.py:39
  71.1 8.5 %collective-permute-start.5 = (bf16[528,256]{1,0:T(8,128)(2,1)S(1)}, bf16[528,256]{1,0:T(8,128)(2,1)S(1)}, u32[]{:S(2)}, u32[]{:S(2)}) collective-permute-start(bf16[528,256]{1,0:T(8,128)(2,1)S(1)} %collective-permute-done.3), channel_id=1, source_target_pairs={{0,14},{2,0},{4,2},{6,4},{8,6},{10,8},{12,10},{14,12},{1,15},{3,1}... | collective-permute-start | bytes 811016 | tf_op jit(solution)/shard_map/ppermute | solution.py:39
  78.0 6.6 %copy-start.5 = (bf16[528,256]{1,0:T(8,128)(2,1)}, bf16[528,256]{1,0:T(8,128)(2,1)S(1)}, u32[]{:S(2)}) copy-start(bf16[528,256]{1,0:T(8,128)(2,1)S(1)} %collective-permute-done.4) | copy-start | bytes 811012
  84.5 21.1 %collective-permute-start.7 = (bf16[8,264,896]{2,1,0:T(8,128)(2,1)}, bf16[8,264,896]{2,1,0:T(8,128)(2,1)}, u32[]{:S(2)}, u32[]{:S(2)}) collective-permute-start(bf16[8,264,896]{2,1,0:T(8,128)(2,1)} %bitcast.69), channel_id=1, source_target_pairs={{0,16},{16,0},{1,17},{17,1},{2,18},{18,2},{3,19},{19,3},{4,20},{20... | collective-permute-start | bytes 11354120 | tf_op jit(solution)/shard_map/ppermute | solution.py:39
  86.5 12.7 %collective-permute-start.6 = (bf16[528,256]{1,0:T(8,128)(2,1)}, bf16[528,256]{1,0:T(8,128)(2,1)S(1)}, u32[]{:S(2)}, u32[]{:S(2)}) collective-permute-start(bf16[528,256]{1,0:T(8,128)(2,1)} %copy-done.5), channel_id=1, source_target_pairs={{0,2},{2,4},{4,6},{6,8},{8,10},{10,12},{12,14},{14,0},{1,3},{3,5},... | collective-permute-start | bytes 811016 | tf_op jit(solution)/shard_map/ppermute | solution.py:39
  90.0 20.8 %collective-permute-start.8 = (bf16[464,256]{1,0:T(8,128)(2,1)}, bf16[464,256]{1,0:T(8,128)(2,1)}, u32[]{:S(2)}, u32[]{:S(2)}) collective-permute-start(bf16[464,256]{1,0:T(8,128)(2,1)} %fusion.18), channel_id=1, source_target_pairs={{0,1},{1,0},{2,3},{3,2},{4,5},{5,4},{6,7},{7,6},{8,9},{9,8},{10,11... | collective-permute-start | bytes 712712 | tf_op jit(solution)/shard_map/ppermute | solution.py:39
  100.5 2.1 %copy-start.1 = (bf16[2112,896]{1,0:T(8,128)(2,1)S(1)}, bf16[2112,896]{1,0:T(8,128)(2,1)}, u32[]{:S(2)}) copy-start(bf16[2112,896]{1,0:T(8,128)(2,1)} %all-gather.5.cloned.1.call-done) | copy-start | bytes 11354116
  105.7 21.0 %copy-start.2 = (bf16[2112,896]{1,0:T(8,128)(2,1)S(1)}, bf16[2112,896]{1,0:T(8,128)(2,1)}, u32[]{:S(2)}) copy-start(bf16[2112,896]{1,0:T(8,128)(2,1)} %all-gather.5.cloned.1.call-done) | copy-start | bytes 11354116
  132.9 25.3 %all-to-all-start.2 = ((bf16[8,144,256]{2,1,0:T(8,128)(2,1)}), bf16[8,144,256]{2,1,0:T(8,128)(2,1)S(1)}, u32[]{:S(2)}, u32[]{:S(2)}) async-start(bf16[8,144,256]{2,1,0:T(8,128)(2,1)} %get-tuple-element.53), calls=%async_computation.2 | async-start | bytes 1179648 | tf_op jit(solution)/shard_map/all_to_all | solution.py:392
  136.5 48.3 %copy-start.4 = (bf16[512,448]{0,1:T(8,128)(2,1)S(1)}, bf16[512,448]{0,1:T(8,128)(2,1)}, u32[]{:S(2)}) copy-start(bf16[512,448]{0,1:T(8,128)(2,1)} %param.12) | copy-start | bytes 1376260
  136.5 48.2 %collective-permute-start.10 = (f32[512]{0:T(512)S(1)}, f32[512]{0:T(512)S(1)}, u32[]{:S(2)}, u32[]{:S(2)}) collective-permute-start(f32[512]{0:T(512)S(1)} %bitcast.86), channel_id=1, source_target_pairs={{0,1},{1,0},{2,3},{3,2},{4,5},{5,4},{6,7},{7,6},{8,9},{9,8},{10,11... | collective-permute-start | bytes 6152 | tf_op jit(solution)/shard_map/ppermute | solution.py:39
  140.1 44.6 %collective-permute-start.9 = (bf16[448,256]{1,0:T(8,128)(2,1)S(1)}, bf16[448,256]{1,0:T(8,128)(2,1)S(1)}, u32[]{:S(2)}, u32[]{:S(2)}) collective-permute-start(bf16[448,256]{1,0:T(8,128)(2,1)S(1)} %dynamic-slice_bitcast_fusion), channel_id=1, source_target_pairs={{0,1},{1,0},{2,3},{3,2},{4,5},{5,4},{6,7},{7,6},{8,9},{9,8},{10,11... | collective-permute-start | bytes 688136 | tf_op jit(solution)/shard_map/ppermute | solution.py:39
  175.0 0.9 copy-start.3
  176.8 19.2 %all-to-all-start.3 = ((bf16[4,192,256]{2,1,0:T(8,128)(2,1)}), bf16[4,192,256]{2,1,0:T(8,128)(2,1)S(1)}, u32[]{:S(2)}, u32[]{:S(2)}) async-start(bf16[4,192,256]{2,1,0:T(8,128)(2,1)} %bitcast.32), calls=%async_computation.4 | async-start | bytes 786432 | tf_op jit(solution)/shard_map/all_to_all | solution.py:66
Sparse Core Ops, SparseCore 0:
  24.8 59.6 all-gather.4
  133.0 41.9 reduce-scatter.1

commit v5 on v4

--- a/solution.py
+++ b/solution.py
@@ -59,6 +59,11 @@
         full = put(full, right, me - step + N_Y)
         full = put(full, left, me + step)
     return full, right
+
+
+def swap(x, dx, dz):
+    pairs = [(a * 2 + b, (a + dx) % 2 * 2 + (b + dz) % 2) for a in range(2) for b in range(2)]
+    return lax.ppermute(x, ("xh", "zh"), pairs)
 
 
 def exchange(blocks):
@@ -124,10 +129,10 @@
     return call(
         arrange_kernel,
         "arrange",
-        16,
+        12,
         [shaped(BF, N_ZL, 2, DEEP, HALF)] * 2,
         [pltpu.VMEM((TOTAL, HALF), F32), pltpu.VMEM((2 * DEEP, HALF), F32)],
-        0,
+        HALF * TOTAL * COLS * 8,
         at,
         feats,
         far,
@@ -182,13 +187,13 @@
 def forward(at, fp_mine, fp_other, mine, other):
     flops = HALF * TOTAL * COLS * 2
     acc = call(
-        first_kernel, "first_half", 14, [shaped(F32, 2, HALF, COLS_PAD)], [], flops,
+        first_kernel, "first_half", 10, [shaped(F32, 2, HALF, COLS_PAD)], [], flops,
         at, fp_mine, mine,
     )[0]
     return call(
         second_kernel,
         "second_half",
-        18,
+        12,
         [
             shaped(BF, 2, COLS_PAD, HALF),
             shaped(F32, 2, COLS_PAD, HALF),
@@ -230,7 +235,7 @@
     return call(
         sums_kernel,
         "sums",
-        14,
+        8,
         [
             shaped(F32, N_Y, 4, HALF),
             shaped(F32, 2, COLS_PAD, HALF),
@@ -283,7 +288,7 @@
     return call(
         functools.partial(backward_kernel, width),
         "backward",
-        24,
+        22,
         [
             shaped(BF, N_Y, PAIR_SIG, HALF),
             shaped(BF, N_Y, PAIR_CONV, HALF),
@@ -299,23 +304,6 @@
     )
 
 
-def pack_kernel(at_ref, sig_ref, conv_ref, out_ref):
-    sig = sig_ref[0].astype(F32)
-    for y in range(1, N_Y):
-        sig += sig_ref[y].astype(F32)
-    pad = jnp.zeros((CONV - SIG, HALF), F32)
-    for b in range(2):
-        out_ref[at_ref[0], b] = jnp.concatenate([sig[b * SIG : (b + 1) * SIG], pad]).astype(BF)
-        out_ref[1 - at_ref[0], b] = conv_ref[b * CONV : (b + 1) * CONV]
-
-
-def pack(xh, sig, conv):
-    return call(
-        pack_kernel, "pack", 8, [shaped(BF, 2, 2, CONV, HALF)], [], 0,
-        xh.astype(jnp.int32).reshape(1), sig, conv,
-    )[0].reshape(4, CONV, HALF)
-
-
 def per_device(sig_feat, conv_feat, weight, gain, text, grad_out, tile_count, tile_block):
     zh = lax.axis_index("zh")
     slots, tile_tokens = sig_feat.shape[:2]
@@ -386,27 +374,35 @@
     )
     stat, sig_p, conv_p = lax.optimization_barrier((stat, sig_p, conv_p))
     text_square = jnp.sum(stat[:, 2:], axis=0).reshape(tokens)
-    conv_p = lax.psum_scatter(
+    conv_g = lax.psum_scatter(
         conv_p.reshape(N_Y * PAIR_CONV, HALF), "y", scatter_dimension=0, tiled=True
-    )
-    sig_p = lax.all_to_all(sig_p, "y", 0, 0, tiled=True)
+    ).reshape(2, CONV, HALF)
+    sig_g = lax.all_to_all(sig_p, "y", 0, 0, tiled=True)
+    sig_g = jnp.sum(sig_g.astype(F32), axis=0).astype(BF).reshape(2, SIG, HALF)
+
+    def pick(x, which):
+        return lax.dynamic_index_in_dim(x, which, 0, keepdims=False)
 
     n_image = n_image[:, :COLS]
-    n_keep = lax.dynamic_index_in_dim(n_image, zh, 0, keepdims=False)
-    n_got = shift(lax.dynamic_index_in_dim(n_image, 1 - zh, 0, keepdims=False), "zh", 1)
-    n_slots = ordered(zh, n_keep, n_got, 1)
+    sig_got = shift(pick(sig_g, 1 - zh), "zh", 1)
+    n_got = shift(pick(n_image, 1 - zh), "zh", 1)
+    text_got = shift(text_square, "zh", 1)
+    conv_g, sig_got, n_got, text_got = lax.optimization_barrier((conv_g, sig_got, n_got, text_got))
+
+    def tokens_first(keep, got, width):
+        return ordered(zh, keep, got, 1).T.reshape(slots, tile_tokens, width)
+
+    conv_got = swap(pick(conv_g, 1 - zh), 1, 1)
+    conv_keep = swap(pick(conv_g, zh), 1, 0)
+    grad_conv = tokens_first(conv_keep, conv_got, CONV)
+    grad_sig = tokens_first(pick(sig_g, zh), sig_got, SIG)
+
+    n_slots = ordered(zh, pick(n_image, zh), n_got, 1)
     n_placed = jnp.dot(n_slots, chooser, preferred_element_type=F32).astype(BF)
-    text_square = text_square + shift(text_square, "zh", 1)
-    inv_text = lax.rsqrt(text_square / model_width + EPS)
+    inv_text = lax.rsqrt((text_square + text_got) / model_width + EPS)
     n_text = (text_f * inv_text[None, :] * gain[:, None]).astype(BF)
     normed = jnp.where(is_image[None, :], n_placed, n_text).T
-
-    sig_g, conv_g = exchange(pack(xh, sig_p, conv_p))
-
-    def tokens_first(x, width):
-        return jnp.concatenate([x[0], x[1]], axis=1).T.reshape(slots, tile_tokens, width)
-
-    return normed, tokens_first(sig_g, SIG), tokens_first(conv_g, CONV)
+    return normed, grad_sig, grad_conv
 
 
 def solution(mesh):

time: 205 us -> 201 us (0.980)
  waiting for transfers between devices: 63.3 us -> 56.1 us
  starting transfers between devices: 62.7 us -> 67.2 us
  local copies, waits for them, and re-layouts: 7.71 us -> 5.46 us
    ppermute x0 -> x2, starting transfers between devices: none -> 10.5 us  [swap(): return lax.ppermute(x, ('xh', 'zh'), pairs)]
    all_to_all x2 -> x1, waiting for transfers between devices: 17.7 us -> 7.85 us  [exchange(): lax.all_to_all(blocks, ('xh', 'zh'), split_axis=0, concat_axis=0, tiled=T...]
    reduce_scatter x1, waiting for transfers between devices: 16.8 us -> 6.99 us  [per_device(): lax.psum_scatter(conv_p.reshape(N_Y * PAIR_CONV, HALF), 'y', scatter_dime...]
    all_to_all x2 -> x1, starting transfers between devices: 19.1 us -> 11.2 us  [exchange(): lax.all_to_all(blocks, ('xh', 'zh'), split_axis=0, concat_axis=0, tiled=T...]
    ppermute x11 -> x12, waiting for transfers between devices: 12.4 us -> 20 us  [shift(): return lax.ppermute(x, axis, [(i, (i + by) % n) for i in range(n)])]
    ppermute x0 -> x2, waiting for transfers between devices: none -> 4.43 us  [swap(): return lax.ppermute(x, ('xh', 'zh'), pairs)]
    ppermute x11 -> x12, starting transfers between devices: 40 us -> 41.9 us  [shift(): return lax.ppermute(x, axis, [(i, (i + by) % n) for i in range(n)])]
    pallas_call x7 -> x6, Pallas kernels: 19.5 us -> 17.6 us  [call(): pl.pallas_call(kernel, in_specs=[SMEM] + [VMEM] * (len(args) - 1), out_sp...]
  transfers between devices with their start and end apart: 16 -> 18, of which waited for: 12 -> 13; matrix products, arithmetic and copies ran while one was open for 4% -> 4% of each run, Pallas kernels for 5% -> 5%
where the time goes in v5:
time: 201 us; the launch traced here: 199 us
  starting transfers between devices  67.2 us (33%)
  waiting for transfers between devices  56.1 us (28%)
  blocking collectives  30.3 us (15%)
  Pallas kernels  17.6 us (9%)
  between operations  15.3 us (8%)
  local copies, waits for them, and re-layouts  5.46 us (3%)
  other arithmetic  4.63 us (2%)
    ppermute x12, starting transfers between devices, shift(): return lax.ppermute(x, axis, [(i, (i + by) % n) for i in range(n)])  41.9 us
    ppermute x12, waiting for transfers between devices, shift(): return lax.ppermute(x, axis, [(i, (i + by) % n) for i in range(n)])  20 us
    pallas_call x6, Pallas kernels, call(): pl.pallas_call(kernel, in_specs=[SMEM] + [VMEM] * (len(args) - 1), out_sp...  17.6 us
    all_gather x1, blocking collectives, per_device(): w_x = lax.all_gather(weight, ('xh', 'xl'), axis=0)  15.9 us
    all_to_all x1, blocking collectives, per_device(): stat = lax.all_to_all(stat, 'y', 0, 0, tiled=True)  14.4 us
    all_to_all x1, waiting for transfers between devices, per_device(): sig_g = lax.all_to_all(sig_p, 'y', 0, 0, tiled=True)  11.7 us
    all_to_all x1, starting transfers between devices, exchange(): lax.all_to_all(blocks, ('xh', 'zh'), split_axis=0, concat_axis=0, tiled=T...  11.2 us
    ppermute x2, starting transfers between devices, swap(): return lax.ppermute(x, ('xh', 'zh'), pairs)  10.5 us
  transfers between devices with their start and end apart: 18, of which 13 were waited for; matrix products, arithmetic and copies ran while one was open for 4% of the time, Pallas kernels for 5%

profile of v5, /device:TPU:6, one launch (start us, length us, event | category | flops | bytes accessed | tf_op | source)
XLA Modules:
  0.0 198.5 jit_solution(4260357372060392007)
XLA Ops:
  7.3 15.9 %all-gather.2.w_ref = bf16[4,132,448]{2,1,0:T(8,128)(2,1)S(1)} all-gather(bf16[1,132,448]{2,1,0:T(8,128)(2,1)} %bitcast.82), channel_id=2, replica_groups=mesh['xh'=2,'xl'=2,'zl'=4,'core'=2,'y'=8,'zh'=2] {'xh','xl'}, dimensions={0}, use_global_device_ids=true | all-gather | bytes 591360 | tf_op jit(solution)/shard_map/all_gather | solution.py:314
  23.2 1.5 side_by_side.1
  25.1 0.8 pad_maximum_fusion
  25.9 11.2 %all-to-all-start = ((bf16[4,192,256]{2,1,0:T(8,128)(2,1)}), bf16[4,192,256]{2,1,0:T(8,128)(2,1)S(1)}, u32[]{:S(2)}, u32[]{:S(2)}) async-start(bf16[4,192,256]{2,1,0:T(8,128)(2,1)} %pad_maximum_fusion), calls=%async_computation | async-start | bytes 786432 | tf_op jit(solution)/shard_map/all_to_all | solution.py:71
  37.9 0.6 convolution_convert_fusion.1
  38.6 7.9 %all-to-all-done = bf16[4,192,256]{2,1,0:T(8,128)(2,1)S(1)} async-done(((bf16[4,192,256]{2,1,0:T(8,128)(2,1)}), bf16[4,192,256]{2,1,0:T(8,128)(2,1)S(1)}, u32[]{:S(2)}, u32[]{:S(2)}) %all-to-all-start) | async-done | bytes 393248 | tf_op jit(solution)/shard_map/all_to_all | solution.py:71
  46.5 0.7 pad_maximum_fusion.1
  47.3 3.5 %collective-permute-start = (bf16[528,256]{1,0:T(8,128)(2,1)}, bf16[528,256]{1,0:T(8,128)(2,1)}, u32[]{:S(2)}, u32[]{:S(2)}) collective-permute-start(bf16[528,256]{1,0:T(8,128)(2,1)} %pad_maximum_fusion.1), channel_id=1, source_target_pairs={{0,2},{2,4},{4,6},{6,8},{8,10},{10,12},{12,14},{14,0},{1,3},{3,5},... | collective-permute-start | bytes 811016 | tf_op jit(solution)/shard_map/ppermute | solution.py:39
  50.7 3.8 %collective-permute-start.1 = (bf16[528,256]{1,0:T(8,128)(2,1)}, bf16[528,256]{1,0:T(8,128)(2,1)S(1)}, u32[]{:S(2)}, u32[]{:S(2)}) collective-permute-start(bf16[528,256]{1,0:T(8,128)(2,1)} %pad_maximum_fusion.1), channel_id=1, source_target_pairs={{0,14},{2,0},{4,2},{6,4},{8,6},{10,8},{12,10},{14,12},{1,15},{3,1}... | collective-permute-start | bytes 811016 | tf_op jit(solution)/shard_map/ppermute | solution.py:39
  54.8 0.7 fusion.18
  55.6 1.8 collective-permute-done
  57.4 2.8 %collective-permute-start.2 = (bf16[528,256]{1,0:T(8,128)(2,1)}, bf16[528,256]{1,0:T(8,128)(2,1)S(1)}, u32[]{:S(2)}, u32[]{:S(2)}) collective-permute-start(bf16[528,256]{1,0:T(8,128)(2,1)} %collective-permute-done), channel_id=1, source_target_pairs={{0,2},{2,4},{4,6},{6,8},{8,10},{10,12},{12,14},{14,0},{1,3},{3,5},... | collective-permute-start | bytes 811016 | tf_op jit(solution)/shard_map/ppermute | solution.py:39
  60.2 0.4 collective-permute-done.1
  60.6 4.0 %collective-permute-start.3 = (bf16[528,256]{1,0:T(8,128)(2,1)S(1)}, bf16[528,256]{1,0:T(8,128)(2,1)S(1)}, u32[]{:S(2)}, u32[]{:S(2)}) collective-permute-start(bf16[528,256]{1,0:T(8,128)(2,1)S(1)} %collective-permute-done.1), channel_id=1, source_target_pairs={{0,14},{2,0},{4,2},{6,4},{8,6},{10,8},{12,10},{14,12},{1,15},{3,1}... | collective-permute-start | bytes 811016 | tf_op jit(solution)/shard_map/ppermute | solution.py:39
  64.6 1.0 bitcast_dynamic-update-slice_fusion.5
  65.6 2.5 %collective-permute-done.2 = bf16[528,256]{1,0:T(8,128)(2,1)S(1)} collective-permute-done((bf16[528,256]{1,0:T(8,128)(2,1)}, bf16[528,256]{1,0:T(8,128)(2,1)S(1)}, u32[]{:S(2)}, u32[]{:S(2)}) %collective-permute-start.2) | collective-permute-done | bytes 270368 | tf_op jit(solution)/shard_map/ppermute | solution.py:39
  68.1 2.6 %collective-permute-start.4 = (bf16[528,256]{1,0:T(8,128)(2,1)S(1)}, bf16[528,256]{1,0:T(8,128)(2,1)S(1)}, u32[]{:S(2)}, u32[]{:S(2)}) collective-permute-start(bf16[528,256]{1,0:T(8,128)(2,1)S(1)} %collective-permute-done.2), channel_id=1, source_target_pairs={{0,2},{2,4},{4,6},{6,8},{8,10},{10,12},{12,14},{14,0},{1,3},{3,5},... | collective-permute-start | bytes 811016 | tf_op jit(solution)/shard_map/ppermute | solution.py:39
  70.8 4.6 %collective-permute-start.5 = (bf16[528,256]{1,0:T(8,128)(2,1)S(1)}, bf16[528,256]{1,0:T(8,128)(2,1)S(1)}, u32[]{:S(2)}, u32[]{:S(2)}) collective-permute-start(bf16[528,256]{1,0:T(8,128)(2,1)S(1)} %collective-permute-done.3), channel_id=1, source_target_pairs={{0,14},{2,0},{4,2},{6,4},{8,6},{10,8},{12,10},{14,12},{1,15},{3,1}... | collective-permute-start | bytes 811016 | tf_op jit(solution)/shard_map/ppermute | solution.py:39
  75.5 2.4 %collective-permute-done.4 = bf16[528,256]{1,0:T(8,128)(2,1)S(1)} collective-permute-done((bf16[528,256]{1,0:T(8,128)(2,1)S(1)}, bf16[528,256]{1,0:T(8,128)(2,1)S(1)}, u32[]{:S(2)}, u32[]{:S(2)}) %collective-permute-start.4) | collective-permute-done | bytes 270368 | tf_op jit(solution)/shard_map/ppermute | solution.py:39
  78.0 0.7 copy-done.3
  78.6 0.8 collective-permute-done.5
  79.5 5.0 %all-gather.5.cloned.1.call-done = bf16[2112,896]{1,0:T(8,128)(2,1)} async-done(((bf16[264,896]{1,0:T(8,128)(2,1)}), bf16[2112,896]{1,0:T(8,128)(2,1)}) %all-gather.5.cloned.1.call-update) | async-done | bytes 3784720 | tf_op jit(solution)/shard_map/all_gather | solution.py:316
  84.5 2.0 collective-permute-start.7
  86.5 3.5 %collective-permute-start.6 = (bf16[528,256]{1,0:T(8,128)(2,1)}, bf16[528,256]{1,0:T(8,128)(2,1)S(1)}, u32[]{:S(2)}, u32[]{:S(2)}) collective-permute-start(bf16[528,256]{1,0:T(8,128)(2,1)} %copy-done.3), channel_id=1, source_target_pairs={{0,2},{2,4},{4,6},{6,8},{8,10},{10,12},{12,14},{14,0},{1,3},{3,5},... | collective-permute-start | bytes 811016 | tf_op jit(solution)/shard_map/ppermute | solution.py:39
  90.1 1.2 fusion.1
  91.3 3.3 %collective-permute-start.8 = (bf16[464,256]{1,0:T(8,128)(2,1)}, bf16[464,256]{1,0:T(8,128)(2,1)S(1)}, u32[]{:S(2)}, u32[]{:S(2)}) collective-permute-start(bf16[464,256]{1,0:T(8,128)(2,1)} %fusion.18), channel_id=1, source_target_pairs={{0,1},{1,0},{2,3},{3,2},{4,5},{5,4},{6,7},{7,6},{8,9},{9,8},{10,11... | collective-permute-start | bytes 712712 | tf_op jit(solution)/shard_map/ppermute | solution.py:39
  94.6 4.5 %collective-permute-done.6.far_ref = bf16[528,256]{1,0:T(8,128)(2,1)S(1)} collective-permute-done((bf16[528,256]{1,0:T(8,128)(2,1)}, bf16[528,256]{1,0:T(8,128)(2,1)S(1)}, u32[]{:S(2)}, u32[]{:S(2)}) %collective-permute-start.6) | collective-permute-done | bytes 270368 | tf_op jit(solution)/shard_map/ppermute | solution.py:39
  99.2 1.3 arrange.1
  100.5 0.7 copy-done.1
  101.2 3.1 %first_half.1.acc_ref = f32[2,256,512]{2,1,0:T(8,128)S(1)} custom-call(s32[2]{0:T(128)S(1)} %pad_add_fusion.at_ref, bf16[4,2,264,256]{3,2,1,0:T(8,128)(2,1)S(1)} %get-tuple-element.40.fp_ref, bf16[8,264,896]{2,1,0:T(8,128)(2,1)S(1)} %bitcast.68), custom_call_target="tpu_custom_call" | custom-call | flops 968884224 | bytes 5914632 | tf_op jit(solution)/shard_map/first_half/pallas_call | solution.py:82
  104.3 5.0 %second_half.1 = (bf16[2,512,256]{2,1,0:T(8,128)(2,1)S(1)}, f32[2,512,256]{2,1,0:T(8,128)S(1)}, f32[1,256]{1,0:T(1,128)S(1)}) custom-call(s32[2]{0:T(128)S(1)} %pad_add_fusion.at_ref, bf16[4,2,264,256]{3,2,1,0:T(8,128)(2,1)S(1)} %get-tuple-element.38.fp_ref, bf16[8,264,896]{2,1,0:T(8,128)(2,1)} %collective-permute-done.7.w_ref.other_ref, ...), custom_call_target="tpu_custom_call" | custom-call | flops 968884224 | bytes 7488520 | tf_op jit(solution)/shard_map/second_half/pallas_call | solution.py:82
  109.3 0.4 sums.1
  109.7 14.4 %all_to_all.15.stat_ref = f32[8,4,256]{2,1,0:T(4,128)S(1)} all-to-all(f32[8,4,256]{2,1,0:T(4,128)S(1)} %get-tuple-element.52), channel_id=1, replica_groups=mesh['xh'=2,'xl'=2,'zl'=4,'core'=2,'y'=8,'zh'=2] {'y'}, dimensions={0} | all-to-all | bytes 65536 | tf_op jit(solution)/shard_map/all_to_all | solution.py:371
  124.1 6.3 %backward.1 = (bf16[8,144,256]{2,1,0:T(8,128)(2,1)}, bf16[8,384,256]{2,1,0:T(8,128)(2,1)}, bf16[2,512,256]{2,1,0:T(8,128)(2,1)S(1)}) custom-call(s32[2]{0:T(128)S(1)} %pad_add_fusion.at_ref, f32[2,512,256]{2,1,0:T(8,128)S(1)} %get-tuple-element.45.slope_ref, bf16[2,512,256]{2,1,0:T(8,128)(2,1)S(1)} %get-tuple-element.46.img_ref, ...), custom_call_target="tpu_custom_call" | custom-call | flops 1937768448 | bytes 12914696 | tf_op jit(solution)/shard_map/backward/pallas_call | solution.py:82
  130.4 3.5 %all-to-all-start.2 = ((bf16[8,144,256]{2,1,0:T(8,128)(2,1)}), bf16[8,144,256]{2,1,0:T(8,128)(2,1)S(1)}, u32[]{:S(2)}, u32[]{:S(2)}) async-start(bf16[8,144,256]{2,1,0:T(8,128)(2,1)} %get-tuple-element.57), calls=%async_computation.3 | async-start | bytes 1179648 | tf_op jit(solution)/shard_map/all_to_all | solution.py:380
  134.1 3.5 %collective-permute-start.10 = (bf16[448,256]{1,0:T(8,128)(2,1)S(1)}, bf16[448,256]{1,0:T(8,128)(2,1)S(1)}, u32[]{:S(2)}, u32[]{:S(2)}) collective-permute-start(bf16[448,256]{1,0:T(8,128)(2,1)S(1)} %dynamic-slice_bitcast_fusion), channel_id=1, source_target_pairs={{0,1},{1,0},{2,3},{3,2},{4,5},{5,4},{6,7},{7,6},{8,9},{9,8},{10,11... | collective-permute-start | bytes 688136 | tf_op jit(solution)/shard_map/ppermute | solution.py:39
  137.6 6.4 %collective-permute-start.11 = (f32[512]{0:T(512)S(1)}, f32[512]{0:T(512)S(1)}, u32[]{:S(2)}, u32[]{:S(2)}) collective-permute-start(f32[512]{0:T(512)S(1)} %bitcast.88), channel_id=1, source_target_pairs={{0,1},{1,0},{2,3},{3,2},{4,5},{5,4},{6,7},{7,6},{8,9},{9,8},{10,11... | collective-permute-start | bytes 6152 | tf_op jit(solution)/shard_map/ppermute | solution.py:39
  144.0 11.7 %all-to-all-done.2 = bf16[8,144,256]{2,1,0:T(8,128)(2,1)S(1)} async-done(((bf16[8,144,256]{2,1,0:T(8,128)(2,1)}), bf16[8,144,256]{2,1,0:T(8,128)(2,1)S(1)}, u32[]{:S(2)}, u32[]{:S(2)}) %all-to-all-start.2) | async-done | bytes 589856 | tf_op jit(solution)/shard_map/all_to_all | solution.py:380
  155.8 1.9 collective-permute-start.9
  158.0 7.6 %collective-permute-done.9 = bf16[72,256]{1,0:T(8,128)(2,1)S(1)} collective-permute-done((bf16[72,256]{1,0:T(8,128)(2,1)S(1)}, bf16[72,256]{1,0:T(8,128)(2,1)S(1)}, u32[]{:S(2)}, u32[]{:S(2)}) %collective-permute-start.9) | collective-permute-done | bytes 36896 | tf_op jit(solution)/shard_map/ppermute | solution.py:39
  165.6 7.0 %reduce-scatter.2.cloned.1.call-done = bf16[384,256]{1,0:T(8,128)(2,1)} async-done(((bf16[3072,256]{1,0:T(8,128)(2,1)}), bf16[384,256]{1,0:T(8,128)(2,1)}) %reduce-scatter.2.cloned.1.call-update) | async-done | bytes 196624 | tf_op jit(solution)/shard_map/reduce_scatter | solution.py:377
  172.6 1.0 constant_dynamic-slice_fusion.1
  173.6 2.5 %collective-permute-start.12 = (bf16[192,256]{0,1:T(8,128)(2,1)S(1)}, bf16[192,256]{0,1:T(8,128)(2,1)S(1)}, u32[]{:S(2)}, u32[]{:S(2)}) collective-permute-start(bf16[192,256]{0,1:T(8,128)(2,1)S(1)} %bitcast.83), channel_id=1, source_target_pairs={{0,256},{1,257},{256,0},{257,1},{2,258},{3,259},{258,2},{259,3},{4... | collective-permute-start | bytes 294920 | tf_op jit(solution)/shard_map/ppermute | solution.py:66
  176.2 8.0 %collective-permute-start.13 = (bf16[192,256]{0,1:T(8,128)(2,1)S(1)}, bf16[192,256]{0,1:T(8,128)(2,1)S(1)}, u32[]{:S(2)}, u32[]{:S(2)}) collective-permute-start(bf16[192,256]{0,1:T(8,128)(2,1)S(1)} %bitcast.84), channel_id=1, source_target_pairs={{0,257},{1,256},{256,1},{257,0},{2,259},{3,258},{258,3},{259,2},{4... | collective-permute-start | bytes 294920 | tf_op jit(solution)/shard_map/ppermute | solution.py:66
  184.4 1.3 fusion
  185.7 0.8 copy.48
  186.5 4.4 %collective-permute-done.13 = bf16[192,256]{0,1:T(8,128)(2,1)S(1)} collective-permute-done((bf16[192,256]{0,1:T(8,128)(2,1)S(1)}, bf16[192,256]{0,1:T(8,128)(2,1)S(1)}, u32[]{:S(2)}, u32[]{:S(2)}) %collective-permute-start.13) | collective-permute-done | bytes 98336 | tf_op jit(solution)/shard_map/ppermute | solution.py:66
  190.9 0.7 pad_maximum_fusion.2
  (69 shorter events, 2.1 us)
Async XLA Ops:
  7.2 30.8 %copy-start = (bf16[512,448]{0,1:T(8,128)(2,1)S(1)}, bf16[512,448]{0,1:T(8,128)(2,1)}, u32[]{:S(2)}) copy-start(bf16[512,448]{0,1:T(8,128)(2,1)} %param.13) | copy-start | bytes 1376260
  7.2 17.7 %copy-start.5 = (bf16[8,64,72]{2,1,0:T(8,128)(2,1)S(1)}, bf16[8,64,72]{2,1,0:T(8,128)(2,1)}, u32[]{:S(2)}) copy-start(bf16[8,64,72]{2,1,0:T(8,128)(2,1)} %param.8) | copy-start | bytes 221188
  7.2 17.5 %copy-start.4 = (bf16[8,64,192]{2,1,0:T(8,128)(2,1)S(1)}, bf16[8,64,192]{2,1,0:T(8,128)(2,1)}, u32[]{:S(2)}) copy-start(bf16[8,64,192]{2,1,0:T(8,128)(2,1)} %param.9) | copy-start | bytes 589828
  7.2 77.3 %all-gather.5.cloned.1.call-start = ((), (), s32[]{:S(2)}) async-start(), calls=%async_computation.5 | async-start | bytes 4257792 | tf_op jit(solution)/shard_map/all_gather | solution.py:316
  24.7 13.0 %copy-start.6 = (f32[448]{0:T(512)S(1)}, f32[448]{0:T(512)}, u32[]{:S(2)}) copy-start(f32[448]{0:T(512)} %param.11) | copy-start | bytes 5380
  24.7 13.1 %copy-start.7 = (s32[1,8]{1,0:T(1,128)S(1)}, s32[1,8]{1,0:T(1,128)}, u32[]{:S(2)}) copy-start(s32[1,8]{1,0:T(1,128)} %param.15) | copy-start | bytes 100
  25.9 20.6 %all-to-all-start = ((bf16[4,192,256]{2,1,0:T(8,128)(2,1)}), bf16[4,192,256]{2,1,0:T(8,128)(2,1)S(1)}, u32[]{:S(2)}, u32[]{:S(2)}) async-start(bf16[4,192,256]{2,1,0:T(8,128)(2,1)} %pad_maximum_fusion), calls=%async_computation | async-start | bytes 786432 | tf_op jit(solution)/shard_map/all_to_all | solution.py:71
  37.1 135.5 %reduce-scatter.2.cloned.1.call-start = ((), (), s32[]{:S(2)}) async-start(), calls=%async_computation.4 | async-start | bytes 1769472 | tf_op jit(solution)/shard_map/reduce_scatter | solution.py:377
  47.3 10.1 %collective-permute-start = (bf16[528,256]{1,0:T(8,128)(2,1)}, bf16[528,256]{1,0:T(8,128)(2,1)}, u32[]{:S(2)}, u32[]{:S(2)}) collective-permute-start(bf16[528,256]{1,0:T(8,128)(2,1)} %pad_maximum_fusion.1), channel_id=1, source_target_pairs={{0,2},{2,4},{4,6},{6,8},{8,10},{10,12},{12,14},{14,0},{1,3},{3,5},... | collective-permute-start | bytes 811016 | tf_op jit(solution)/shard_map/ppermute | solution.py:39
  50.7 9.8 %collective-permute-start.1 = (bf16[528,256]{1,0:T(8,128)(2,1)}, bf16[528,256]{1,0:T(8,128)(2,1)S(1)}, u32[]{:S(2)}, u32[]{:S(2)}) collective-permute-start(bf16[528,256]{1,0:T(8,128)(2,1)} %pad_maximum_fusion.1), channel_id=1, source_target_pairs={{0,14},{2,0},{4,2},{6,4},{8,6},{10,8},{12,10},{14,12},{1,15},{3,1}... | collective-permute-start | bytes 811016 | tf_op jit(solution)/shard_map/ppermute | solution.py:39
  57.4 10.7 %collective-permute-start.2 = (bf16[528,256]{1,0:T(8,128)(2,1)}, bf16[528,256]{1,0:T(8,128)(2,1)S(1)}, u32[]{:S(2)}, u32[]{:S(2)}) collective-permute-start(bf16[528,256]{1,0:T(8,128)(2,1)} %collective-permute-done), channel_id=1, source_target_pairs={{0,2},{2,4},{4,6},{6,8},{8,10},{10,12},{12,14},{14,0},{1,3},{3,5},... | collective-permute-start | bytes 811016 | tf_op jit(solution)/shard_map/ppermute | solution.py:39
  60.6 10.3 %collective-permute-start.3 = (bf16[528,256]{1,0:T(8,128)(2,1)S(1)}, bf16[528,256]{1,0:T(8,128)(2,1)S(1)}, u32[]{:S(2)}, u32[]{:S(2)}) collective-permute-start(bf16[528,256]{1,0:T(8,128)(2,1)S(1)} %collective-permute-done.1), channel_id=1, source_target_pairs={{0,14},{2,0},{4,2},{6,4},{8,6},{10,8},{12,10},{14,12},{1,15},{3,1}... | collective-permute-start | bytes 811016 | tf_op jit(solution)/shard_map/ppermute | solution.py:39
  68.1 9.8 %collective-permute-start.4 = (bf16[528,256]{1,0:T(8,128)(2,1)S(1)}, bf16[528,256]{1,0:T(8,128)(2,1)S(1)}, u32[]{:S(2)}, u32[]{:S(2)}) collective-permute-start(bf16[528,256]{1,0:T(8,128)(2,1)S(1)} %collective-permute-done.2), channel_id=1, source_target_pairs={{0,2},{2,4},{4,6},{6,8},{8,10},{10,12},{12,14},{14,0},{1,3},{3,5},... | collective-permute-start | bytes 811016 | tf_op jit(solution)/shard_map/ppermute | solution.py:39
  70.8 8.6 %collective-permute-start.5 = (bf16[528,256]{1,0:T(8,128)(2,1)S(1)}, bf16[528,256]{1,0:T(8,128)(2,1)S(1)}, u32[]{:S(2)}, u32[]{:S(2)}) collective-permute-start(bf16[528,256]{1,0:T(8,128)(2,1)S(1)} %collective-permute-done.3), channel_id=1, source_target_pairs={{0,14},{2,0},{4,2},{6,4},{8,6},{10,8},{12,10},{14,12},{1,15},{3,1}... | collective-permute-start | bytes 811016 | tf_op jit(solution)/shard_map/ppermute | solution.py:39
  77.9 0.7 copy-start.3
  84.5 19.8 %collective-permute-start.7 = (bf16[8,264,896]{2,1,0:T(8,128)(2,1)}, bf16[8,264,896]{2,1,0:T(8,128)(2,1)}, u32[]{:S(2)}, u32[]{:S(2)}) collective-permute-start(bf16[8,264,896]{2,1,0:T(8,128)(2,1)} %bitcast.67), channel_id=1, source_target_pairs={{0,16},{16,0},{1,17},{17,1},{2,18},{18,2},{3,19},{19,3},{4,20},{20... | collective-permute-start | bytes 11354120 | tf_op jit(solution)/shard_map/ppermute | solution.py:39
  86.5 12.7 %collective-permute-start.6 = (bf16[528,256]{1,0:T(8,128)(2,1)}, bf16[528,256]{1,0:T(8,128)(2,1)S(1)}, u32[]{:S(2)}, u32[]{:S(2)}) collective-permute-start(bf16[528,256]{1,0:T(8,128)(2,1)} %copy-done.3), channel_id=1, source_target_pairs={{0,2},{2,4},{4,6},{6,8},{8,10},{10,12},{12,14},{14,0},{1,3},{3,5},... | collective-permute-start | bytes 811016 | tf_op jit(solution)/shard_map/ppermute | solution.py:39
  91.3 18.0 %collective-permute-start.8 = (bf16[464,256]{1,0:T(8,128)(2,1)}, bf16[464,256]{1,0:T(8,128)(2,1)S(1)}, u32[]{:S(2)}, u32[]{:S(2)}) collective-permute-start(bf16[464,256]{1,0:T(8,128)(2,1)} %fusion.18), channel_id=1, source_target_pairs={{0,1},{1,0},{2,3},{3,2},{4,5},{5,4},{6,7},{7,6},{8,9},{9,8},{10,11... | collective-permute-start | bytes 712712 | tf_op jit(solution)/shard_map/ppermute | solution.py:39
  99.2 2.1 %copy-start.1 = (bf16[2112,896]{1,0:T(8,128)(2,1)S(1)}, bf16[2112,896]{1,0:T(8,128)(2,1)}, u32[]{:S(2)}) copy-start(bf16[2112,896]{1,0:T(8,128)(2,1)} %all-gather.5.cloned.1.call-done) | copy-start | bytes 11354116
  130.4 25.3 %all-to-all-start.2 = ((bf16[8,144,256]{2,1,0:T(8,128)(2,1)}), bf16[8,144,256]{2,1,0:T(8,128)(2,1)S(1)}, u32[]{:S(2)}, u32[]{:S(2)}) async-start(bf16[8,144,256]{2,1,0:T(8,128)(2,1)} %get-tuple-element.57), calls=%async_computation.3 | async-start | bytes 1179648 | tf_op jit(solution)/shard_map/all_to_all | solution.py:380
  134.0 50.3 %copy-start.2 = (bf16[512,448]{0,1:T(8,128)(2,1)S(1)}, bf16[512,448]{0,1:T(8,128)(2,1)}, u32[]{:S(2)}) copy-start(bf16[512,448]{0,1:T(8,128)(2,1)} %param.12) | copy-start | bytes 1376260
  134.1 23.9 %collective-permute-start.10 = (bf16[448,256]{1,0:T(8,128)(2,1)S(1)}, bf16[448,256]{1,0:T(8,128)(2,1)S(1)}, u32[]{:S(2)}, u32[]{:S(2)}) collective-permute-start(bf16[448,256]{1,0:T(8,128)(2,1)S(1)} %dynamic-slice_bitcast_fusion), channel_id=1, source_target_pairs={{0,1},{1,0},{2,3},{3,2},{4,5},{5,4},{6,7},{7,6},{8,9},{9,8},{10,11... | collective-permute-start | bytes 688136 | tf_op jit(solution)/shard_map/ppermute | solution.py:39
  137.6 20.4 %collective-permute-start.11 = (f32[512]{0:T(512)S(1)}, f32[512]{0:T(512)S(1)}, u32[]{:S(2)}, u32[]{:S(2)}) collective-permute-start(f32[512]{0:T(512)S(1)} %bitcast.88), channel_id=1, source_target_pairs={{0,1},{1,0},{2,3},{3,2},{4,5},{5,4},{6,7},{7,6},{8,9},{9,8},{10,11... | collective-permute-start | bytes 6152 | tf_op jit(solution)/shard_map/ppermute | solution.py:39
  155.8 9.8 %collective-permute-start.9 = (bf16[72,256]{1,0:T(8,128)(2,1)S(1)}, bf16[72,256]{1,0:T(8,128)(2,1)S(1)}, u32[]{:S(2)}, u32[]{:S(2)}) collective-permute-start(bf16[72,256]{1,0:T(8,128)(2,1)S(1)} %dynamic-slice_bitcast_fusion.3), channel_id=1, source_target_pairs={{0,1},{1,0},{2,3},{3,2},{4,5},{5,4},{6,7},{7,6},{8,9},{9,8},{10,11... | collective-permute-start | bytes 110600 | tf_op jit(solution)/shard_map/ppermute | solution.py:39
  173.6 12.8 %collective-permute-start.12 = (bf16[192,256]{0,1:T(8,128)(2,1)S(1)}, bf16[192,256]{0,1:T(8,128)(2,1)S(1)}, u32[]{:S(2)}, u32[]{:S(2)}) collective-permute-start(bf16[192,256]{0,1:T(8,128)(2,1)S(1)} %bitcast.83), channel_id=1, source_target_pairs={{0,256},{1,257},{256,0},{257,1},{2,258},{3,259},{258,2},{259,3},{4... | collective-permute-start | bytes 294920 | tf_op jit(solution)/shard_map/ppermute | solution.py:66
  176.2 14.7 %collective-permute-start.13 = (bf16[192,256]{0,1:T(8,128)(2,1)S(1)}, bf16[192,256]{0,1:T(8,128)(2,1)S(1)}, u32[]{:S(2)}, u32[]{:S(2)}) collective-permute-start(bf16[192,256]{0,1:T(8,128)(2,1)S(1)} %bitcast.84), channel_id=1, source_target_pairs={{0,257},{1,256},{256,1},{257,0},{2,259},{3,258},{258,3},{259,2},{4... | collective-permute-start | bytes 294920 | tf_op jit(solution)/shard_map/ppermute | solution.py:66
Sparse Core Ops, SparseCore 0:
  24.8 59.6 all-gather.4
  130.6 41.9 reduce-scatter.1

commit v6 on v5

--- a/solution.py
+++ b/solution.py
@@ -132,7 +132,7 @@
         12,
         [shaped(BF, N_ZL, 2, DEEP, HALF)] * 2,
         [pltpu.VMEM((TOTAL, HALF), F32), pltpu.VMEM((2 * DEEP, HALF), F32)],
-        HALF * TOTAL * COLS * 8,
+        HALF * TOTAL * COLS * 16,
         at,
         feats,
         far,
@@ -185,7 +185,7 @@
 
 
 def forward(at, fp_mine, fp_other, mine, other):
-    flops = HALF * TOTAL * COLS * 2
+    flops = HALF * TOTAL * COLS * 8
     acc = call(
         first_kernel, "first_half", 10, [shaped(F32, 2, HALF, COLS_PAD)], [], flops,
         at, fp_mine, mine,

time: 201 us -> 201 us (level)
  no operation moved by 1% of the time
where the time goes in v6:
time: 201 us; the launch traced here: 198 us
  starting transfers between devices  67.5 us (34%)
  waiting for transfers between devices  55.9 us (28%)
  blocking collectives  30.3 us (15%)
  Pallas kernels  17.6 us (9%)
  between operations  15.3 us (8%)
  local copies, waits for them, and re-layouts  4.74 us (2%)
  other arithmetic  4.63 us (2%)
    ppermute x12, starting transfers between devices, shift(): return lax.ppermute(x, axis, [(i, (i + by) % n) for i in range(n)])  42.2 us
    ppermute x12, waiting for transfers between devices, shift(): return lax.ppermute(x, axis, [(i, (i + by) % n) for i in range(n)])  19.8 us
    pallas_call x6, Pallas kernels, call(): pl.pallas_call(kernel, in_specs=[SMEM] + [VMEM] * (len(args) - 1), out_sp...  17.6 us
    all_gather x1, blocking collectives, per_device(): w_x = lax.all_gather(weight, ('xh', 'xl'), axis=0)  15.9 us
    all_to_all x1, blocking collectives, per_device(): stat = lax.all_to_all(stat, 'y', 0, 0, tiled=True)  14.4 us
    all_to_all x1, waiting for transfers between devices, per_device(): sig_g = lax.all_to_all(sig_p, 'y', 0, 0, tiled=True)  11.7 us
    all_to_all x1, starting transfers between devices, exchange(): lax.all_to_all(blocks, ('xh', 'zh'), split_axis=0, concat_axis=0, tiled=T...  11.2 us
    ppermute x2, starting transfers between devices, swap(): return lax.ppermute(x, ('xh', 'zh'), pairs)  10.5 us
  transfers between devices with their start and end apart: 18, of which 13 were waited for; matrix products, arithmetic and copies ran while one was open for 4% of the time, Pallas kernels for 5%

profile of v6, /device:TPU:6, one launch (start us, length us, event | category | flops | bytes accessed | tf_op | source)
XLA Modules:
  0.0 197.9 jit_solution(18249733526803903080)
XLA Ops:
  7.3 15.9 %all-gather.2.w_ref = bf16[4,132,448]{2,1,0:T(8,128)(2,1)S(1)} all-gather(bf16[1,132,448]{2,1,0:T(8,128)(2,1)} %bitcast.82), channel_id=2, replica_groups=mesh['xh'=2,'xl'=2,'zl'=4,'core'=2,'y'=8,'zh'=2] {'xh','xl'}, dimensions={0}, use_global_device_ids=true | all-gather | bytes 591360 | tf_op jit(solution)/shard_map/all_gather | solution.py:314
  23.2 1.5 side_by_side.1
  25.1 0.8 pad_maximum_fusion
  25.9 11.2 %all-to-all-start = ((bf16[4,192,256]{2,1,0:T(8,128)(2,1)}), bf16[4,192,256]{2,1,0:T(8,128)(2,1)S(1)}, u32[]{:S(2)}, u32[]{:S(2)}) async-start(bf16[4,192,256]{2,1,0:T(8,128)(2,1)} %pad_maximum_fusion), calls=%async_computation | async-start | bytes 786432 | tf_op jit(solution)/shard_map/all_to_all | solution.py:71
  37.9 0.6 convolution_convert_fusion.1
  38.6 7.9 %all-to-all-done = bf16[4,192,256]{2,1,0:T(8,128)(2,1)S(1)} async-done(((bf16[4,192,256]{2,1,0:T(8,128)(2,1)}), bf16[4,192,256]{2,1,0:T(8,128)(2,1)S(1)}, u32[]{:S(2)}, u32[]{:S(2)}) %all-to-all-start) | async-done | bytes 393248 | tf_op jit(solution)/shard_map/all_to_all | solution.py:71
  46.5 0.7 pad_maximum_fusion.1
  47.3 3.5 %collective-permute-start = (bf16[528,256]{1,0:T(8,128)(2,1)}, bf16[528,256]{1,0:T(8,128)(2,1)}, u32[]{:S(2)}, u32[]{:S(2)}) collective-permute-start(bf16[528,256]{1,0:T(8,128)(2,1)} %pad_maximum_fusion.1), channel_id=1, source_target_pairs={{0,2},{2,4},{4,6},{6,8},{8,10},{10,12},{12,14},{14,0},{1,3},{3,5},... | collective-permute-start | bytes 811016 | tf_op jit(solution)/shard_map/ppermute | solution.py:39
  50.7 3.8 %collective-permute-start.1 = (bf16[528,256]{1,0:T(8,128)(2,1)}, bf16[528,256]{1,0:T(8,128)(2,1)S(1)}, u32[]{:S(2)}, u32[]{:S(2)}) collective-permute-start(bf16[528,256]{1,0:T(8,128)(2,1)} %pad_maximum_fusion.1), channel_id=1, source_target_pairs={{0,14},{2,0},{4,2},{6,4},{8,6},{10,8},{12,10},{14,12},{1,15},{3,1}... | collective-permute-start | bytes 811016 | tf_op jit(solution)/shard_map/ppermute | solution.py:39
  54.8 0.7 fusion.18
  55.6 1.8 collective-permute-done
  57.4 2.8 %collective-permute-start.2 = (bf16[528,256]{1,0:T(8,128)(2,1)}, bf16[528,256]{1,0:T(8,128)(2,1)S(1)}, u32[]{:S(2)}, u32[]{:S(2)}) collective-permute-start(bf16[528,256]{1,0:T(8,128)(2,1)} %collective-permute-done), channel_id=1, source_target_pairs={{0,2},{2,4},{4,6},{6,8},{8,10},{10,12},{12,14},{14,0},{1,3},{3,5},... | collective-permute-start | bytes 811016 | tf_op jit(solution)/shard_map/ppermute | solution.py:39
  60.2 0.4 collective-permute-done.1
  60.6 4.0 %collective-permute-start.3 = (bf16[528,256]{1,0:T(8,128)(2,1)S(1)}, bf16[528,256]{1,0:T(8,128)(2,1)S(1)}, u32[]{:S(2)}, u32[]{:S(2)}) collective-permute-start(bf16[528,256]{1,0:T(8,128)(2,1)S(1)} %collective-permute-done.1), channel_id=1, source_target_pairs={{0,14},{2,0},{4,2},{6,4},{8,6},{10,8},{12,10},{14,12},{1,15},{3,1}... | collective-permute-start | bytes 811016 | tf_op jit(solution)/shard_map/ppermute | solution.py:39
  64.6 1.0 bitcast_dynamic-update-slice_fusion.5
  65.6 2.5 %collective-permute-done.2 = bf16[528,256]{1,0:T(8,128)(2,1)S(1)} collective-permute-done((bf16[528,256]{1,0:T(8,128)(2,1)}, bf16[528,256]{1,0:T(8,128)(2,1)S(1)}, u32[]{:S(2)}, u32[]{:S(2)}) %collective-permute-start.2) | collective-permute-done | bytes 270368 | tf_op jit(solution)/shard_map/ppermute | solution.py:39
  68.1 2.6 %collective-permute-start.4 = (bf16[528,256]{1,0:T(8,128)(2,1)S(1)}, bf16[528,256]{1,0:T(8,128)(2,1)S(1)}, u32[]{:S(2)}, u32[]{:S(2)}) collective-permute-start(bf16[528,256]{1,0:T(8,128)(2,1)S(1)} %collective-permute-done.2), channel_id=1, source_target_pairs={{0,2},{2,4},{4,6},{6,8},{8,10},{10,12},{12,14},{14,0},{1,3},{3,5},... | collective-permute-start | bytes 811016 | tf_op jit(solution)/shard_map/ppermute | solution.py:39
  70.8 4.6 %collective-permute-start.5 = (bf16[528,256]{1,0:T(8,128)(2,1)S(1)}, bf16[528,256]{1,0:T(8,128)(2,1)S(1)}, u32[]{:S(2)}, u32[]{:S(2)}) collective-permute-start(bf16[528,256]{1,0:T(8,128)(2,1)S(1)} %collective-permute-done.3), channel_id=1, source_target_pairs={{0,14},{2,0},{4,2},{6,4},{8,6},{10,8},{12,10},{14,12},{1,15},{3,1}... | collective-permute-start | bytes 811016 | tf_op jit(solution)/shard_map/ppermute | solution.py:39
  75.5 2.4 %collective-permute-done.4 = bf16[528,256]{1,0:T(8,128)(2,1)S(1)} collective-permute-done((bf16[528,256]{1,0:T(8,128)(2,1)S(1)}, bf16[528,256]{1,0:T(8,128)(2,1)S(1)}, u32[]{:S(2)}, u32[]{:S(2)}) %collective-permute-start.4) | collective-permute-done | bytes 270368 | tf_op jit(solution)/shard_map/ppermute | solution.py:39
  78.0 0.7 copy-done.3
  78.6 0.8 collective-permute-done.5
  79.5 5.0 %all-gather.5.cloned.1.call-done = bf16[2112,896]{1,0:T(8,128)(2,1)} async-done(((bf16[264,896]{1,0:T(8,128)(2,1)}), bf16[2112,896]{1,0:T(8,128)(2,1)}) %all-gather.5.cloned.1.call-update) | async-done | bytes 3784720 | tf_op jit(solution)/shard_map/all_gather | solution.py:316
  84.5 2.0 collective-permute-start.7
  86.5 3.5 %collective-permute-start.6 = (bf16[528,256]{1,0:T(8,128)(2,1)}, bf16[528,256]{1,0:T(8,128)(2,1)S(1)}, u32[]{:S(2)}, u32[]{:S(2)}) collective-permute-start(bf16[528,256]{1,0:T(8,128)(2,1)} %copy-done.3), channel_id=1, source_target_pairs={{0,2},{2,4},{4,6},{6,8},{8,10},{10,12},{12,14},{14,0},{1,3},{3,5},... | collective-permute-start | bytes 811016 | tf_op jit(solution)/shard_map/ppermute | solution.py:39
  90.0 0.1 copy.44.gain_ref
  90.1 1.2 fusion.1
  91.3 3.6 %collective-permute-start.8 = (bf16[464,256]{1,0:T(8,128)(2,1)}, bf16[464,256]{1,0:T(8,128)(2,1)S(1)}, u32[]{:S(2)}, u32[]{:S(2)}) collective-permute-start(bf16[464,256]{1,0:T(8,128)(2,1)} %fusion.18), channel_id=1, source_target_pairs={{0,1},{1,0},{2,3},{3,2},{4,5},{5,4},{6,7},{7,6},{8,9},{9,8},{10,11... | collective-permute-start | bytes 712712 | tf_op jit(solution)/shard_map/ppermute | solution.py:39
  94.9 4.2 %collective-permute-done.6.far_ref = bf16[528,256]{1,0:T(8,128)(2,1)S(1)} collective-permute-done((bf16[528,256]{1,0:T(8,128)(2,1)}, bf16[528,256]{1,0:T(8,128)(2,1)S(1)}, u32[]{:S(2)}, u32[]{:S(2)}) %collective-permute-start.6) | collective-permute-done | bytes 270368 | tf_op jit(solution)/shard_map/ppermute | solution.py:39
  99.2 1.3 arrange.1
  100.5 3.1 %first_half.1.acc_ref = f32[2,256,512]{2,1,0:T(8,128)S(1)} custom-call(s32[2]{0:T(128)S(1)} %pad_add_fusion.at_ref, bf16[4,2,264,256]{3,2,1,0:T(8,128)(2,1)S(1)} %get-tuple-element.40.fp_ref, bf16[8,264,896]{2,1,0:T(8,128)(2,1)S(1)} %bitcast.68), custom_call_target="tpu_custom_call" | custom-call | flops 3875536896 | bytes 5914632 | tf_op jit(solution)/shard_map/first_half/pallas_call | solution.py:82
  103.6 5.0 %second_half.1 = (bf16[2,512,256]{2,1,0:T(8,128)(2,1)S(1)}, f32[2,512,256]{2,1,0:T(8,128)S(1)}, f32[1,256]{1,0:T(1,128)S(1)}) custom-call(s32[2]{0:T(128)S(1)} %pad_add_fusion.at_ref, bf16[4,2,264,256]{3,2,1,0:T(8,128)(2,1)S(1)} %get-tuple-element.38.fp_ref, bf16[8,264,896]{2,1,0:T(8,128)(2,1)} %collective-permute-done.7.w_ref.other_ref, ...), custom_call_target="tpu_custom_call" | custom-call | flops 3875536896 | bytes 7488520 | tf_op jit(solution)/shard_map/second_half/pallas_call | solution.py:82
  108.6 0.4 sums.1
  109.0 14.4 %all_to_all.15.stat_ref = f32[8,4,256]{2,1,0:T(4,128)S(1)} all-to-all(f32[8,4,256]{2,1,0:T(4,128)S(1)} %get-tuple-element.52), channel_id=1, replica_groups=mesh['xh'=2,'xl'=2,'zl'=4,'core'=2,'y'=8,'zh'=2] {'y'}, dimensions={0} | all-to-all | bytes 65536 | tf_op jit(solution)/shard_map/all_to_all | solution.py:371
  123.4 6.3 %backward.1 = (bf16[8,144,256]{2,1,0:T(8,128)(2,1)}, bf16[8,384,256]{2,1,0:T(8,128)(2,1)}, bf16[2,512,256]{2,1,0:T(8,128)(2,1)S(1)}) custom-call(s32[2]{0:T(128)S(1)} %pad_add_fusion.at_ref, f32[2,512,256]{2,1,0:T(8,128)S(1)} %get-tuple-element.45.slope_ref, bf16[2,512,256]{2,1,0:T(8,128)(2,1)S(1)} %get-tuple-element.46.img_ref, ...), custom_call_target="tpu_custom_call" | custom-call | flops 1937768448 | bytes 12914696 | tf_op jit(solution)/shard_map/backward/pallas_call | solution.py:82
  129.7 3.5 %all-to-all-start.2 = ((bf16[8,144,256]{2,1,0:T(8,128)(2,1)}), bf16[8,144,256]{2,1,0:T(8,128)(2,1)S(1)}, u32[]{:S(2)}, u32[]{:S(2)}) async-start(bf16[8,144,256]{2,1,0:T(8,128)(2,1)} %get-tuple-element.57), calls=%async_computation.3 | async-start | bytes 1179648 | tf_op jit(solution)/shard_map/all_to_all | solution.py:380
  133.4 3.5 %collective-permute-start.10 = (bf16[448,256]{1,0:T(8,128)(2,1)S(1)}, bf16[448,256]{1,0:T(8,128)(2,1)S(1)}, u32[]{:S(2)}, u32[]{:S(2)}) collective-permute-start(bf16[448,256]{1,0:T(8,128)(2,1)S(1)} %dynamic-slice_bitcast_fusion), channel_id=1, source_target_pairs={{0,1},{1,0},{2,3},{3,2},{4,5},{5,4},{6,7},{7,6},{8,9},{9,8},{10,11... | collective-permute-start | bytes 688136 | tf_op jit(solution)/shard_map/ppermute | solution.py:39
  136.9 6.4 %collective-permute-start.11 = (f32[512]{0:T(512)S(1)}, f32[512]{0:T(512)S(1)}, u32[]{:S(2)}, u32[]{:S(2)}) collective-permute-start(f32[512]{0:T(512)S(1)} %bitcast.88), channel_id=1, source_target_pairs={{0,1},{1,0},{2,3},{3,2},{4,5},{5,4},{6,7},{7,6},{8,9},{9,8},{10,11... | collective-permute-start | bytes 6152 | tf_op jit(solution)/shard_map/ppermute | solution.py:39
  143.3 11.7 %all-to-all-done.2 = bf16[8,144,256]{2,1,0:T(8,128)(2,1)S(1)} async-done(((bf16[8,144,256]{2,1,0:T(8,128)(2,1)}), bf16[8,144,256]{2,1,0:T(8,128)(2,1)S(1)}, u32[]{:S(2)}, u32[]{:S(2)}) %all-to-all-start.2) | async-done | bytes 589856 | tf_op jit(solution)/shard_map/all_to_all | solution.py:380
  155.1 1.9 collective-permute-start.9
  157.3 7.6 %collective-permute-done.9 = bf16[72,256]{1,0:T(8,128)(2,1)S(1)} collective-permute-done((bf16[72,256]{1,0:T(8,128)(2,1)S(1)}, bf16[72,256]{1,0:T(8,128)(2,1)S(1)}, u32[]{:S(2)}, u32[]{:S(2)}) %collective-permute-start.9) | collective-permute-done | bytes 36896 | tf_op jit(solution)/shard_map/ppermute | solution.py:39
  164.9 7.0 %reduce-scatter.2.cloned.1.call-done = bf16[384,256]{1,0:T(8,128)(2,1)} async-done(((bf16[3072,256]{1,0:T(8,128)(2,1)}), bf16[384,256]{1,0:T(8,128)(2,1)}) %reduce-scatter.2.cloned.1.call-update) | async-done | bytes 196624 | tf_op jit(solution)/shard_map/reduce_scatter | solution.py:377
  171.9 1.0 constant_dynamic-slice_fusion.1
  172.9 2.6 %collective-permute-start.12 = (bf16[192,256]{0,1:T(8,128)(2,1)S(1)}, bf16[192,256]{0,1:T(8,128)(2,1)S(1)}, u32[]{:S(2)}, u32[]{:S(2)}) collective-permute-start(bf16[192,256]{0,1:T(8,128)(2,1)S(1)} %bitcast.83), channel_id=1, source_target_pairs={{0,256},{1,257},{256,0},{257,1},{2,258},{3,259},{258,2},{259,3},{4... | collective-permute-start | bytes 294920 | tf_op jit(solution)/shard_map/ppermute | solution.py:66
  175.6 7.9 %collective-permute-start.13 = (bf16[192,256]{0,1:T(8,128)(2,1)S(1)}, bf16[192,256]{0,1:T(8,128)(2,1)S(1)}, u32[]{:S(2)}, u32[]{:S(2)}) collective-permute-start(bf16[192,256]{0,1:T(8,128)(2,1)S(1)} %bitcast.84), channel_id=1, source_target_pairs={{0,257},{1,256},{256,1},{257,0},{2,259},{3,258},{258,3},{259,2},{4... | collective-permute-start | bytes 294920 | tf_op jit(solution)/shard_map/ppermute | solution.py:66
  183.6 1.3 fusion
  185.0 0.8 copy.48
  185.8 4.5 %collective-permute-done.13 = bf16[192,256]{0,1:T(8,128)(2,1)S(1)} collective-permute-done((bf16[192,256]{0,1:T(8,128)(2,1)S(1)}, bf16[192,256]{0,1:T(8,128)(2,1)S(1)}, u32[]{:S(2)}, u32[]{:S(2)}) %collective-permute-start.13) | collective-permute-done | bytes 98336 | tf_op jit(solution)/shard_map/ppermute | solution.py:66
  190.3 0.7 pad_maximum_fusion.2
  (69 shorter events, 1.9 us)
Async XLA Ops:
  7.2 30.8 %copy-start = (bf16[512,448]{0,1:T(8,128)(2,1)S(1)}, bf16[512,448]{0,1:T(8,128)(2,1)}, u32[]{:S(2)}) copy-start(bf16[512,448]{0,1:T(8,128)(2,1)} %param.13) | copy-start | bytes 1376260
  7.2 17.7 %copy-start.5 = (bf16[8,64,72]{2,1,0:T(8,128)(2,1)S(1)}, bf16[8,64,72]{2,1,0:T(8,128)(2,1)}, u32[]{:S(2)}) copy-start(bf16[8,64,72]{2,1,0:T(8,128)(2,1)} %param.8) | copy-start | bytes 221188
  7.2 17.5 %copy-start.4 = (bf16[8,64,192]{2,1,0:T(8,128)(2,1)S(1)}, bf16[8,64,192]{2,1,0:T(8,128)(2,1)}, u32[]{:S(2)}) copy-start(bf16[8,64,192]{2,1,0:T(8,128)(2,1)} %param.9) | copy-start | bytes 589828
  7.2 77.3 %all-gather.5.cloned.1.call-start = ((), (), s32[]{:S(2)}) async-start(), calls=%async_computation.5 | async-start | bytes 4257792 | tf_op jit(solution)/shard_map/all_gather | solution.py:316
  24.7 13.0 %copy-start.6 = (f32[448]{0:T(512)S(1)}, f32[448]{0:T(512)}, u32[]{:S(2)}) copy-start(f32[448]{0:T(512)} %param.11) | copy-start | bytes 5380
  24.7 13.1 %copy-start.7 = (s32[1,8]{1,0:T(1,128)S(1)}, s32[1,8]{1,0:T(1,128)}, u32[]{:S(2)}) copy-start(s32[1,8]{1,0:T(1,128)} %param.15) | copy-start | bytes 100
  25.9 20.6 %all-to-all-start = ((bf16[4,192,256]{2,1,0:T(8,128)(2,1)}), bf16[4,192,256]{2,1,0:T(8,128)(2,1)S(1)}, u32[]{:S(2)}, u32[]{:S(2)}) async-start(bf16[4,192,256]{2,1,0:T(8,128)(2,1)} %pad_maximum_fusion), calls=%async_computation | async-start | bytes 786432 | tf_op jit(solution)/shard_map/all_to_all | solution.py:71
  37.1 134.8 %reduce-scatter.2.cloned.1.call-start = ((), (), s32[]{:S(2)}) async-start(), calls=%async_computation.4 | async-start | bytes 1769472 | tf_op jit(solution)/shard_map/reduce_scatter | solution.py:377
  47.3 10.1 %collective-permute-start = (bf16[528,256]{1,0:T(8,128)(2,1)}, bf16[528,256]{1,0:T(8,128)(2,1)}, u32[]{:S(2)}, u32[]{:S(2)}) collective-permute-start(bf16[528,256]{1,0:T(8,128)(2,1)} %pad_maximum_fusion.1), channel_id=1, source_target_pairs={{0,2},{2,4},{4,6},{6,8},{8,10},{10,12},{12,14},{14,0},{1,3},{3,5},... | collective-permute-start | bytes 811016 | tf_op jit(solution)/shard_map/ppermute | solution.py:39
  50.7 9.8 %collective-permute-start.1 = (bf16[528,256]{1,0:T(8,128)(2,1)}, bf16[528,256]{1,0:T(8,128)(2,1)S(1)}, u32[]{:S(2)}, u32[]{:S(2)}) collective-permute-start(bf16[528,256]{1,0:T(8,128)(2,1)} %pad_maximum_fusion.1), channel_id=1, source_target_pairs={{0,14},{2,0},{4,2},{6,4},{8,6},{10,8},{12,10},{14,12},{1,15},{3,1}... | collective-permute-start | bytes 811016 | tf_op jit(solution)/shard_map/ppermute | solution.py:39
  57.4 10.7 %collective-permute-start.2 = (bf16[528,256]{1,0:T(8,128)(2,1)}, bf16[528,256]{1,0:T(8,128)(2,1)S(1)}, u32[]{:S(2)}, u32[]{:S(2)}) collective-permute-start(bf16[528,256]{1,0:T(8,128)(2,1)} %collective-permute-done), channel_id=1, source_target_pairs={{0,2},{2,4},{4,6},{6,8},{8,10},{10,12},{12,14},{14,0},{1,3},{3,5},... | collective-permute-start | bytes 811016 | tf_op jit(solution)/shard_map/ppermute | solution.py:39
  60.6 10.3 %collective-permute-start.3 = (bf16[528,256]{1,0:T(8,128)(2,1)S(1)}, bf16[528,256]{1,0:T(8,128)(2,1)S(1)}, u32[]{:S(2)}, u32[]{:S(2)}) collective-permute-start(bf16[528,256]{1,0:T(8,128)(2,1)S(1)} %collective-permute-done.1), channel_id=1, source_target_pairs={{0,14},{2,0},{4,2},{6,4},{8,6},{10,8},{12,10},{14,12},{1,15},{3,1}... | collective-permute-start | bytes 811016 | tf_op jit(solution)/shard_map/ppermute | solution.py:39
  68.1 9.8 %collective-permute-start.4 = (bf16[528,256]{1,0:T(8,128)(2,1)S(1)}, bf16[528,256]{1,0:T(8,128)(2,1)S(1)}, u32[]{:S(2)}, u32[]{:S(2)}) collective-permute-start(bf16[528,256]{1,0:T(8,128)(2,1)S(1)} %collective-permute-done.2), channel_id=1, source_target_pairs={{0,2},{2,4},{4,6},{6,8},{8,10},{10,12},{12,14},{14,0},{1,3},{3,5},... | collective-permute-start | bytes 811016 | tf_op jit(solution)/shard_map/ppermute | solution.py:39
  70.8 8.6 %collective-permute-start.5 = (bf16[528,256]{1,0:T(8,128)(2,1)S(1)}, bf16[528,256]{1,0:T(8,128)(2,1)S(1)}, u32[]{:S(2)}, u32[]{:S(2)}) collective-permute-start(bf16[528,256]{1,0:T(8,128)(2,1)S(1)} %collective-permute-done.3), channel_id=1, source_target_pairs={{0,14},{2,0},{4,2},{6,4},{8,6},{10,8},{12,10},{14,12},{1,15},{3,1}... | collective-permute-start | bytes 811016 | tf_op jit(solution)/shard_map/ppermute | solution.py:39
  77.9 0.7 copy-start.3
  84.5 19.1 %collective-permute-start.7 = (bf16[8,264,896]{2,1,0:T(8,128)(2,1)}, bf16[8,264,896]{2,1,0:T(8,128)(2,1)}, u32[]{:S(2)}, u32[]{:S(2)}) collective-permute-start(bf16[8,264,896]{2,1,0:T(8,128)(2,1)} %bitcast.67), channel_id=1, source_target_pairs={{0,16},{16,0},{1,17},{17,1},{2,18},{18,2},{3,19},{19,3},{4,20},{20... | collective-permute-start | bytes 11354120 | tf_op jit(solution)/shard_map/ppermute | solution.py:39
  86.5 12.7 %collective-permute-start.6 = (bf16[528,256]{1,0:T(8,128)(2,1)}, bf16[528,256]{1,0:T(8,128)(2,1)S(1)}, u32[]{:S(2)}, u32[]{:S(2)}) collective-permute-start(bf16[528,256]{1,0:T(8,128)(2,1)} %copy-done.3), channel_id=1, source_target_pairs={{0,2},{2,4},{4,6},{6,8},{8,10},{10,12},{12,14},{14,0},{1,3},{3,5},... | collective-permute-start | bytes 811016 | tf_op jit(solution)/shard_map/ppermute | solution.py:39
  91.3 9.2 %copy-start.1 = (bf16[2112,896]{1,0:T(8,128)(2,1)S(1)}, bf16[2112,896]{1,0:T(8,128)(2,1)}, u32[]{:S(2)}) copy-start(bf16[2112,896]{1,0:T(8,128)(2,1)} %all-gather.5.cloned.1.call-done) | copy-start | bytes 11354116
  91.3 17.3 %collective-permute-start.8 = (bf16[464,256]{1,0:T(8,128)(2,1)}, bf16[464,256]{1,0:T(8,128)(2,1)S(1)}, u32[]{:S(2)}, u32[]{:S(2)}) collective-permute-start(bf16[464,256]{1,0:T(8,128)(2,1)} %fusion.18), channel_id=1, source_target_pairs={{0,1},{1,0},{2,3},{3,2},{4,5},{5,4},{6,7},{7,6},{8,9},{9,8},{10,11... | collective-permute-start | bytes 712712 | tf_op jit(solution)/shard_map/ppermute | solution.py:39
  129.7 25.3 %all-to-all-start.2 = ((bf16[8,144,256]{2,1,0:T(8,128)(2,1)}), bf16[8,144,256]{2,1,0:T(8,128)(2,1)S(1)}, u32[]{:S(2)}, u32[]{:S(2)}) async-start(bf16[8,144,256]{2,1,0:T(8,128)(2,1)} %get-tuple-element.57), calls=%async_computation.3 | async-start | bytes 1179648 | tf_op jit(solution)/shard_map/all_to_all | solution.py:380
  133.3 50.4 %copy-start.2 = (bf16[512,448]{0,1:T(8,128)(2,1)S(1)}, bf16[512,448]{0,1:T(8,128)(2,1)}, u32[]{:S(2)}) copy-start(bf16[512,448]{0,1:T(8,128)(2,1)} %param.12) | copy-start | bytes 1376260
  133.4 23.9 %collective-permute-start.10 = (bf16[448,256]{1,0:T(8,128)(2,1)S(1)}, bf16[448,256]{1,0:T(8,128)(2,1)S(1)}, u32[]{:S(2)}, u32[]{:S(2)}) collective-permute-start(bf16[448,256]{1,0:T(8,128)(2,1)S(1)} %dynamic-slice_bitcast_fusion), channel_id=1, source_target_pairs={{0,1},{1,0},{2,3},{3,2},{4,5},{5,4},{6,7},{7,6},{8,9},{9,8},{10,11... | collective-permute-start | bytes 688136 | tf_op jit(solution)/shard_map/ppermute | solution.py:39
  136.9 20.4 %collective-permute-start.11 = (f32[512]{0:T(512)S(1)}, f32[512]{0:T(512)S(1)}, u32[]{:S(2)}, u32[]{:S(2)}) collective-permute-start(f32[512]{0:T(512)S(1)} %bitcast.88), channel_id=1, source_target_pairs={{0,1},{1,0},{2,3},{3,2},{4,5},{5,4},{6,7},{7,6},{8,9},{9,8},{10,11... | collective-permute-start | bytes 6152 | tf_op jit(solution)/shard_map/ppermute | solution.py:39
  155.1 9.8 %collective-permute-start.9 = (bf16[72,256]{1,0:T(8,128)(2,1)S(1)}, bf16[72,256]{1,0:T(8,128)(2,1)S(1)}, u32[]{:S(2)}, u32[]{:S(2)}) collective-permute-start(bf16[72,256]{1,0:T(8,128)(2,1)S(1)} %dynamic-slice_bitcast_fusion.3), channel_id=1, source_target_pairs={{0,1},{1,0},{2,3},{3,2},{4,5},{5,4},{6,7},{7,6},{8,9},{9,8},{10,11... | collective-permute-start | bytes 110600 | tf_op jit(solution)/shard_map/ppermute | solution.py:39
  172.9 12.8 %collective-permute-start.12 = (bf16[192,256]{0,1:T(8,128)(2,1)S(1)}, bf16[192,256]{0,1:T(8,128)(2,1)S(1)}, u32[]{:S(2)}, u32[]{:S(2)}) collective-permute-start(bf16[192,256]{0,1:T(8,128)(2,1)S(1)} %bitcast.83), channel_id=1, source_target_pairs={{0,256},{1,257},{256,0},{257,1},{2,258},{3,259},{258,2},{259,3},{4... | collective-permute-start | bytes 294920 | tf_op jit(solution)/shard_map/ppermute | solution.py:66
  175.6 14.7 %collective-permute-start.13 = (bf16[192,256]{0,1:T(8,128)(2,1)S(1)}, bf16[192,256]{0,1:T(8,128)(2,1)S(1)}, u32[]{:S(2)}, u32[]{:S(2)}) collective-permute-start(bf16[192,256]{0,1:T(8,128)(2,1)S(1)} %bitcast.84), channel_id=1, source_target_pairs={{0,257},{1,256},{256,1},{257,0},{2,259},{3,258},{258,3},{259,2},{4... | collective-permute-start | bytes 294920 | tf_op jit(solution)/shard_map/ppermute | solution.py:66
Sparse Core Ops, SparseCore 0:
  24.8 59.6 all-gather.4
  129.8 41.9 reduce-scatter.1

commit v7 on v6

--- a/solution.py
+++ b/solution.py
@@ -353,9 +353,7 @@
     give = jnp.concatenate([half_of(grad_slots, 1 - zh), jnp.pad(terms, ((0, 10), (0, 0)))])
     keep = half_of(grad_slots, zh)
 
-    mine, feats, right, give, keep = lax.optimization_barrier(
-        (mine, feats, right, give, keep)
-    )
+    mine, _, _, give, keep = lax.optimization_barrier((mine, feats, right, give, keep))
     other = shift(mine, "core", 1)
     fp_mine, fp_other = arrange(at, feats, shift(right, "y", 1))
     got = shift(give, "zh", 1)

time: 201 us -> 207 us (1.030)
  the two profiles are of different devices: /device:TPU:6 before, /device:TPU:128 now
where the time goes in v7:
time: 207 us; the launch traced here: 206 us
  starting transfers between devices  67.3 us (33%)
  waiting for transfers between devices  66.4 us (32%)
  blocking collectives  27.9 us (13%)
  Pallas kernels  17.6 us (9%)
  between operations  15.3 us (7%)
  local copies, waits for them, and re-layouts  4.74 us (2%)
  other arithmetic  4.63 us (2%)
    ppermute x12, starting transfers between devices, shift(): return lax.ppermute(x, axis, [(i, (i + by) % n) for i in range(n)])  44.4 us
    ppermute x12, waiting for transfers between devices, shift(): return lax.ppermute(x, axis, [(i, (i + by) % n) for i in range(n)])  27.5 us
    pallas_call x6, Pallas kernels, call(): pl.pallas_call(kernel, in_specs=[SMEM] + [VMEM] * (len(args) - 1), out_sp...  17.6 us
    all_to_all x1, blocking collectives, per_device(): stat = lax.all_to_all(stat, 'y', 0, 0, tiled=True)  14.4 us
    all_gather x1, blocking collectives, per_device(): w_x = lax.all_gather(weight, ('xh', 'xl'), axis=0)  13.5 us
    all_to_all x1, waiting for transfers between devices, exchange(): lax.all_to_all(blocks, ('xh', 'zh'), split_axis=0, concat_axis=0, tiled=T...  13.5 us
    all_to_all x1, waiting for transfers between devices, per_device(): sig_g = lax.all_to_all(sig_p, 'y', 0, 0, tiled=True)  10.7 us
    ppermute x2, starting transfers between devices, swap(): return lax.ppermute(x, ('xh', 'zh'), pairs)  9.86 us
  transfers between devices with their start and end apart: 18, of which 11 were waited for; matrix products, arithmetic and copies ran while one was open for 4% of the time, Pallas kernels for 5%

profile of v7, /device:TPU:128, one launch (start us, length us, event | category | flops | bytes accessed | tf_op | source)
XLA Modules:
  0.0 205.9 jit_solution(14207152375722083539)
XLA Ops:
  7.3 13.5 %all-gather.2.w_ref = bf16[4,132,448]{2,1,0:T(8,128)(2,1)S(1)} all-gather(bf16[1,132,448]{2,1,0:T(8,128)(2,1)} %bitcast.82), channel_id=2, replica_groups=mesh['xh'=2,'xl'=2,'zl'=4,'core'=2,'y'=8,'zh'=2] {'xh','xl'}, dimensions={0}, use_global_device_ids=true | all-gather | bytes 591360 | tf_op jit(solution)/shard_map/all_gather | solution.py:314
  20.9 1.5 side_by_side.1
  22.8 0.8 pad_maximum_fusion
  23.5 9.4 %all-to-all-start = ((bf16[4,192,256]{2,1,0:T(8,128)(2,1)}), bf16[4,192,256]{2,1,0:T(8,128)(2,1)S(1)}, u32[]{:S(2)}, u32[]{:S(2)}) async-start(bf16[4,192,256]{2,1,0:T(8,128)(2,1)} %pad_maximum_fusion), calls=%async_computation | async-start | bytes 786432 | tf_op jit(solution)/shard_map/all_to_all | solution.py:71
  33.8 0.6 convolution_convert_fusion.1
  34.5 13.5 %all-to-all-done = bf16[4,192,256]{2,1,0:T(8,128)(2,1)S(1)} async-done(((bf16[4,192,256]{2,1,0:T(8,128)(2,1)}), bf16[4,192,256]{2,1,0:T(8,128)(2,1)S(1)}, u32[]{:S(2)}, u32[]{:S(2)}) %all-to-all-start) | async-done | bytes 393248 | tf_op jit(solution)/shard_map/all_to_all | solution.py:71
  48.1 0.7 pad_maximum_fusion.1
  48.8 3.6 %collective-permute-start = (bf16[528,256]{1,0:T(8,128)(2,1)}, bf16[528,256]{1,0:T(8,128)(2,1)}, u32[]{:S(2)}, u32[]{:S(2)}) collective-permute-start(bf16[528,256]{1,0:T(8,128)(2,1)} %pad_maximum_fusion.1), channel_id=1, source_target_pairs={{0,2},{2,4},{4,6},{6,8},{8,10},{10,12},{12,14},{14,0},{1,3},{3,5},... | collective-permute-start | bytes 811016 | tf_op jit(solution)/shard_map/ppermute | solution.py:39
  52.4 4.4 %collective-permute-start.1 = (bf16[528,256]{1,0:T(8,128)(2,1)}, bf16[528,256]{1,0:T(8,128)(2,1)S(1)}, u32[]{:S(2)}, u32[]{:S(2)}) collective-permute-start(bf16[528,256]{1,0:T(8,128)(2,1)} %pad_maximum_fusion.1), channel_id=1, source_target_pairs={{0,14},{2,0},{4,2},{6,4},{8,6},{10,8},{12,10},{14,12},{1,15},{3,1}... | collective-permute-start | bytes 811016 | tf_op jit(solution)/shard_map/ppermute | solution.py:39
  56.9 0.7 fusion.18
  57.6 0.1 broadcast_in_dim.59
  57.8 1.8 collective-permute-done
  59.5 1.9 collective-permute-start.2
  61.5 5.1 %collective-permute-start.3 = (bf16[528,256]{1,0:T(8,128)(2,1)S(1)}, bf16[528,256]{1,0:T(8,128)(2,1)S(1)}, u32[]{:S(2)}, u32[]{:S(2)}) collective-permute-start(bf16[528,256]{1,0:T(8,128)(2,1)S(1)} %collective-permute-done.1), channel_id=1, source_target_pairs={{0,14},{2,0},{4,2},{6,4},{8,6},{10,8},{12,10},{14,12},{1,15},{3,1}... | collective-permute-start | bytes 811016 | tf_op jit(solution)/shard_map/ppermute | solution.py:39
  66.6 1.0 bitcast_dynamic-update-slice_fusion.5
  67.6 1.7 collective-permute-done.2
  69.3 1.9 collective-permute-start.4
  71.2 5.1 %collective-permute-start.5 = (bf16[528,256]{1,0:T(8,128)(2,1)S(1)}, bf16[528,256]{1,0:T(8,128)(2,1)S(1)}, u32[]{:S(2)}, u32[]{:S(2)}) collective-permute-start(bf16[528,256]{1,0:T(8,128)(2,1)S(1)} %collective-permute-done.3), channel_id=1, source_target_pairs={{0,14},{2,0},{4,2},{6,4},{8,6},{10,8},{12,10},{14,12},{1,15},{3,1}... | collective-permute-start | bytes 811016 | tf_op jit(solution)/shard_map/ppermute | solution.py:39
  76.4 2.4 %collective-permute-done.4 = bf16[528,256]{1,0:T(8,128)(2,1)S(1)} collective-permute-done((bf16[528,256]{1,0:T(8,128)(2,1)S(1)}, bf16[528,256]{1,0:T(8,128)(2,1)S(1)}, u32[]{:S(2)}, u32[]{:S(2)}) %collective-permute-start.4) | collective-permute-done | bytes 270368 | tf_op jit(solution)/shard_map/ppermute | solution.py:39
  78.9 0.7 copy-done.3
  79.6 0.8 collective-permute-done.5
  80.4 1.9 collective-permute-start.7
  82.3 3.0 %collective-permute-start.6 = (bf16[528,256]{1,0:T(8,128)(2,1)}, bf16[528,256]{1,0:T(8,128)(2,1)S(1)}, u32[]{:S(2)}, u32[]{:S(2)}) collective-permute-start(bf16[528,256]{1,0:T(8,128)(2,1)} %copy-done.3), channel_id=1, source_target_pairs={{0,2},{2,4},{4,6},{6,8},{8,10},{10,12},{12,14},{14,0},{1,3},{3,5},... | collective-permute-start | bytes 811016 | tf_op jit(solution)/shard_map/ppermute | solution.py:39
  85.4 0.1 copy.44.gain_ref
  85.5 1.2 fusion.1
  86.7 8.6 %collective-permute-done.6.far_ref = bf16[528,256]{1,0:T(8,128)(2,1)S(1)} collective-permute-done((bf16[528,256]{1,0:T(8,128)(2,1)}, bf16[528,256]{1,0:T(8,128)(2,1)S(1)}, u32[]{:S(2)}, u32[]{:S(2)}) %collective-permute-start.6) | collective-permute-done | bytes 270368 | tf_op jit(solution)/shard_map/ppermute | solution.py:39
  95.3 1.3 arrange.1
  96.6 4.2 %collective-permute-start.8 = (bf16[464,256]{1,0:T(8,128)(2,1)S(1)}, bf16[464,256]{1,0:T(8,128)(2,1)S(1)}, u32[]{:S(2)}, u32[]{:S(2)}) collective-permute-start(bf16[464,256]{1,0:T(8,128)(2,1)S(1)} %copy-done.5), channel_id=1, source_target_pairs={{0,1},{1,0},{2,3},{3,2},{4,5},{5,4},{6,7},{7,6},{8,9},{9,8},{10,11... | collective-permute-start | bytes 712712 | tf_op jit(solution)/shard_map/ppermute | solution.py:39
  100.8 3.1 %first_half.1.acc_ref = f32[2,256,512]{2,1,0:T(8,128)S(1)} custom-call(s32[2]{0:T(128)S(1)} %pad_add_fusion.at_ref, bf16[4,2,264,256]{3,2,1,0:T(8,128)(2,1)S(1)} %get-tuple-element.36.fp_ref, bf16[8,264,896]{2,1,0:T(8,128)(2,1)S(1)} %bitcast.68), custom_call_target="tpu_custom_call" | custom-call | flops 3875536896 | bytes 5914632 | tf_op jit(solution)/shard_map/first_half/pallas_call | solution.py:82
  103.9 5.0 %second_half.1 = (bf16[2,512,256]{2,1,0:T(8,128)(2,1)S(1)}, f32[2,512,256]{2,1,0:T(8,128)S(1)}, f32[1,256]{1,0:T(1,128)S(1)}) custom-call(s32[2]{0:T(128)S(1)} %pad_add_fusion.at_ref, bf16[4,2,264,256]{3,2,1,0:T(8,128)(2,1)S(1)} %get-tuple-element.33.fp_ref, bf16[8,264,896]{2,1,0:T(8,128)(2,1)} %collective-permute-done.7.w_ref.other_ref, ...), custom_call_target="tpu_custom_call" | custom-call | flops 3875536896 | bytes 7488520 | tf_op jit(solution)/shard_map/second_half/pallas_call | solution.py:82
  108.9 6.2 %collective-permute-done.8.got_ref = bf16[464,256]{1,0:T(8,128)(2,1)S(1)} collective-permute-done((bf16[464,256]{1,0:T(8,128)(2,1)S(1)}, bf16[464,256]{1,0:T(8,128)(2,1)S(1)}, u32[]{:S(2)}, u32[]{:S(2)}) %collective-permute-start.8) | collective-permute-done | bytes 237600 | tf_op jit(solution)/shard_map/ppermute | solution.py:39
  115.1 0.4 sums.1
  115.5 14.4 %all_to_all.15.stat_ref = f32[8,4,256]{2,1,0:T(4,128)S(1)} all-to-all(f32[8,4,256]{2,1,0:T(4,128)S(1)} %get-tuple-element.48), channel_id=1, replica_groups=mesh['xh'=2,'xl'=2,'zl'=4,'core'=2,'y'=8,'zh'=2] {'y'}, dimensions={0} | all-to-all | bytes 65536 | tf_op jit(solution)/shard_map/all_to_all | solution.py:369
  129.9 6.3 %backward.1 = (bf16[8,144,256]{2,1,0:T(8,128)(2,1)}, bf16[8,384,256]{2,1,0:T(8,128)(2,1)}, bf16[2,512,256]{2,1,0:T(8,128)(2,1)S(1)}) custom-call(s32[2]{0:T(128)S(1)} %pad_add_fusion.at_ref, f32[2,512,256]{2,1,0:T(8,128)S(1)} %get-tuple-element.41.slope_ref, bf16[2,512,256]{2,1,0:T(8,128)(2,1)S(1)} %get-tuple-element.42.img_ref, ...), custom_call_target="tpu_custom_call" | custom-call | flops 1937768448 | bytes 12914696 | tf_op jit(solution)/shard_map/backward/pallas_call | solution.py:82
  136.2 3.5 %all-to-all-start.2 = ((bf16[8,144,256]{2,1,0:T(8,128)(2,1)}), bf16[8,144,256]{2,1,0:T(8,128)(2,1)S(1)}, u32[]{:S(2)}, u32[]{:S(2)}) async-start(bf16[8,144,256]{2,1,0:T(8,128)(2,1)} %get-tuple-element.53), calls=%async_computation.3 | async-start | bytes 1179648 | tf_op jit(solution)/shard_map/all_to_all | solution.py:378
  139.9 4.0 %collective-permute-start.10 = (bf16[448,256]{1,0:T(8,128)(2,1)S(1)}, bf16[448,256]{1,0:T(8,128)(2,1)S(1)}, u32[]{:S(2)}, u32[]{:S(2)}) collective-permute-start(bf16[448,256]{1,0:T(8,128)(2,1)S(1)} %dynamic-slice_bitcast_fusion), channel_id=1, source_target_pairs={{0,1},{1,0},{2,3},{3,2},{4,5},{5,4},{6,7},{7,6},{8,9},{9,8},{10,11... | collective-permute-start | bytes 688136 | tf_op jit(solution)/shard_map/ppermute | solution.py:39
  143.9 5.9 %collective-permute-start.11 = (f32[512]{0:T(512)S(1)}, f32[512]{0:T(512)S(1)}, u32[]{:S(2)}, u32[]{:S(2)}) collective-permute-start(f32[512]{0:T(512)S(1)} %bitcast.88), channel_id=1, source_target_pairs={{0,1},{1,0},{2,3},{3,2},{4,5},{5,4},{6,7},{7,6},{8,9},{9,8},{10,11... | collective-permute-start | bytes 6152 | tf_op jit(solution)/shard_map/ppermute | solution.py:39
  149.8 10.7 %all-to-all-done.2 = bf16[8,144,256]{2,1,0:T(8,128)(2,1)S(1)} async-done(((bf16[8,144,256]{2,1,0:T(8,128)(2,1)}), bf16[8,144,256]{2,1,0:T(8,128)(2,1)S(1)}, u32[]{:S(2)}, u32[]{:S(2)}) %all-to-all-start.2) | async-done | bytes 589856 | tf_op jit(solution)/shard_map/all_to_all | solution.py:378
  160.6 3.4 %collective-permute-start.9 = (bf16[72,256]{1,0:T(8,128)(2,1)S(1)}, bf16[72,256]{1,0:T(8,128)(2,1)S(1)}, u32[]{:S(2)}, u32[]{:S(2)}) collective-permute-start(bf16[72,256]{1,0:T(8,128)(2,1)S(1)} %dynamic-slice_bitcast_fusion.3), channel_id=1, source_target_pairs={{0,1},{1,0},{2,3},{3,2},{4,5},{5,4},{6,7},{7,6},{8,9},{9,8},{10,11... | collective-permute-start | bytes 110600 | tf_op jit(solution)/shard_map/ppermute | solution.py:39
  164.3 6.1 %collective-permute-done.9 = bf16[72,256]{1,0:T(8,128)(2,1)S(1)} collective-permute-done((bf16[72,256]{1,0:T(8,128)(2,1)S(1)}, bf16[72,256]{1,0:T(8,128)(2,1)S(1)}, u32[]{:S(2)}, u32[]{:S(2)}) %collective-permute-start.9) | collective-permute-done | bytes 36896 | tf_op jit(solution)/shard_map/ppermute | solution.py:39
  170.4 6.6 %reduce-scatter.2.cloned.1.call-done = bf16[384,256]{1,0:T(8,128)(2,1)} async-done(((bf16[3072,256]{1,0:T(8,128)(2,1)}), bf16[384,256]{1,0:T(8,128)(2,1)}) %reduce-scatter.2.cloned.1.call-update) | async-done | bytes 196624 | tf_op jit(solution)/shard_map/reduce_scatter | solution.py:375
  176.9 1.0 constant_dynamic-slice_fusion.1
  178.0 6.1 %collective-permute-start.12 = (bf16[192,256]{0,1:T(8,128)(2,1)S(1)}, bf16[192,256]{0,1:T(8,128)(2,1)S(1)}, u32[]{:S(2)}, u32[]{:S(2)}) collective-permute-start(bf16[192,256]{0,1:T(8,128)(2,1)S(1)} %bitcast.83), channel_id=1, source_target_pairs={{0,256},{1,257},{256,0},{257,1},{2,258},{3,259},{258,2},{259,3},{4... | collective-permute-start | bytes 294920 | tf_op jit(solution)/shard_map/ppermute | solution.py:66
  184.2 3.7 %collective-permute-start.13 = (bf16[192,256]{0,1:T(8,128)(2,1)S(1)}, bf16[192,256]{0,1:T(8,128)(2,1)S(1)}, u32[]{:S(2)}, u32[]{:S(2)}) collective-permute-start(bf16[192,256]{0,1:T(8,128)(2,1)S(1)} %bitcast.84), channel_id=1, source_target_pairs={{0,257},{1,256},{256,1},{257,0},{2,259},{3,258},{258,3},{259,2},{4... | collective-permute-start | bytes 294920 | tf_op jit(solution)/shard_map/ppermute | solution.py:66
  188.0 1.3 fusion
  189.4 0.8 copy.48
  190.2 8.2 %collective-permute-done.13 = bf16[192,256]{0,1:T(8,128)(2,1)S(1)} collective-permute-done((bf16[192,256]{0,1:T(8,128)(2,1)S(1)}, bf16[192,256]{0,1:T(8,128)(2,1)S(1)}, u32[]{:S(2)}, u32[]{:S(2)}) %collective-permute-start.13) | collective-permute-done | bytes 98336 | tf_op jit(solution)/shard_map/ppermute | solution.py:66
  198.3 0.7 pad_maximum_fusion.2
  (71 shorter events, 1.7 us)
Async XLA Ops:
  7.2 26.6 %copy-start = (bf16[512,448]{0,1:T(8,128)(2,1)S(1)}, bf16[512,448]{0,1:T(8,128)(2,1)}, u32[]{:S(2)}) copy-start(bf16[512,448]{0,1:T(8,128)(2,1)} %param.13) | copy-start | bytes 1376260
  7.2 15.4 %copy-start.6 = (bf16[8,64,72]{2,1,0:T(8,128)(2,1)S(1)}, bf16[8,64,72]{2,1,0:T(8,128)(2,1)}, u32[]{:S(2)}) copy-start(bf16[8,64,72]{2,1,0:T(8,128)(2,1)} %param.8) | copy-start | bytes 221188
  7.2 15.2 %copy-start.4 = (bf16[8,64,192]{2,1,0:T(8,128)(2,1)S(1)}, bf16[8,64,192]{2,1,0:T(8,128)(2,1)}, u32[]{:S(2)}) copy-start(bf16[8,64,192]{2,1,0:T(8,128)(2,1)} %param.9) | copy-start | bytes 589828
  7.2 73.2 %all-gather.5.cloned.1.call-start = ((), (), s32[]{:S(2)}) async-start(), calls=%async_computation.5 | async-start | bytes 4257792 | tf_op jit(solution)/shard_map/all_gather | solution.py:316
  22.4 11.2 %copy-start.7 = (f32[448]{0:T(512)S(1)}, f32[448]{0:T(512)}, u32[]{:S(2)}) copy-start(f32[448]{0:T(512)} %param.11) | copy-start | bytes 5380
  22.4 11.2 %copy-start.8 = (s32[1,8]{1,0:T(1,128)S(1)}, s32[1,8]{1,0:T(1,128)}, u32[]{:S(2)}) copy-start(s32[1,8]{1,0:T(1,128)} %param.15) | copy-start | bytes 100
  23.5 24.5 %all-to-all-start = ((bf16[4,192,256]{2,1,0:T(8,128)(2,1)}), bf16[4,192,256]{2,1,0:T(8,128)(2,1)S(1)}, u32[]{:S(2)}, u32[]{:S(2)}) async-start(bf16[4,192,256]{2,1,0:T(8,128)(2,1)} %pad_maximum_fusion), calls=%async_computation | async-start | bytes 786432 | tf_op jit(solution)/shard_map/all_to_all | solution.py:71
  32.9 144.0 %reduce-scatter.2.cloned.1.call-start = ((), (), s32[]{:S(2)}) async-start(), calls=%async_computation.4 | async-start | bytes 1769472 | tf_op jit(solution)/shard_map/reduce_scatter | solution.py:375
  48.8 10.8 %collective-permute-start = (bf16[528,256]{1,0:T(8,128)(2,1)}, bf16[528,256]{1,0:T(8,128)(2,1)}, u32[]{:S(2)}, u32[]{:S(2)}) collective-permute-start(bf16[528,256]{1,0:T(8,128)(2,1)} %pad_maximum_fusion.1), channel_id=1, source_target_pairs={{0,2},{2,4},{4,6},{6,8},{8,10},{10,12},{12,14},{14,0},{1,3},{3,5},... | collective-permute-start | bytes 811016 | tf_op jit(solution)/shard_map/ppermute | solution.py:39
  52.4 9.1 %collective-permute-start.1 = (bf16[528,256]{1,0:T(8,128)(2,1)}, bf16[528,256]{1,0:T(8,128)(2,1)S(1)}, u32[]{:S(2)}, u32[]{:S(2)}) collective-permute-start(bf16[528,256]{1,0:T(8,128)(2,1)} %pad_maximum_fusion.1), channel_id=1, source_target_pairs={{0,14},{2,0},{4,2},{6,4},{8,6},{10,8},{12,10},{14,12},{1,15},{3,1}... | collective-permute-start | bytes 811016 | tf_op jit(solution)/shard_map/ppermute | solution.py:39
  59.5 9.8 %collective-permute-start.2 = (bf16[528,256]{1,0:T(8,128)(2,1)}, bf16[528,256]{1,0:T(8,128)(2,1)S(1)}, u32[]{:S(2)}, u32[]{:S(2)}) collective-permute-start(bf16[528,256]{1,0:T(8,128)(2,1)} %collective-permute-done), channel_id=1, source_target_pairs={{0,2},{2,4},{4,6},{6,8},{8,10},{10,12},{12,14},{14,0},{1,3},{3,5},... | collective-permute-start | bytes 811016 | tf_op jit(solution)/shard_map/ppermute | solution.py:39
  61.5 9.8 %collective-permute-start.3 = (bf16[528,256]{1,0:T(8,128)(2,1)S(1)}, bf16[528,256]{1,0:T(8,128)(2,1)S(1)}, u32[]{:S(2)}, u32[]{:S(2)}) collective-permute-start(bf16[528,256]{1,0:T(8,128)(2,1)S(1)} %collective-permute-done.1), channel_id=1, source_target_pairs={{0,14},{2,0},{4,2},{6,4},{8,6},{10,8},{12,10},{14,12},{1,15},{3,1}... | collective-permute-start | bytes 811016 | tf_op jit(solution)/shard_map/ppermute | solution.py:39
  69.3 9.6 %collective-permute-start.4 = (bf16[528,256]{1,0:T(8,128)(2,1)S(1)}, bf16[528,256]{1,0:T(8,128)(2,1)S(1)}, u32[]{:S(2)}, u32[]{:S(2)}) collective-permute-start(bf16[528,256]{1,0:T(8,128)(2,1)S(1)} %collective-permute-done.2), channel_id=1, source_target_pairs={{0,2},{2,4},{4,6},{6,8},{8,10},{10,12},{12,14},{14,0},{1,3},{3,5},... | collective-permute-start | bytes 811016 | tf_op jit(solution)/shard_map/ppermute | solution.py:39
  71.2 9.1 %collective-permute-start.5 = (bf16[528,256]{1,0:T(8,128)(2,1)S(1)}, bf16[528,256]{1,0:T(8,128)(2,1)S(1)}, u32[]{:S(2)}, u32[]{:S(2)}) collective-permute-start(bf16[528,256]{1,0:T(8,128)(2,1)S(1)} %collective-permute-done.3), channel_id=1, source_target_pairs={{0,14},{2,0},{4,2},{6,4},{8,6},{10,8},{12,10},{14,12},{1,15},{3,1}... | collective-permute-start | bytes 811016 | tf_op jit(solution)/shard_map/ppermute | solution.py:39
  78.9 0.7 copy-start.3
  80.4 23.5 %collective-permute-start.7 = (bf16[8,264,896]{2,1,0:T(8,128)(2,1)}, bf16[8,264,896]{2,1,0:T(8,128)(2,1)}, u32[]{:S(2)}, u32[]{:S(2)}) collective-permute-start(bf16[8,264,896]{2,1,0:T(8,128)(2,1)} %bitcast.67), channel_id=1, source_target_pairs={{0,16},{16,0},{1,17},{17,1},{2,18},{18,2},{3,19},{19,3},{4,20},{20... | collective-permute-start | bytes 11354120 | tf_op jit(solution)/shard_map/ppermute | solution.py:39
  82.3 12.9 %collective-permute-start.6 = (bf16[528,256]{1,0:T(8,128)(2,1)}, bf16[528,256]{1,0:T(8,128)(2,1)S(1)}, u32[]{:S(2)}, u32[]{:S(2)}) collective-permute-start(bf16[528,256]{1,0:T(8,128)(2,1)} %copy-done.3), channel_id=1, source_target_pairs={{0,2},{2,4},{4,6},{6,8},{8,10},{10,12},{12,14},{14,0},{1,3},{3,5},... | collective-permute-start | bytes 811016 | tf_op jit(solution)/shard_map/ppermute | solution.py:39
  86.7 9.9 %copy-start.5 = (bf16[464,256]{1,0:T(8,128)(2,1)S(1)}, bf16[464,256]{1,0:T(8,128)(2,1)}, u32[]{:S(2)}) copy-start(bf16[464,256]{1,0:T(8,128)(2,1)} %fusion.18) | copy-start | bytes 712708
  86.7 14.1 %copy-start.1 = (bf16[2112,896]{1,0:T(8,128)(2,1)S(1)}, bf16[2112,896]{1,0:T(8,128)(2,1)}, u32[]{:S(2)}) copy-start(bf16[2112,896]{1,0:T(8,128)(2,1)} %all-gather.5.cloned.1.call-done) | copy-start | bytes 11354116
  96.6 18.5 %collective-permute-start.8 = (bf16[464,256]{1,0:T(8,128)(2,1)S(1)}, bf16[464,256]{1,0:T(8,128)(2,1)S(1)}, u32[]{:S(2)}, u32[]{:S(2)}) collective-permute-start(bf16[464,256]{1,0:T(8,128)(2,1)S(1)} %copy-done.5), channel_id=1, source_target_pairs={{0,1},{1,0},{2,3},{3,2},{4,5},{5,4},{6,7},{7,6},{8,9},{9,8},{10,11... | collective-permute-start | bytes 712712 | tf_op jit(solution)/shard_map/ppermute | solution.py:39
  136.2 24.2 %all-to-all-start.2 = ((bf16[8,144,256]{2,1,0:T(8,128)(2,1)}), bf16[8,144,256]{2,1,0:T(8,128)(2,1)S(1)}, u32[]{:S(2)}, u32[]{:S(2)}) async-start(bf16[8,144,256]{2,1,0:T(8,128)(2,1)} %get-tuple-element.53), calls=%async_computation.3 | async-start | bytes 1179648 | tf_op jit(solution)/shard_map/all_to_all | solution.py:378
  139.8 48.2 %copy-start.2 = (bf16[512,448]{0,1:T(8,128)(2,1)S(1)}, bf16[512,448]{0,1:T(8,128)(2,1)}, u32[]{:S(2)}) copy-start(bf16[512,448]{0,1:T(8,128)(2,1)} %param.12) | copy-start | bytes 1376260
  139.9 24.4 %collective-permute-start.10 = (bf16[448,256]{1,0:T(8,128)(2,1)S(1)}, bf16[448,256]{1,0:T(8,128)(2,1)S(1)}, u32[]{:S(2)}, u32[]{:S(2)}) collective-permute-start(bf16[448,256]{1,0:T(8,128)(2,1)S(1)} %dynamic-slice_bitcast_fusion), channel_id=1, source_target_pairs={{0,1},{1,0},{2,3},{3,2},{4,5},{5,4},{6,7},{7,6},{8,9},{9,8},{10,11... | collective-permute-start | bytes 688136 | tf_op jit(solution)/shard_map/ppermute | solution.py:39
  143.9 20.4 %collective-permute-start.11 = (f32[512]{0:T(512)S(1)}, f32[512]{0:T(512)S(1)}, u32[]{:S(2)}, u32[]{:S(2)}) collective-permute-start(f32[512]{0:T(512)S(1)} %bitcast.88), channel_id=1, source_target_pairs={{0,1},{1,0},{2,3},{3,2},{4,5},{5,4},{6,7},{7,6},{8,9},{9,8},{10,11... | collective-permute-start | bytes 6152 | tf_op jit(solution)/shard_map/ppermute | solution.py:39
  160.6 9.8 %collective-permute-start.9 = (bf16[72,256]{1,0:T(8,128)(2,1)S(1)}, bf16[72,256]{1,0:T(8,128)(2,1)S(1)}, u32[]{:S(2)}, u32[]{:S(2)}) collective-permute-start(bf16[72,256]{1,0:T(8,128)(2,1)S(1)} %dynamic-slice_bitcast_fusion.3), channel_id=1, source_target_pairs={{0,1},{1,0},{2,3},{3,2},{4,5},{5,4},{6,7},{7,6},{8,9},{9,8},{10,11... | collective-permute-start | bytes 110600 | tf_op jit(solution)/shard_map/ppermute | solution.py:39
  178.0 12.2 %collective-permute-start.12 = (bf16[192,256]{0,1:T(8,128)(2,1)S(1)}, bf16[192,256]{0,1:T(8,128)(2,1)S(1)}, u32[]{:S(2)}, u32[]{:S(2)}) collective-permute-start(bf16[192,256]{0,1:T(8,128)(2,1)S(1)} %bitcast.83), channel_id=1, source_target_pairs={{0,256},{1,257},{256,0},{257,1},{2,258},{3,259},{258,2},{259,3},{4... | collective-permute-start | bytes 294920 | tf_op jit(solution)/shard_map/ppermute | solution.py:66
  184.2 14.1 %collective-permute-start.13 = (bf16[192,256]{0,1:T(8,128)(2,1)S(1)}, bf16[192,256]{0,1:T(8,128)(2,1)S(1)}, u32[]{:S(2)}, u32[]{:S(2)}) collective-permute-start(bf16[192,256]{0,1:T(8,128)(2,1)S(1)} %bitcast.84), channel_id=1, source_target_pairs={{0,257},{1,256},{256,1},{257,0},{2,259},{3,258},{258,3},{259,2},{4... | collective-permute-start | bytes 294920 | tf_op jit(solution)/shard_map/ppermute | solution.py:66
Sparse Core Ops, SparseCore 0:
  22.5 57.4 all-gather.4
  136.4 40.5 reduce-scatter.1
